TPU v7x, 32 devices: a whole 2x2x4 slice. The times are simulated.
32 devices in a mesh: parts: 2 (over y), own: 16 (over z, x, core).
Axes of the slice: x: 2, y: 2, z: 4, core: 2. Of those that a mesh axis runs over, the one named last changes fastest.
Arguments:
- amplitudes: bfloat16 [128, 1024, 256], P(('parts', 'own')), parts along dimension 0, may hold values from -6 to 6
- integrals: bfloat16 [1536, 256, 256], P(('parts', 'own')), parts along dimension 0, may hold values from -0.375 to 0.375
- tasks: int32 [1536, 2], P(('parts', 'own')), parts along dimension 0, may hold values from 0 to 63, as said below
Outputs:
- residual: float32 [128, 1024, 256], P(('parts', 'own')), parts along dimension 0
There are 2 independent parts, one for each index of `parts`. A program takes and returns all parts, laid end to end along the dimension named above; each array names one. Nothing has to cross between parts.
Inputs may be any that keep to these rules, and one draw needn't show every extreme that they name: `tasks`: task k stored on group g = k // 48 has source and target tiles in g * 4 - 2 to (g + 1) * 4 + 1; the first task of each group has the lowest such source, the second the highest; the third targets the tile just below the group's own and the fourth the tile just above, where such tiles exist.
All inputs are finite; a program needn't handle non-finite values.
Results may differ from a plain program's by a relative error of at most 0.0021.
Values may be sent and summed in bfloat16 or wider, within the bound.
No kernel may reach another device: no remote copies, remote signals or barrier semaphores. Data moves between devices by JAX's collectives and lax.ppermute only.
A program may use at most 256 MiB of HBM per device.

v0:
```python
import jax
import jax.numpy as jnp
from jax import lax
from jax.sharding import PartitionSpec as P

HALO = 2


def extended(cells, sides, width):
    for axis, dim in sides:
        count = lax.axis_size(axis)
        ends = count - 1
        head = lax.slice_in_dim(cells, 0, width, axis=dim)
        tail = lax.slice_in_dim(cells, cells.shape[dim] - width, cells.shape[dim], axis=dim)
        cells = jnp.concatenate(
            [
                lax.ppermute(tail, axis, [(i, (i + 1) % count) for i in range(ends)]),
                cells,
                lax.ppermute(head, axis, [((i + 1) % count, i) for i in range(ends)]),
            ],
            axis=dim,
        )
    return cells


def shifted(block, axis, distance):
    devices = range(lax.axis_size(axis))
    route = [(i - distance, i) for i in devices if i - distance in devices]
    return lax.ppermute(block, axis, route)


def on_device(amplitudes, integrals, tasks):
    tile_count = amplitudes.shape[0]
    rows_here = amplitudes.shape[1]
    width_here = amplitudes.shape[2]
    first_tile = lax.axis_index("own") * tile_count
    widened = extended(amplitudes, (("own", 0),), tile_count)
    reach = widened.shape[0]
    extent = tile_count + 2 * HALO
    source = tasks[:, 0] - first_tile + tile_count
    target = tasks[:, 1] - first_tile + HALO
    pick_table = (source[:, None] == jnp.arange(reach, dtype=jnp.int32)[None, :]).astype(
        jnp.bfloat16
    )
    flat_amp = widened.reshape(reach, rows_here * width_here)
    picked = jnp.dot(pick_table, flat_amp, preferred_element_type=jnp.float32).astype(jnp.bfloat16)
    picked = picked.reshape(-1, rows_here, width_here)
    products = jnp.einsum("krw,kwv->krv", picked, integrals, preferred_element_type=jnp.float32)
    place_table = (jnp.arange(extent, dtype=jnp.int32)[:, None] == target[None, :]).astype(
        jnp.float32
    )
    summed = jnp.dot(
        place_table,
        products.reshape(-1, rows_here * width_here),
        precision=lax.Precision.HIGHEST,
        preferred_element_type=jnp.float32,
    )
    summed = summed.reshape(extent, rows_here, width_here)
    lower_rim = summed[:HALO].astype(jnp.bfloat16)
    upper_rim = summed[HALO + tile_count :].astype(jnp.bfloat16)
    from_above = shifted(lower_rim, "own", -1)
    from_below = shifted(upper_rim, "own", 1)
    resident = summed[HALO : HALO + tile_count]
    resident = resident.at[:HALO].add(from_below.astype(jnp.float32))
    resident = resident.at[tile_count - HALO :].add(from_above.astype(jnp.float32))
    return resident


def solution(mesh):
    return jax.shard_map(
        on_device,
        mesh=mesh,
        in_specs=(
            P(("parts", "own"), None, None),
            P(("parts", "own"), None, None),
            P(("parts", "own"), None),
        ),
        out_specs=P(("parts", "own"), None, None),
        check_vma=False,
    )
```

profile of v0, /device:TPU:1, one launch (start us, length us, event | category | flops | bytes accessed | tf_op | source)
XLA Modules:
  0.0 243.1 jit_solution(2248571052226537720)
XLA Ops:
  0.0 4.5 %collective-permute-start = (bf16[4,1024,256]{2,1,0:T(8,128)(2,1)}, bf16[4,1024,256]{2,1,0:T(8,128)(2,1)S(1)}, u32[]{:S(2)}, u32[]{:S(2)}) collective-permute-start(bf16[4,1024,256]{2,1,0:T(8,128)(2,1)} %param.7), channel_id=1, source_target_pairs={{0,1},{1,2},{2,3},{3,4},{4,5},{5,6},{6,7},{7,8},{8,9},{9,10},{10,1... | collective-permute-start | bytes 6291464 | tf_op jit(solution)/shard_map/ppermute | solution.py:17
  4.5 1.9 collective-permute-start.1
  6.4 0.8 add_bitcast_fusion.1
  7.2 43.0 %collective-permute-done = bf16[4,1024,256]{2,1,0:T(8,128)(2,1)S(1)} collective-permute-done((bf16[4,1024,256]{2,1,0:T(8,128)(2,1)}, bf16[4,1024,256]{2,1,0:T(8,128)(2,1)S(1)}, u32[]{:S(2)}, u32[]{:S(2)}) %collective-permute-start) | collective-permute-done | bytes 2097184 | tf_op jit(solution)/shard_map/ppermute | solution.py:17
  50.3 3.2 %pad_maximum_fusion = bf16[12,1024,256]{2,1,0:T(8,128)(2,1)S(1)} fusion(bf16[4,1024,256]{2,1,0:T(8,128)(2,1)} %collective-permute-done.1, bf16[4,1024,256]{2,1,0:T(8,128)(2,1)} %param.7, bf16[4,1024,256]{2,1,0:T(8,128)(2,1)S(1)} %collective-permute-done), kind=kLoop, calls=%fused_computation.1 | loop fusion | flops 6291456 | bytes 12582912 | tf_op jit(solution)/shard_map/concatenate | solution.py:15
  53.4 3.9 %pad.7 = bf16[16,1024,256]{2,1,0:T(8,128)(2,1)} pad(bf16[12,1024,256]{2,1,0:T(8,128)(2,1)S(1)} %pad_maximum_fusion, bf16[]{:T(256)} %constant.67), padding=0_4x0_0x0_0 | pad | bytes 14680066
  57.3 11.4 %copy.4 = bf16[2,8,1024,256]{3,1,2,0:T(8,128)(2,1)} copy(bf16[2,8,1024,256]{3,2,1,0:T(8,128)(2,1)} %bitcast.37) | data formatting | bytes 16777216
  68.7 15.1 %convolution_convert_fusion = bf16[48,262144]{1,0:T(8,128)(2,1)} fusion(bf16[12,262144]{1,0:T(8,128)(2,1)} %bitcast.36, s32[48]{0:T(128)S(1)} %get-tuple-element.32), kind=kOutput, calls=%fused_computation | convolution fusion | flops 314573376 | bytes 31457472 | tf_op jit(solution)/shard_map/dot_general | solution.py:46
  83.8 23.1 %copy.5 = bf16[6,8,1024,256]{3,2,1,0:T(8,128)(2,1)} copy(bf16[6,8,1024,256]{3,1,2,0:T(8,128)(2,1)} %bitcast.35) | data formatting | bytes 50331648
  106.9 27.0 %fusion.7 = f32[48,1024,256]{2,1,0:T(8,128)} fusion(bf16[48,1024,256]{2,1,0:T(8,128)(2,1)} %bitcast.34, bf16[48,256,256]{2,1,0:T(8,128)(2,1)} %param.8), kind=kOutput, calls=%fused_computation.18 | convolution fusion | flops 6442450944 | bytes 81788928 | tf_op jit(solution)/shard_map/krw,kwv->krv/dot_general | solution.py:48
  134.0 45.9 %copy.6 = f32[6,8,1024,256]{3,1,2,0:T(8,128)} copy(f32[6,8,1024,256]{3,2,1,0:T(8,128)} %bitcast.32) | data formatting | bytes 100663296
  179.8 25.7 %fusion.6 = (bf16[8,262144]{1,0:T(8,128)(2,1)}, f32[8,262144]{1,0:T(8,128)}) fusion(f32[48,262144]{1,0:T(8,128)} %bitcast.33, s32[48]{0:T(128)S(1)} %get-tuple-element.31), kind=kOutput, calls=%fused_computation.17 | convolution fusion | flops 1210057088 | bytes 62914752 | tf_op jit(solution)/shard_map/dot_general | solution.py:52
  205.5 4.8 %fusion.5 = (bf16[2,262144]{1,0:T(2,128)(2,1)S(1)}, bf16[2,262144]{1,0:T(2,128)(2,1)S(1)}) fusion(bf16[8,262144]{1,0:T(8,128)(2,1)} %get-tuple-element.33), kind=kLoop, calls=%fused_computation.16 | loop fusion | bytes 4194304 | tf_op jit(solution)/shard_map/slice | solution.py:59
  210.4 0.1 copy.17
  210.5 4.3 %collective-permute-start.2 = (bf16[2,1024,256]{2,1,0:T(8,128)(2,1)S(1)}, bf16[2,1024,256]{2,1,0:T(8,128)(2,1)S(1)}, u32[]{:S(2)}, u32[]{:S(2)}) collective-permute-start(bf16[2,1024,256]{2,1,0:T(8,128)(2,1)S(1)} %bitcast.44), channel_id=1, source_target_pairs={{0,1},{1,2},{2,3},{3,4},{4,5},{5,6},{6,7},{7,8},{8,9},{9,10},{10,1... | collective-permute-start | bytes 3145736 | tf_op jit(solution)/shard_map/ppermute | solution.py:29
  214.8 0.1 copy.16
  214.9 1.9 collective-permute-start.3
  216.9 0.9 slice.81
  217.8 0.9 slice.80
  218.8 0.8 copy.15
  219.6 18.1 %collective-permute-done.2 = bf16[2,1024,256]{2,1,0:T(8,128)(2,1)S(1)} collective-permute-done((bf16[2,1024,256]{2,1,0:T(8,128)(2,1)S(1)}, bf16[2,1024,256]{2,1,0:T(8,128)(2,1)S(1)}, u32[]{:S(2)}, u32[]{:S(2)}) %collective-permute-start.2) | collective-permute-done | bytes 1048608 | tf_op jit(solution)/shard_map/ppermute | solution.py:29
  237.8 0.2 fusion
  238.0 2.0 copy-done.1
  240.0 3.1 %fusion.1 = f32[4,1024,256]{2,1,0:T(8,128)} fusion(f32[4,1024,256]{2,1,0:T(8,128)} %copy-done.1, bf16[2,1024,256]{2,1,0:T(8,128)(2,1)S(1)} %collective-permute-done.3), kind=kLoop, calls=%fused_computation.6 | loop fusion | flops 1048576 | bytes 5242880 | tf_op jit(solution)/shard_map/scatter-add | solution.py:65
  (5 shorter events, 0.0 us)
Async XLA Ops:
  0.0 50.3 %collective-permute-start = (bf16[4,1024,256]{2,1,0:T(8,128)(2,1)}, bf16[4,1024,256]{2,1,0:T(8,128)(2,1)S(1)}, u32[]{:S(2)}, u32[]{:S(2)}) collective-permute-start(bf16[4,1024,256]{2,1,0:T(8,128)(2,1)} %param.7), channel_id=1, source_target_pairs={{0,1},{1,2},{2,3},{3,4},{4,5},{5,6},{6,7},{7,8},{8,9},{9,10},{10,1... | collective-permute-start | bytes 6291464 | tf_op jit(solution)/shard_map/ppermute | solution.py:17
  4.5 45.7 %collective-permute-start.1 = (bf16[4,1024,256]{2,1,0:T(8,128)(2,1)}, bf16[4,1024,256]{2,1,0:T(8,128)(2,1)}, u32[]{:S(2)}, u32[]{:S(2)}) collective-permute-start(bf16[4,1024,256]{2,1,0:T(8,128)(2,1)} %param.7), channel_id=1, source_target_pairs={{1,0},{2,1},{3,2},{4,3},{5,4},{6,5},{7,6},{8,7},{9,8},{10,9},{11,1... | collective-permute-start | bytes 6291464 | tf_op jit(solution)/shard_map/ppermute | solution.py:19
  205.5 11.3 %copy-start = (f32[8,262144]{1,0:T(8,128)S(1)}, f32[8,262144]{1,0:T(8,128)}, u32[]{:S(2)}) copy-start(f32[8,262144]{1,0:T(8,128)} %get-tuple-element.34) | copy-start | bytes 25165828
  210.5 27.3 %collective-permute-start.2 = (bf16[2,1024,256]{2,1,0:T(8,128)(2,1)S(1)}, bf16[2,1024,256]{2,1,0:T(8,128)(2,1)S(1)}, u32[]{:S(2)}, u32[]{:S(2)}) collective-permute-start(bf16[2,1024,256]{2,1,0:T(8,128)(2,1)S(1)} %bitcast.44), channel_id=1, source_target_pairs={{0,1},{1,2},{2,3},{3,4},{4,5},{5,6},{6,7},{7,8},{8,9},{9,10},{10,1... | collective-permute-start | bytes 3145736 | tf_op jit(solution)/shard_map/ppermute | solution.py:29
  214.9 23.0 %collective-permute-start.3 = (bf16[2,1024,256]{2,1,0:T(8,128)(2,1)S(1)}, bf16[2,1024,256]{2,1,0:T(8,128)(2,1)S(1)}, u32[]{:S(2)}, u32[]{:S(2)}) collective-permute-start(bf16[2,1024,256]{2,1,0:T(8,128)(2,1)S(1)} %bitcast.43), channel_id=1, source_target_pairs={{1,0},{2,1},{3,2},{4,3},{5,4},{6,5},{7,6},{8,7},{9,8},{10,9},{11,1... | collective-permute-start | bytes 3145736 | tf_op jit(solution)/shard_map/ppermute | solution.py:29
  238.0 2.0 copy-start.1
where the time goes:
time: 244 us; the launch traced here: 243 us
  local copies, waits for them, and re-layouts  94.1 us (39%)
  matrix products  67.8 us (28%)
  waiting for transfers between devices  61.2 us (25%)
  starting transfers between devices  12.6 us (5%)
  other arithmetic  7.27 us (3%)
    unnamed x11, local copies, waits for them, and re-layouts  87.4 us
    ppermute x1, waiting for transfers between devices, extended(): lax.ppermute(tail, axis, [(i, (i + 1) % count) for i in range(ends)])  43 us
    dot_general x1, matrix products, on_device(): jnp.einsum('krw,kwv->krv', picked, integrals, preferred_element_type=jnp....  27 us
    dot_general x1, matrix products, on_device(): jnp.dot(place_table, products.reshape(-1, rows_here * width_here), precis...  25.7 us
    ppermute x2, waiting for transfers between devices, shifted(): return lax.ppermute(block, axis, route)  18.1 us
    dot_general x1, matrix products, on_device(): jnp.dot(pick_table, flat_amp, preferred_element_type=jnp.float32)  15.1 us
    ppermute x2, starting transfers between devices, shifted(): return lax.ppermute(block, axis, route)  6.21 us
  transfers between devices with their start and end apart: 4, of which 2 were waited for; matrix products, arithmetic and copies ran while one was open for 2% of the time, Pallas kernels for 0%

commit v1 on v0

v1 whole, which is shorter than its diff:
```python
import functools

import jax
import jax.numpy as jnp
from jax import lax
from jax.experimental import pallas as pl
from jax.experimental.pallas import tpu as pltpu
from jax.sharding import PartitionSpec as P

HALO = 2
SPLIT = (512, 512)
CHIP_SPLIT = (384, 384, 256)
VMEM_LIMIT = 24 * 1024 * 1024

OWN, CHIP, CROSS = 0, 1, 2
LISTS = 6


def row_chunks(rows, split):
    total = sum(split)
    sizes = [rows * part // total for part in split]
    starts = [sum(sizes[:i]) for i in range(len(sizes))]
    return list(zip(starts, sizes))


def vmem():
    return pl.BlockSpec(memory_space=pltpu.VMEM)


def smem():
    return pl.BlockSpec(memory_space=pltpu.SMEM)


def hbm():
    return pl.BlockSpec(memory_space=pltpu.HBM)


def in_vmem(x):
    return pltpu.with_memory_space_constraint(x, pltpu.VMEM)


def in_hbm(x):
    return pltpu.with_memory_space_constraint(x, pltpu.HBM)


def accumulate(plan, which, source, integrals, sums, rows=None):
    start, size = rows or (0, source.shape[1])
    offset = 0 if sums.shape[1] == size else start
    begin = 0 if source.shape[1] == size else start
    block = 256 if size % 256 == 0 else 128
    count = plan[which, plan.shape[1] - 1]

    def some(first, width):
        entries = [plan[which, first + u] for u in range(width)]
        for r in range(0, size, block):
            products = [
                jnp.dot(
                    source[(entry >> 4) & 15, pl.ds(begin + r, block)],
                    integrals[entry >> 8],
                    preferred_element_type=jnp.float32,
                )
                for entry in entries
            ]
            for entry, product in zip(entries, products):
                sums[entry & 15, pl.ds(offset + r, block)] += product

    def pair(i, carry):
        some(2 * i, 2)
        return carry

    def single(i, carry):
        some(i, 1)
        return carry

    pairs = count // 2
    lax.fori_loop(0, pairs, pair, 0)
    lax.fori_loop(2 * pairs, count, single, 0)


def make_plan(axis, tile_count, tasks, plan):
    odd = lax.rem(lax.axis_index(axis), 2)
    first = lax.axis_index(axis) * tile_count
    last = plan.shape[1] - 1
    for which in range(LISTS):
        plan[which, last] = 0
    plan[LISTS, 0] = odd

    def place(tile):
        own = tile - first
        below = own < 0
        above = own >= tile_count
        crossing = jnp.logical_or(
            jnp.logical_and(below, odd == 0), jnp.logical_and(above, odd == 1)
        )
        slot = jnp.where(below, own + HALO, jnp.where(above, own - tile_count, own))
        kind = jnp.where(crossing, CROSS, jnp.where(jnp.logical_or(below, above), CHIP, OWN))
        return slot, kind

    def one(k, carry):
        src, src_kind = place(tasks[0, k])
        dst, dst_kind = place(tasks[1, k])
        dst = dst + jnp.where(dst_kind == CHIP, tile_count, 0)
        which = 2 * src_kind + jnp.where(dst_kind == CROSS, 1, 0)
        count = plan[which, last]
        plan[which, count] = k * 256 + src * 16 + dst
        plan[which, last] = count + 1
        return carry

    lax.fori_loop(0, tasks.shape[1], one, 0)


def edges(odd, tile_count):
    edge = tile_count - HALO
    return odd * edge, (1 - odd) * edge


def pick_kernel(axis, chunks, amplitudes, *refs):
    *picked, sems = refs
    near, far = edges(lax.rem(lax.axis_index(axis), 2), amplitudes.shape[0])
    copies = [
        pltpu.make_async_copy(
            amplitudes.at[pl.ds(near, HALO), pl.ds(start, size)], picked[i], sems.at[i]
        )
        for i, (start, size) in enumerate(chunks)
    ]
    i = len(chunks)
    copies.append(
        pltpu.make_async_copy(amplitudes.at[pl.ds(far, HALO)], picked[i], sems.at[i])
    )
    for copy in copies:
        copy.start()
    for copy in copies:
        copy.wait()


def first_kernel(axis, chunks, tasks, amplitudes, chip, integrals, plan, own, held, *refs):
    *sums, sems = refs
    copies = [
        pltpu.make_async_copy(amplitudes, own, sems.at[0]),
        pltpu.make_async_copy(integrals, held, sems.at[1]),
    ]
    for copy in copies:
        copy.start()
    make_plan(axis, amplitudes.shape[0], tasks, plan)
    for ref in sums:
        ref[...] = jnp.zeros_like(ref)
    for copy in copies:
        copy.wait()
    for rows, total in zip(chunks, sums):
        accumulate(plan, 2 * OWN + 1, own, held, total, rows)
        accumulate(plan, 2 * CHIP + 1, chip, held, total, rows)


def own_kernel(plan, own, integrals, sums):
    sums[...] = jnp.zeros_like(sums)
    accumulate(plan, 2 * OWN, own, integrals, sums)


def cross_kernel(plan, halo, integrals, sums, rim, total):
    accumulate(plan, 2 * CROSS + 1, halo, integrals, total)
    rim[...] = total[...].astype(rim.dtype)


def stay_kernel(rows, plan, halo, integrals, sums, total):
    accumulate(plan, 2 * CROSS, halo, integrals, total, rows)


def chip_kernel(rows, chip_chunks, plan, halo, chip, integrals, sums, total, *rims):
    accumulate(plan, 2 * CROSS, halo, integrals, total, rows)
    accumulate(plan, 2 * CHIP, chip, integrals, total)
    for (start, size), rim in zip(chip_chunks, rims):
        rim[...] = total[total.shape[0] - HALO :, pl.ds(start, size)].astype(rim.dtype)


def rest_kernel(chunks, chip_chunks, plan, sums, *refs):
    chip, cross = refs[: len(chip_chunks)], refs[len(chip_chunks) : -3]
    out, whole, sems = refs[-3:]
    near, far = edges(plan[LISTS, 0], out.shape[0])
    copies = []
    for j in range(HALO):
        for (start, size), rim in zip(chip_chunks, chip):
            rows = pl.ds(start, size)
            whole[j, rows] = sums[far + j, rows] + rim[j].astype(jnp.float32)
        copies.append(pltpu.make_async_copy(whole.at[j], out.at[far + j], sems.at[j]))
        copies[-1].start()
    done = pl.ds(0, chunks[-1][0])
    for j in range(HALO):
        for (start, size), rim in zip(chunks[:-1], cross):
            rows = pl.ds(start, size)
            whole[HALO + j, rows] = sums[near + j, rows] + rim[j].astype(jnp.float32)
        copies.append(
            pltpu.make_async_copy(
                whole.at[HALO + j, done], out.at[near + j, done], sems.at[HALO + j]
            )
        )
        copies[-1].start()
    for copy in copies:
        copy.wait()


def last_kernel(rows, plan, sums, rim, before, out, part, sems):
    near, _ = edges(plan[LISTS, 0], out.shape[0])
    rows = pl.ds(*rows)
    copies = []
    for j in range(HALO):
        part[j] = sums[near + j, rows] + rim[j].astype(jnp.float32)
        copies.append(pltpu.make_async_copy(part.at[j], out.at[near + j, rows], sems.at[j]))
        copies[-1].start()
    for copy in copies:
        copy.wait()


def on_device(amplitudes, integrals, tasks):
    tile_count, rows, width = amplitudes.shape
    task_count = integrals.shape[0]
    chunks = row_chunks(rows, SPLIT)
    chip_chunks = row_chunks(rows, CHIP_SPLIT)
    sizes = [size for _, size in chunks]
    count = len(chunks)
    axis = "own"
    devices = lax.axis_size(axis)
    cross_pairs = [(i, i + 1) for i in range(1, devices - 1, 2)]
    cross_pairs += [(b, a) for a, b in cross_pairs]
    chip_pairs = [(i, i ^ 1) for i in range(devices)]
    f32, bf16, i32 = jnp.float32, amplitudes.dtype, jnp.int32

    def call(kernel, name, operands, in_specs, after=(), **kwargs):
        here = len(operands)

        def body(*refs):
            kernel(*refs[:here], *refs[here + len(after) :])

        return pl.pallas_call(
            body,
            in_specs=in_specs + [pl.BlockSpec(memory_space=pl.ANY)] * len(after),
            compiler_params=pltpu.CompilerParams(vmem_limit_bytes=VMEM_LIMIT),
            cost_estimate=pl.CostEstimate(flops=1, bytes_accessed=1, transcendentals=0),
            name=name,
            **kwargs,
        )(*operands, *after)

    def swap_cross(x):
        return in_vmem(lax.ppermute(x, axis, cross_pairs))

    def swap_chip(x):
        return in_vmem(lax.ppermute(x, axis, chip_pairs))

    amplitudes, integrals = in_hbm(amplitudes), in_hbm(integrals)
    picked = call(
        functools.partial(pick_kernel, axis, chunks),
        "pick",
        [amplitudes],
        [hbm()],
        out_shape=[jax.ShapeDtypeStruct((HALO, size, width), bf16) for size in sizes + [rows]],
        out_specs=[hbm()] * (count + 1),
        scratch_shapes=[pltpu.SemaphoreType.DMA((count + 1,))],
    )
    cross_halo = [swap_cross(x) for x in picked[:count]]
    chip_halo = swap_chip(picked[count])

    plan, own, held, *cross_sums = call(
        functools.partial(first_kernel, axis, chunks),
        "cross_targets",
        [tasks.T, amplitudes, chip_halo, integrals],
        [smem(), hbm(), vmem(), hbm()],
        out_shape=[
            jax.ShapeDtypeStruct((LISTS + 1, task_count + 1), i32),
            pltpu.VMEM(amplitudes.shape, bf16),
            pltpu.VMEM(integrals.shape, bf16),
        ]
        + [pltpu.VMEM((HALO, size, width), f32) for size in sizes],
        out_specs=[smem()] + [vmem()] * (count + 2),
        scratch_shapes=[pltpu.SemaphoreType.DMA((2,))],
    )
    own, held = in_vmem(own), in_vmem(held)
    whole = pltpu.VMEM((tile_count + HALO, rows, width), f32)
    sums = call(
        own_kernel,
        "own_sources",
        [plan, own, held],
        [smem()] + [vmem()] * 2,
        out_shape=whole,
        out_specs=vmem(),
    )

    from_cross = []
    for chunk, halo, cross_sum in zip(chunks, cross_halo, cross_sums):
        size = chunk[1]
        rim, _ = call(
            cross_kernel,
            "cross_rim",
            [plan, halo, held, in_vmem(cross_sum)],
            [smem()] + [vmem()] * 3,
            after=[in_vmem(sums)],
            out_shape=[
                pltpu.VMEM((HALO, size, width), bf16),
                pltpu.VMEM((HALO, size, width), f32),
            ],
            out_specs=[vmem()] * 2,
            input_output_aliases={3: 1},
        )
        from_cross.append(swap_cross(rim))
        if len(from_cross) < count:
            sums = call(
                functools.partial(stay_kernel, chunk),
                "cross_sources",
                [plan, halo, held, in_vmem(sums)],
                [smem()] + [vmem()] * 3,
                after=[rim],
                out_shape=whole,
                out_specs=vmem(),
                input_output_aliases={3: 0},
            )
    sums, *rims = call(
        functools.partial(chip_kernel, chunks[-1], chip_chunks),
        "chip_rim",
        [plan, cross_halo[-1], chip_halo, held, in_vmem(sums)],
        [smem()] + [vmem()] * 4,
        after=[rim],
        out_shape=[whole] + [pltpu.VMEM((HALO, size, width), bf16) for _, size in chip_chunks],
        out_specs=[vmem()] * (1 + len(chip_chunks)),
        input_output_aliases={4: 0},
    )
    from_chip = [swap_chip(x) for x in rims]

    sums = in_vmem(sums)
    shape = jax.ShapeDtypeStruct((tile_count, rows, width), f32)
    out = call(
        functools.partial(rest_kernel, chunks, chip_chunks),
        "residual",
        [plan, sums, *from_chip, *from_cross[:-1]],
        [smem()] + [vmem()] * (count + len(chip_chunks)),
        out_shape=shape,
        out_specs=hbm(),
        scratch_shapes=[
            pltpu.VMEM((2 * HALO, rows, width), f32),
            pltpu.SemaphoreType.DMA((2 * HALO,)),
        ],
    )
    return call(
        functools.partial(last_kernel, chunks[-1]),
        "residual_last",
        [plan, sums, from_cross[-1], out],
        [smem()] + [vmem()] * 2 + [hbm()],
        out_shape=shape,
        out_specs=hbm(),
        scratch_shapes=[
            pltpu.VMEM((HALO, sizes[-1], width), f32),
            pltpu.SemaphoreType.DMA((HALO,)),
        ],
        input_output_aliases={3: 0},
    )


def solution(mesh):
    return jax.shard_map(
        on_device,
        mesh=mesh,
        in_specs=(
            P(("parts", "own"), None, None),
            P(("parts", "own"), None, None),
            P(("parts", "own"), None),
        ),
        out_specs=P(("parts", "own"), None, None),
        check_vma=False,
    )
```

time: 244 us -> 54.6 us (0.22)
  local copies, waits for them, and re-layouts: 94.1 us -> 0.67 us
  matrix products: 67.8 us -> 0 us
  waiting for transfers between devices: 61.2 us -> 11.6 us
  Pallas kernels: 0 us -> 27.9 us
  other arithmetic: 7.27 us -> 0 us
    unnamed x11 -> x2, local copies, waits for them, and re-layouts: 87.4 us -> 0.67 us
    dot_general x3 -> x0, matrix products: 67.8 us -> none  [the longest x1 27 us: on_device(): jnp.einsum('krw,kwv->krv', picked, integrals, preferred_element_type=jnp....]
    ppermute x4 -> x8, waiting for transfers between devices: 61.2 us -> 11.6 us  [the longest x4 9.49 us: swap_cross(): return in_vmem(lax.ppermute(x, axis, cross_pairs))]
    pallas_call x0 -> x9, Pallas kernels: none -> 27.9 us  [call(): pl.pallas_call(body, in_specs=in_specs + [pl.BlockSpec(memory_space=pl.AN...]
    slice x2 -> x0, local copies, waits for them, and re-layouts: 5.75 us -> none  [the longest x1 4.8 us: on_device(): lower_rim = summed[:HALO].astype(jnp.bfloat16)]
    scatter-add x2 -> x0, other arithmetic: 3.34 us -> none  [the longest x1 3.13 us: on_device(): resident.at[tile_count - HALO:].add(from_above.astype(jnp.float32))]
    concatenate x1 -> x0, other arithmetic: 3.17 us -> none  [extended(): jnp.concatenate([lax.ppermute(tail, axis, [(i, (i + 1) % count) for i in...]
    ppermute x4 -> x8, starting transfers between devices: 12.6 us -> 13.5 us  [the longest x4 12.7 us: swap_cross(): return in_vmem(lax.ppermute(x, axis, cross_pairs))]
  transfers between devices with their start and end apart: 4 -> 8, of which waited for: 2 -> 4; matrix products, arithmetic and copies ran while one was open for 2% -> 0% of each run, Pallas kernels for 0% -> 46%
where the time goes in v1:
time: 54.6 us; the launch traced here: 53.7 us
  Pallas kernels  27.9 us (51%)
  starting transfers between devices  13.5 us (25%)
  waiting for transfers between devices  11.6 us (21%)
  local copies, waits for them, and re-layouts  0.67 us (1%)
    pallas_call x9, Pallas kernels, call(): pl.pallas_call(body, in_specs=in_specs + [pl.BlockSpec(memory_space=pl.AN...  27.9 us
    ppermute x4, starting transfers between devices, swap_cross(): return in_vmem(lax.ppermute(x, axis, cross_pairs))  12.7 us
    ppermute x4, waiting for transfers between devices, swap_cross(): return in_vmem(lax.ppermute(x, axis, cross_pairs))  9.49 us
    ppermute x4, waiting for transfers between devices, swap_chip(): return in_vmem(lax.ppermute(x, axis, chip_pairs))  2.08 us
  transfers between devices with their start and end apart: 8, of which 4 were waited for; matrix products, arithmetic and copies ran while one was open for 0% of the time, Pallas kernels for 46%

profile of v1, /device:TPU:1, one launch (start us, length us, event | category | flops | bytes accessed | tf_op | source)
XLA Modules:
  0.0 53.7 jit_solution(8656590265202299149)
XLA Ops:
  0.0 1.6 %pick.1 = (bf16[2,512,256]{2,1,0:T(8,128)(2,1)S(1)}, bf16[2,512,256]{2,1,0:T(8,128)(2,1)S(1)}, bf16[2,1024,256]{2,1,0:T(8,128)(2,1)S(1)}) custom-call(bf16[4,1024,256]{2,1,0:T(8,128)(2,1)} %refs_1_.1), custom_call_target="tpu_custom_call" | custom-call | flops 1 | bytes 1 | tf_op jit(solution)/shard_map/pick/pallas_call | solution.py:233
  1.6 0.1 collective-permute-start
  1.7 4.5 %collective-permute-start.2 = (bf16[2,512,256]{2,1,0:T(8,128)(2,1)S(1)}, bf16[2,512,256]{2,1,0:T(8,128)(2,1)S(1)}, u32[]{:S(2)}, u32[]{:S(2)}) collective-permute-start(bf16[2,512,256]{2,1,0:T(8,128)(2,1)S(1)} %get-tuple-element.23), channel_id=1, source_target_pairs={{1,2},{3,4},{5,6},{7,8},{9,10},{11,12},{13,14},{2,1},{4,3},{6,5},{... | collective-permute-start | bytes 1572872 | tf_op jit(solution)/shard_map/ppermute | solution.py:243
  6.2 1.9 %collective-permute-start.1 = (bf16[2,512,256]{2,1,0:T(8,128)(2,1)S(1)}, bf16[2,512,256]{2,1,0:T(8,128)(2,1)S(1)}, u32[]{:S(2)}, u32[]{:S(2)}) collective-permute-start(bf16[2,512,256]{2,1,0:T(8,128)(2,1)S(1)} %get-tuple-element.21), channel_id=1, source_target_pairs={{1,2},{3,4},{5,6},{7,8},{9,10},{11,12},{13,14},{2,1},{4,3},{6,5},{... | collective-permute-start | bytes 1572872 | tf_op jit(solution)/shard_map/ppermute | solution.py:243
  8.1 0.0 copy-start
  8.1 0.7 %copy-done = s32[48,2]{0,1:T(2,128)S(1)} copy-done((s32[48,2]{0,1:T(2,128)S(1)}, s32[48,2]{0,1:T(2,128)}, u32[]{:S(2)}) %copy-start) | copy-done | bytes 408
  8.8 7.3 %cross_targets.1 = (s32[7,49]{1,0:T(8,128)S(1)}, bf16[4,1024,256]{2,1,0:T(8,128)(2,1)S(1)}, bf16[48,256,256]{2,1,0:T(8,128)(2,1)S(1)}, f32[2,512,256]{2,1,0:T(8,128)S(1)}, f32[2,512,256]{2,1,0:T(8,128)S(1)}) custom-call(s32[2,48]{1,0:T(2,128)S(1)} %bitcast.1, bf16[4,1024,256]{2,1,0:T(8,128)(2,1)} %refs_1_.1, ...), custom_call_target="tpu_custom_call" | custom-call | flops 1 | bytes 1 | tf_op jit(solution)/shard_map/cross_targets/pallas_call | solution.py:233
  16.1 5.1 %own_sources.1.refs_4_.refs_3_ = f32[6,1024,256]{2,1,0:T(8,128)S(1)} custom-call(s32[7,49]{1,0:T(8,128)S(1)} %get-tuple-element.20.refs_0_, bf16[4,1024,256]{2,1,0:T(8,128)(2,1)S(1)} %get-tuple-element.24.refs_1_, bf16[48,256,256]{2,1,0:T(8,128)(2,1)S(1)} %get-tuple-element.22.refs_2_.refs_3_), custom_call_target="tpu_custom_call" | custom-call | flops 1 | bytes 1 | tf_op jit(solution)/shard_map/own_sources/pallas_call | solution.py:233
  21.2 2.3 %collective-permute-done.2.refs_1_ = bf16[2,512,256]{2,1,0:T(8,128)(2,1)S(1)} collective-permute-done((bf16[2,512,256]{2,1,0:T(8,128)(2,1)S(1)}, bf16[2,512,256]{2,1,0:T(8,128)(2,1)S(1)}, u32[]{:S(2)}, u32[]{:S(2)}) %collective-permute-start.2) | collective-permute-done | bytes 524320 | tf_op jit(solution)/shard_map/ppermute | solution.py:243
  23.5 1.2 %cross_rim.2 = (bf16[2,512,256]{2,1,0:T(8,128)(2,1)S(1)}, f32[2,512,256]{2,1,0:T(8,128)S(1)}) custom-call(s32[7,49]{1,0:T(8,128)S(1)} %get-tuple-element.20.refs_0_, bf16[2,512,256]{2,1,0:T(8,128)(2,1)S(1)} %collective-permute-done.2.refs_1_, bf16[48,256,256]{2,1,0:T(8,128)(2,1)S(1)} %get-tuple-element.22.refs_2_.refs_3_, ...), custom_call_target="tpu_custom_call", output_to_operand_aliasing={{1}: (3, {})} | custom-call | flops 1 | bytes 1 | tf_op jit(solution)/shard_map/cross_rim/pallas_call | solution.py:233
  24.7 4.4 %collective-permute-start.7 = (bf16[2,512,256]{2,1,0:T(8,128)(2,1)S(1)}, bf16[2,512,256]{2,1,0:T(8,128)(2,1)S(1)}, u32[]{:S(2)}, u32[]{:S(2)}) collective-permute-start(bf16[2,512,256]{2,1,0:T(8,128)(2,1)S(1)} %get-tuple-element.26.refs_4_), channel_id=1, source_target_pairs={{1,2},{3,4},{5,6},{7,8},{9,10},{11,12},{13,14},{2,1},{4,3},{6,5},{... | collective-permute-start | bytes 1572872 | tf_op jit(solution)/shard_map/ppermute | solution.py:243
  29.1 2.5 %cross_sources.1.refs_4_ = f32[6,1024,256]{2,1,0:T(8,128)S(1)} custom-call(s32[7,49]{1,0:T(8,128)S(1)} %get-tuple-element.20.refs_0_, bf16[2,512,256]{2,1,0:T(8,128)(2,1)S(1)} %collective-permute-done.2.refs_1_, bf16[48,256,256]{2,1,0:T(8,128)(2,1)S(1)} %get-tuple-element.22.refs_2_.refs_3_, ...), custom_call_target="tpu_custom_call", output_to_operand_aliasing={{}: (3, {})} | custom-call | flops 1 | bytes 1 | tf_op jit(solution)/shard_map/cross_sources/pallas_call | solution.py:233
  31.6 1.2 %cross_rim.3 = (bf16[2,512,256]{2,1,0:T(8,128)(2,1)S(1)}, f32[2,512,256]{2,1,0:T(8,128)S(1)}) custom-call(s32[7,49]{1,0:T(8,128)S(1)} %get-tuple-element.20.refs_0_, bf16[2,512,256]{2,1,0:T(8,128)(2,1)S(1)} %collective-permute-done.1.refs_1_, bf16[48,256,256]{2,1,0:T(8,128)(2,1)S(1)} %get-tuple-element.22.refs_2_.refs_3_, ...), custom_call_target="tpu_custom_call", output_to_operand_aliasing={{1}: (3, {})} | custom-call | flops 1 | bytes 1 | tf_op jit(solution)/shard_map/cross_rim/pallas_call | solution.py:233
  32.9 1.9 %collective-permute-start.3 = (bf16[2,512,256]{2,1,0:T(8,128)(2,1)S(1)}, bf16[2,512,256]{2,1,0:T(8,128)(2,1)S(1)}, u32[]{:S(2)}, u32[]{:S(2)}) collective-permute-start(bf16[2,512,256]{2,1,0:T(8,128)(2,1)S(1)} %get-tuple-element.28.refs_5_), channel_id=1, source_target_pairs={{1,2},{3,4},{5,6},{7,8},{9,10},{11,12},{13,14},{2,1},{4,3},{6,5},{... | collective-permute-start | bytes 1572872 | tf_op jit(solution)/shard_map/ppermute | solution.py:243
  34.8 5.0 %chip_rim.1 = (f32[6,1024,256]{2,1,0:T(8,128)S(1)}, bf16[2,384,256]{2,1,0:T(8,128)(2,1)S(1)}, bf16[2,384,256]{2,1,0:T(8,128)(2,1)S(1)}, bf16[2,256,256]{2,1,0:T(8,128)(2,1)S(1)}) custom-call(s32[7,49]{1,0:T(8,128)S(1)} %get-tuple-element.20.refs_0_, bf16[2,512,256]{2,1,0:T(8,128)(2,1)S(1)} %collective-permute-done.1.refs_1_, ...), custom_call_target="tpu_custom_call", output_to_operand_aliasing={{0}: (4, {})} | custom-call | flops 1 | bytes 1 | tf_op jit(solution)/shard_map/chip_rim/pallas_call | solution.py:233
  39.8 0.1 collective-permute-start.4
  39.9 0.5 collective-permute-start.5
  40.4 0.1 collective-permute-start.6
  40.5 2.1 %collective-permute-done.6.refs_4_ = bf16[2,256,256]{2,1,0:T(8,128)(2,1)S(1)} collective-permute-done((bf16[2,256,256]{2,1,0:T(8,128)(2,1)S(1)}, bf16[2,256,256]{2,1,0:T(8,128)(2,1)S(1)}, u32[]{:S(2)}, u32[]{:S(2)}) %collective-permute-start.6) | collective-permute-done | bytes 262176 | tf_op jit(solution)/shard_map/ppermute | solution.py:246
  42.6 0.0 collective-permute-done.4.refs_2_
  42.6 3.9 %collective-permute-done.7.refs_5_ = bf16[2,512,256]{2,1,0:T(8,128)(2,1)S(1)} collective-permute-done((bf16[2,512,256]{2,1,0:T(8,128)(2,1)S(1)}, bf16[2,512,256]{2,1,0:T(8,128)(2,1)S(1)}, u32[]{:S(2)}, u32[]{:S(2)}) %collective-permute-start.7) | collective-permute-done | bytes 524320 | tf_op jit(solution)/shard_map/ppermute | solution.py:243
  46.5 2.4 %residual.1.refs_3_ = f32[4,1024,256]{2,1,0:T(8,128)} custom-call(s32[7,49]{1,0:T(8,128)S(1)} %get-tuple-element.20.refs_0_, f32[6,1024,256]{2,1,0:T(8,128)S(1)} %get-tuple-element.29.refs_1_, bf16[2,384,256]{2,1,0:T(8,128)(2,1)S(1)} %collective-permute-done.4.refs_2_, bf16[2,384,256]{2,1,0:T(8,128)(2,1)S(1)} %collective-permute-done.5.refs_3_, ...), custom_call_target="tpu_custom_call" | custom-call | flops 1 | bytes 1 | tf_op jit(solution)/shard_map/residual/pallas_call | solution.py:233
  48.9 3.2 %collective-permute-done.3.refs_2_ = bf16[2,512,256]{2,1,0:T(8,128)(2,1)S(1)} collective-permute-done((bf16[2,512,256]{2,1,0:T(8,128)(2,1)S(1)}, bf16[2,512,256]{2,1,0:T(8,128)(2,1)S(1)}, u32[]{:S(2)}, u32[]{:S(2)}) %collective-permute-start.3) | collective-permute-done | bytes 524320 | tf_op jit(solution)/shard_map/ppermute | solution.py:243
  52.1 1.6 %residual_last.1 = f32[4,1024,256]{2,1,0:T(8,128)} custom-call(s32[7,49]{1,0:T(8,128)S(1)} %get-tuple-element.20.refs_0_, f32[6,1024,256]{2,1,0:T(8,128)S(1)} %get-tuple-element.29.refs_1_, bf16[2,512,256]{2,1,0:T(8,128)(2,1)S(1)} %collective-permute-done.3.refs_2_, f32[4,1024,256]{2,1,0:T(8,128)} %residual.1.refs_3_), custom_call_target="tpu_custom_call", output_to_operand_aliasing={{}: (3, {})} | custom-call | flops 1 | bytes 1 | tf_op jit(solution)/shard_map/residual_last/pallas_call | solution.py:233
  (3 shorter events, 0.0 us)
Async XLA Ops:
  1.6 6.5 %collective-permute-start = (bf16[2,1024,256]{2,1,0:T(8,128)(2,1)S(1)}, bf16[2,1024,256]{2,1,0:T(8,128)(2,1)S(1)}, u32[]{:S(2)}, u32[]{:S(2)}) collective-permute-start(bf16[2,1024,256]{2,1,0:T(8,128)(2,1)S(1)} %get-tuple-element.19), channel_id=1, source_target_pairs={{0,1},{1,0},{2,3},{3,2},{4,5},{5,4},{6,7},{7,6},{8,9},{9,8},{10,11... | collective-permute-start | bytes 3145736 | tf_op jit(solution)/shard_map/ppermute | solution.py:246
  1.7 21.8 %collective-permute-start.2 = (bf16[2,512,256]{2,1,0:T(8,128)(2,1)S(1)}, bf16[2,512,256]{2,1,0:T(8,128)(2,1)S(1)}, u32[]{:S(2)}, u32[]{:S(2)}) collective-permute-start(bf16[2,512,256]{2,1,0:T(8,128)(2,1)S(1)} %get-tuple-element.23), channel_id=1, source_target_pairs={{1,2},{3,4},{5,6},{7,8},{9,10},{11,12},{13,14},{2,1},{4,3},{6,5},{... | collective-permute-start | bytes 1572872 | tf_op jit(solution)/shard_map/ppermute | solution.py:243
  6.2 25.5 %collective-permute-start.1 = (bf16[2,512,256]{2,1,0:T(8,128)(2,1)S(1)}, bf16[2,512,256]{2,1,0:T(8,128)(2,1)S(1)}, u32[]{:S(2)}, u32[]{:S(2)}) collective-permute-start(bf16[2,512,256]{2,1,0:T(8,128)(2,1)S(1)} %get-tuple-element.21), channel_id=1, source_target_pairs={{1,2},{3,4},{5,6},{7,8},{9,10},{11,12},{13,14},{2,1},{4,3},{6,5},{... | collective-permute-start | bytes 1572872 | tf_op jit(solution)/shard_map/ppermute | solution.py:243
  8.1 0.7 %copy-start = (s32[48,2]{0,1:T(2,128)S(1)}, s32[48,2]{0,1:T(2,128)}, u32[]{:S(2)}) copy-start(s32[48,2]{0,1:T(2,128)} %param.5) | copy-start | bytes 1156
  24.7 21.7 %collective-permute-start.7 = (bf16[2,512,256]{2,1,0:T(8,128)(2,1)S(1)}, bf16[2,512,256]{2,1,0:T(8,128)(2,1)S(1)}, u32[]{:S(2)}, u32[]{:S(2)}) collective-permute-start(bf16[2,512,256]{2,1,0:T(8,128)(2,1)S(1)} %get-tuple-element.26.refs_4_), channel_id=1, source_target_pairs={{1,2},{3,4},{5,6},{7,8},{9,10},{11,12},{13,14},{2,1},{4,3},{6,5},{... | collective-permute-start | bytes 1572872 | tf_op jit(solution)/shard_map/ppermute | solution.py:243
  32.9 19.2 %collective-permute-start.3 = (bf16[2,512,256]{2,1,0:T(8,128)(2,1)S(1)}, bf16[2,512,256]{2,1,0:T(8,128)(2,1)S(1)}, u32[]{:S(2)}, u32[]{:S(2)}) collective-permute-start(bf16[2,512,256]{2,1,0:T(8,128)(2,1)S(1)} %get-tuple-element.28.refs_5_), channel_id=1, source_target_pairs={{1,2},{3,4},{5,6},{7,8},{9,10},{11,12},{13,14},{2,1},{4,3},{6,5},{... | collective-permute-start | bytes 1572872 | tf_op jit(solution)/shard_map/ppermute | solution.py:243
  39.8 2.7 %collective-permute-start.4 = (bf16[2,384,256]{2,1,0:T(8,128)(2,1)S(1)}, bf16[2,384,256]{2,1,0:T(8,128)(2,1)S(1)}, u32[]{:S(2)}, u32[]{:S(2)}) collective-permute-start(bf16[2,384,256]{2,1,0:T(8,128)(2,1)S(1)} %get-tuple-element.30), channel_id=1, source_target_pairs={{0,1},{1,0},{2,3},{3,2},{4,5},{5,4},{6,7},{7,6},{8,9},{9,8},{10,11... | collective-permute-start | bytes 1179656 | tf_op jit(solution)/shard_map/ppermute | solution.py:246
  39.9 2.7 %collective-permute-start.5 = (bf16[2,384,256]{2,1,0:T(8,128)(2,1)S(1)}, bf16[2,384,256]{2,1,0:T(8,128)(2,1)S(1)}, u32[]{:S(2)}, u32[]{:S(2)}) collective-permute-start(bf16[2,384,256]{2,1,0:T(8,128)(2,1)S(1)} %get-tuple-element.31), channel_id=1, source_target_pairs={{0,1},{1,0},{2,3},{3,2},{4,5},{5,4},{6,7},{7,6},{8,9},{9,8},{10,11... | collective-permute-start | bytes 1179656 | tf_op jit(solution)/shard_map/ppermute | solution.py:246
  40.4 2.1 %collective-permute-start.6 = (bf16[2,256,256]{2,1,0:T(8,128)(2,1)S(1)}, bf16[2,256,256]{2,1,0:T(8,128)(2,1)S(1)}, u32[]{:S(2)}, u32[]{:S(2)}) collective-permute-start(bf16[2,256,256]{2,1,0:T(8,128)(2,1)S(1)} %get-tuple-element.32), channel_id=1, source_target_pairs={{0,1},{1,0},{2,3},{3,2},{4,5},{5,4},{6,7},{7,6},{8,9},{9,8},{10,11... | collective-permute-start | bytes 786440 | tf_op jit(solution)/shard_map/ppermute | solution.py:246

commit v2 on v1

v2 whole, which is shorter than its diff:
```python
import functools

import jax
import jax.numpy as jnp
from jax import lax
from jax.experimental import pallas as pl
from jax.experimental.pallas import tpu as pltpu
from jax.sharding import PartitionSpec as P

HALO = 2
SPLIT = (512, 512)
CHIP_SPLIT = (352, 352, 320)
VMEM_LIMIT = 24 * 1024 * 1024

OWN, CHIP, CROSS = 0, 1, 2
LISTS = 9


def row_chunks(rows, split):
    total = sum(split)
    sizes = [rows * part // total for part in split]
    starts = [sum(sizes[:i]) for i in range(len(sizes))]
    return list(zip(starts, sizes))


def vmem():
    return pl.BlockSpec(memory_space=pltpu.VMEM)


def smem():
    return pl.BlockSpec(memory_space=pltpu.SMEM)


def hbm():
    return pl.BlockSpec(memory_space=pltpu.HBM)


def in_vmem(x):
    return pltpu.with_memory_space_constraint(x, pltpu.VMEM)


def in_hbm(x):
    return pltpu.with_memory_space_constraint(x, pltpu.HBM)


def accumulate(plan, which, source, begin, integrals, sums, offset, size):
    blocks = [(r, min(256, size - r)) for r in range(0, size, 256)]
    count = plan[which, plan.shape[1] - 1]

    def some(first, width):
        entries = [plan[which, first + u] for u in range(width)]
        for r, block in blocks:
            products = [
                jnp.dot(
                    source[(entry >> 4) & 15, pl.ds(begin + r, block)],
                    integrals[entry >> 8],
                    preferred_element_type=jnp.float32,
                )
                for entry in entries
            ]
            for entry, product in zip(entries, products):
                sums[entry & 15, pl.ds(offset + r, block)] += product

    def pair(i, carry):
        some(2 * i, 2)
        return carry

    def single(i, carry):
        some(i, 1)
        return carry

    pairs = count // 2
    lax.fori_loop(0, pairs, pair, 0)
    lax.fori_loop(2 * pairs, count, single, 0)


def make_plan(axis, tile_count, tasks, plan):
    odd = lax.rem(lax.axis_index(axis), 2)
    first = lax.axis_index(axis) * tile_count
    last = plan.shape[1] - 1
    for which in range(LISTS):
        plan[which, last] = 0

    def place(tile):
        own = tile - first
        below = own < 0
        above = own >= tile_count
        crossing = jnp.logical_or(
            jnp.logical_and(below, odd == 0), jnp.logical_and(above, odd == 1)
        )
        slot = jnp.where(below, own + HALO, jnp.where(above, own - tile_count, own))
        kind = jnp.where(crossing, CROSS, jnp.where(jnp.logical_or(below, above), CHIP, OWN))
        return slot, kind

    def one(k, carry):
        src, src_kind = place(tasks[0, k])
        dst, dst_kind = place(tasks[1, k])
        which = 3 * src_kind + dst_kind
        count = plan[which, last]
        plan[which, count] = k * 256 + src * 16 + dst
        plan[which, last] = count + 1
        return carry

    lax.fori_loop(0, tasks.shape[1], one, 0)


def edges(axis, tile_count):
    odd = lax.rem(lax.axis_index(axis), 2)
    edge = tile_count - HALO
    return odd * edge, (1 - odd) * edge


def pick_kernel(axis, chunks, amplitudes, *refs):
    *picked, sems = refs
    near, far = edges(axis, amplitudes.shape[0])
    copies = [
        pltpu.make_async_copy(
            amplitudes.at[pl.ds(near, HALO), pl.ds(start, size)], picked[i], sems.at[i]
        )
        for i, (start, size) in enumerate(chunks)
    ]
    i = len(chunks)
    copies.append(
        pltpu.make_async_copy(amplitudes.at[pl.ds(far, HALO)], picked[i], sems.at[i])
    )
    for copy in copies:
        copy.start()
    for copy in copies:
        copy.wait()


def first_kernel(axis, chunks, tasks, amplitudes, integrals, chip, *refs):
    plan, own, held, chip_sums, *sums, sems = refs
    copies = [
        pltpu.make_async_copy(amplitudes, own, sems.at[0]),
        pltpu.make_async_copy(integrals, held, sems.at[1]),
    ]
    for copy in copies:
        copy.start()
    make_plan(axis, amplitudes.shape[0], tasks, plan)
    for ref in [chip_sums, *sums]:
        ref[...] = jnp.zeros_like(ref)
    for copy in copies:
        copy.wait()
    for kind, source in ((OWN, own), (CHIP, chip)):
        for (start, size), total in zip(chunks, sums):
            accumulate(plan, 3 * kind + CROSS, source, start, held, total, 0, size)
        accumulate(plan, 3 * kind + CHIP, source, 0, held, chip_sums, 0, chip.shape[1])


def cross_kernel(plan, integrals, sums, halo, total, rim):
    accumulate(plan, 3 * CROSS + CROSS, halo, 0, integrals, total, 0, halo.shape[1])
    rim[...] = total[...].astype(rim.dtype)


def rims_kernel(chunks, chip_chunks, plan, integrals, sums, chip_sums, *refs):
    halos, (*chip_rims, total, chip_total, rim) = refs[: len(chunks)], refs[len(chunks) :]
    accumulate(plan, 3 * CROSS + CROSS, halos[-1], 0, integrals, total, 0, total.shape[1])
    rim[...] = total[...].astype(rim.dtype)
    for (start, size), halo in zip(chunks, halos):
        accumulate(plan, 3 * CROSS + CHIP, halo, 0, integrals, chip_total, start, size)
    for (start, size), chip_rim in zip(chip_chunks, chip_rims):
        chip_rim[...] = chip_total[:, pl.ds(start, size)].astype(chip_rim.dtype)


def own_kernel(plan, own, integrals, chip, total):
    total[...] = jnp.zeros_like(total)
    accumulate(plan, 3 * OWN + OWN, own, 0, integrals, total, 0, own.shape[1])
    accumulate(plan, 3 * CHIP + OWN, chip, 0, integrals, total, 0, own.shape[1])


def resident_kernel(chunks, plan, integrals, sums, *refs):
    *halos, total = refs
    for (start, size), halo in zip(chunks, halos):
        accumulate(plan, 3 * CROSS + OWN, halo, 0, integrals, total, start, size)


def add_rim(first, chunks, sums, rims, out, part, sems):
    begin, end = chunks[0][0], sum(chunks[-1])
    copies = []
    for j in range(HALO):
        for (start, size), rim in zip(chunks, rims):
            rows = pl.ds(start - begin, size)
            part[j, rows] = sums[first + j, pl.ds(start, size)] + rim[j].astype(jnp.float32)
        target = out.at[first + j, pl.ds(begin, end - begin)]
        copies.append(pltpu.make_async_copy(part.at[j], target, sems.at[j]))
        copies[-1].start()
    for copy in copies:
        copy.wait()


def far_kernel(axis, chip_chunks, sums, *refs):
    rims, (*_, out, part, sems) = refs[: len(chip_chunks)], refs[len(chip_chunks) :]
    add_rim(edges(axis, out.shape[0])[1], chip_chunks, sums, rims, out, part, sems)


def near_kernel(axis, chunk, sums, rim, *refs):
    *_, out, part, sems = refs
    add_rim(edges(axis, out.shape[0])[0], [chunk], sums, [rim], out, part, sems)


def on_device(amplitudes, integrals, tasks):
    tile_count, rows, width = amplitudes.shape
    task_count = integrals.shape[0]
    chunks = row_chunks(rows, SPLIT)
    chip_chunks = row_chunks(rows, CHIP_SPLIT)
    count = len(chunks)
    axis = "own"
    devices = lax.axis_size(axis)
    cross_pairs = [(i, i + 1) for i in range(1, devices - 1, 2)]
    cross_pairs += [(b, a) for a, b in cross_pairs]
    chip_pairs = [(i, i ^ 1) for i in range(devices)]
    f32, bf16, i32 = jnp.float32, amplitudes.dtype, jnp.int32

    def call(kernel, name, operands, in_specs, after=(), **kwargs):
        here = len(operands)

        def body(*refs):
            kernel(*refs[:here], *refs[here + len(after) :])

        return pl.pallas_call(
            body,
            in_specs=in_specs + [pl.BlockSpec(memory_space=pl.ANY)] * len(after),
            compiler_params=pltpu.CompilerParams(vmem_limit_bytes=VMEM_LIMIT),
            cost_estimate=pl.CostEstimate(flops=1, bytes_accessed=1, transcendentals=0),
            name=name,
            **kwargs,
        )(*operands, *after)

    def swap_cross(x):
        return in_vmem(lax.ppermute(x, axis, cross_pairs))

    def swap_chip(x):
        return in_vmem(lax.ppermute(x, axis, chip_pairs))

    amplitudes, integrals = in_hbm(amplitudes), in_hbm(integrals)
    picked = call(
        functools.partial(pick_kernel, axis, chunks),
        "pick",
        [amplitudes],
        [hbm()],
        out_shape=[jax.ShapeDtypeStruct((HALO, size, width), bf16) for _, size in chunks]
        + [jax.ShapeDtypeStruct((HALO, rows, width), bf16)],
        out_specs=[hbm()] * (count + 1),
        scratch_shapes=[pltpu.SemaphoreType.DMA((count + 1,))],
    )
    halos = [swap_cross(x) for x in picked[:count]]
    chip_halo = swap_chip(picked[count])

    edge_shape = pltpu.VMEM((HALO, rows, width), f32)
    plan, own, held, chip_sums, *cross_sums = call(
        functools.partial(first_kernel, axis, chunks),
        "rim_targets",
        [tasks.T, amplitudes, integrals, chip_halo],
        [smem(), hbm(), hbm(), vmem()],
        out_shape=[
            jax.ShapeDtypeStruct((LISTS, task_count + 1), i32),
            pltpu.VMEM(amplitudes.shape, bf16),
            pltpu.VMEM(integrals.shape, bf16),
            edge_shape,
        ]
        + [pltpu.VMEM((HALO, size, width), f32) for _, size in chunks],
        out_specs=[smem()] + [vmem()] * (count + 3),
        scratch_shapes=[pltpu.SemaphoreType.DMA((2,))],
    )
    own, held, chip_sums = in_vmem(own), in_vmem(held), in_vmem(chip_sums)

    rims = []
    after = ()
    for i in range(count - 1):
        size = chunks[i][1]
        _, rim = call(
            cross_kernel,
            "cross_rim",
            [plan, held, in_vmem(cross_sums[i]), halos[i]],
            [smem()] + [vmem()] * 3,
            after=after,
            out_shape=[
                pltpu.VMEM((HALO, size, width), f32),
                pltpu.VMEM((HALO, size, width), bf16),
            ],
            out_specs=[vmem()] * 2,
            input_output_aliases={2: 0},
        )
        rims.append(rim)
        after = [in_vmem(rim)]
    resident_shape = pltpu.VMEM((tile_count, rows, width), f32)
    resident = call(
        own_kernel,
        "own_targets",
        [plan, own, held, chip_halo],
        [smem()] + [vmem()] * 3,
        after=after,
        out_shape=resident_shape,
        out_specs=vmem(),
    )
    resident = in_vmem(resident)
    size = chunks[-1][1]
    *chip_rims, _, _, rim = call(
        functools.partial(rims_kernel, chunks, chip_chunks),
        "last_rims",
        [plan, held, in_vmem(cross_sums[-1]), chip_sums, *halos],
        [smem()] + [vmem()] * (3 + count),
        after=[resident],
        out_shape=[pltpu.VMEM((HALO, part, width), bf16) for _, part in chip_chunks]
        + [
            pltpu.VMEM((HALO, size, width), f32),
            edge_shape,
            pltpu.VMEM((HALO, size, width), bf16),
        ],
        out_specs=[vmem()] * (3 + len(chip_chunks)),
        input_output_aliases={2: len(chip_chunks), 3: len(chip_chunks) + 1},
    )
    rims.append(rim)
    from_chip = [swap_chip(x) for x in chip_rims]
    from_cross = [swap_cross(x) for x in rims]
    resident = call(
        functools.partial(resident_kernel, chunks),
        "cross_sources",
        [plan, held, resident, *halos],
        [smem()] + [vmem()] * (2 + count),
        after=[in_vmem(rim)],
        out_shape=resident_shape,
        out_specs=vmem(),
        input_output_aliases={2: 0},
    )
    resident = in_vmem(resident)

    def write(kernel, name, blocks, length, out=None):
        before = [] if out is None else [out]
        return call(
            kernel,
            name,
            [resident, *blocks, *before],
            [vmem()] * (1 + len(blocks)) + [hbm()] * len(before),
            out_shape=jax.ShapeDtypeStruct((tile_count, rows, width), f32),
            out_specs=hbm(),
            scratch_shapes=[
                pltpu.VMEM((HALO, length, width), f32),
                pltpu.SemaphoreType.DMA((HALO,)),
            ],
            input_output_aliases={1 + len(blocks): 0} if before else {},
        )

    def near(i, out=None):
        kernel = functools.partial(near_kernel, axis, chunks[i])
        return write(kernel, "residual_near", [from_cross[i]], chunks[i][1], out)

    out = near(0)
    out = write(functools.partial(far_kernel, axis, chip_chunks), "residual_far", from_chip, rows, out)
    for i in range(1, count):
        out = near(i, out)
    return out


def solution(mesh):
    return jax.shard_map(
        on_device,
        mesh=mesh,
        in_specs=(
            P(("parts", "own"), None, None),
            P(("parts", "own"), None, None),
            P(("parts", "own"), None),
        ),
        out_specs=P(("parts", "own"), None, None),
        check_vma=False,
    )
```

time: 54.6 us -> 53.6 us (0.982)
  waiting for transfers between devices: 11.6 us -> 9.52 us
  starting transfers between devices: 13.5 us -> 14.5 us
    ppermute x4, waiting for transfers between devices: 2.08 us -> 0.01 us  [swap_chip(): return in_vmem(lax.ppermute(x, axis, chip_pairs))]
    ppermute x4, starting transfers between devices: 12.7 us -> 13.8 us  [swap_cross(): return in_vmem(lax.ppermute(x, axis, cross_pairs))]
  transfers between devices with their start and end apart: 8 -> 8, of which waited for: 4 -> 3; matrix products, arithmetic and copies ran while one was open for 0% -> 0% of each run, Pallas kernels for 46% -> 48%
where the time goes in v2:
time: 53.6 us; the launch traced here: 52.6 us
  Pallas kernels  27.7 us (52%)
  starting transfers between devices  14.5 us (27%)
  waiting for transfers between devices  9.52 us (18%)
  local copies, waits for them, and re-layouts  0.67 us (1%)
    pallas_call x9, Pallas kernels, call(): pl.pallas_call(body, in_specs=in_specs + [pl.BlockSpec(memory_space=pl.AN...  27.7 us
    ppermute x4, starting transfers between devices, swap_cross(): return in_vmem(lax.ppermute(x, axis, cross_pairs))  13.8 us
    ppermute x4, waiting for transfers between devices, swap_cross(): return in_vmem(lax.ppermute(x, axis, cross_pairs))  9.5 us
  transfers between devices with their start and end apart: 8, of which 3 were waited for; matrix products, arithmetic and copies ran while one was open for 0% of the time, Pallas kernels for 48%

profile of v2, /device:TPU:1, one launch (start us, length us, event | category | flops | bytes accessed | tf_op | source)
XLA Modules:
  0.0 52.6 jit_solution(6280171311266283704)
XLA Ops:
  0.0 1.6 %pick.1 = (bf16[2,512,256]{2,1,0:T(8,128)(2,1)S(1)}, bf16[2,512,256]{2,1,0:T(8,128)(2,1)S(1)}, bf16[2,1024,256]{2,1,0:T(8,128)(2,1)S(1)}) custom-call(bf16[4,1024,256]{2,1,0:T(8,128)(2,1)} %refs_1_.1), custom_call_target="tpu_custom_call" | custom-call | flops 1 | bytes 1 | tf_op jit(solution)/shard_map/pick/pallas_call | solution.py:221
  1.6 0.1 collective-permute-start
  1.7 4.5 %collective-permute-start.1 = (bf16[2,512,256]{2,1,0:T(8,128)(2,1)S(1)}, bf16[2,512,256]{2,1,0:T(8,128)(2,1)S(1)}, u32[]{:S(2)}, u32[]{:S(2)}) collective-permute-start(bf16[2,512,256]{2,1,0:T(8,128)(2,1)S(1)} %get-tuple-element.24), channel_id=1, source_target_pairs={{1,2},{3,4},{5,6},{7,8},{9,10},{11,12},{13,14},{2,1},{4,3},{6,5},{... | collective-permute-start | bytes 1572872 | tf_op jit(solution)/shard_map/ppermute | solution.py:231
  6.2 1.9 %collective-permute-start.2 = (bf16[2,512,256]{2,1,0:T(8,128)(2,1)S(1)}, bf16[2,512,256]{2,1,0:T(8,128)(2,1)S(1)}, u32[]{:S(2)}, u32[]{:S(2)}) collective-permute-start(bf16[2,512,256]{2,1,0:T(8,128)(2,1)S(1)} %get-tuple-element.26), channel_id=1, source_target_pairs={{1,2},{3,4},{5,6},{7,8},{9,10},{11,12},{13,14},{2,1},{4,3},{6,5},{... | collective-permute-start | bytes 1572872 | tf_op jit(solution)/shard_map/ppermute | solution.py:231
  8.1 0.0 copy-start
  8.1 0.7 %copy-done = s32[48,2]{0,1:T(2,128)S(1)} copy-done((s32[48,2]{0,1:T(2,128)S(1)}, s32[48,2]{0,1:T(2,128)}, u32[]{:S(2)}) %copy-start) | copy-done | bytes 408
  8.8 9.2 %rim_targets.1 = (s32[9,49]{1,0:T(8,128)S(1)}, bf16[4,1024,256]{2,1,0:T(8,128)(2,1)S(1)}, bf16[48,256,256]{2,1,0:T(8,128)(2,1)S(1)}, f32[2,1024,256]{2,1,0:T(8,1...) custom-call(s32[2,48]{1,0:T(2,128)S(1)} %bitcast.1, bf16[4,1024,256]{2,1,0:T(8,128)(2,1)} %refs_1_.1, ...), custom_call_target="tpu_custom_call" | custom-call | flops 1 | bytes 1 | tf_op jit(solution)/shard_map/rim_targets/pallas_call | solution.py:221
  18.0 5.5 %collective-permute-done.1.refs_3_.refs_4_ = bf16[2,512,256]{2,1,0:T(8,128)(2,1)S(1)} collective-permute-done((bf16[2,512,256]{2,1,0:T(8,128)(2,1)S(1)}, bf16[2,512,256]{2,1,0:T(8,128)(2,1)S(1)}, u32[]{:S(2)}, u32[]{:S(2)}) %collective-permute-start.1) | collective-permute-done | bytes 524320 | tf_op jit(solution)/shard_map/ppermute | solution.py:231
  23.5 1.9 %cross_rim.1 = (f32[2,512,256]{2,1,0:T(8,128)S(1)}, bf16[2,512,256]{2,1,0:T(8,128)(2,1)S(1)}) custom-call(s32[9,49]{1,0:T(8,128)S(1)} %get-tuple-element.20.refs_0_, bf16[48,256,256]{2,1,0:T(8,128)(2,1)S(1)} %get-tuple-element.21.refs_1_.refs_2_, f32[2,512,256]{2,1,0:T(8,128)S(1)} %get-tuple-element.23.refs_2_, ...), custom_call_target="tpu_custom_call", output_to_operand_aliasing={{0}: (2, {})} | custom-call | flops 1 | bytes 1 | tf_op jit(solution)/shard_map/cross_rim/pallas_call | solution.py:221
  25.5 4.1 %collective-permute-start.7 = (bf16[2,512,256]{2,1,0:T(8,128)(2,1)S(1)}, bf16[2,512,256]{2,1,0:T(8,128)(2,1)S(1)}, u32[]{:S(2)}, u32[]{:S(2)}) collective-permute-start(bf16[2,512,256]{2,1,0:T(8,128)(2,1)S(1)} %get-tuple-element.25.refs_4_), channel_id=1, source_target_pairs={{1,2},{3,4},{5,6},{7,8},{9,10},{11,12},{13,14},{2,1},{4,3},{6,5},{... | collective-permute-start | bytes 1572872 | tf_op jit(solution)/shard_map/ppermute | solution.py:231
  29.5 5.3 %own_targets.1.refs_6_.refs_2_ = f32[4,1024,256]{2,1,0:T(8,128)S(1)} custom-call(s32[9,49]{1,0:T(8,128)S(1)} %get-tuple-element.20.refs_0_, bf16[4,1024,256]{2,1,0:T(8,128)(2,1)S(1)} %get-tuple-element.22.refs_1_, bf16[48,256,256]{2,1,0:T(8,128)(2,1)S(1)} %get-tuple-element.21.refs_1_.refs_2_, bf16[2,1024,256]{2,1,0:T(8,128)(2,1)S(1)} %collective-permute-done.refs_3_, ...), custom_call_target="tpu_custom_call" | custom-call | flops 1 | bytes 1 | tf_op jit(solution)/shard_map/own_targets/pallas_call | solution.py:221
  34.8 0.0 collective-permute-done.2.refs_5_.refs_4_
  34.9 3.8 %last_rims.1 = (bf16[2,352,256]{2,1,0:T(8,128)(2,1)S(1)}, bf16[2,352,256]{2,1,0:T(8,128)(2,1)S(1)}, bf16[2,320,256]{2,1,0:T(8,128)(2,1)S(1)}, f32[2,512,256]{2,1...) custom-call(s32[9,49]{1,0:T(8,128)S(1)} %get-tuple-element.20.refs_0, ...), custom_call_target="tpu_custom_call", output_to_operand_aliasing={{3}: (2, {}), {4}: (3, {})} | custom-call | flops 1 | bytes 1 | tf_op jit(solution)/shard_map/last_rims/pallas_call | solution.py:221
  38.7 3.3 %collective-permute-start.3 = (bf16[2,512,256]{2,1,0:T(8,128)(2,1)S(1)}, bf16[2,512,256]{2,1,0:T(8,128)(2,1)S(1)}, u32[]{:S(2)}, u32[]{:S(2)}) collective-permute-start(bf16[2,512,256]{2,1,0:T(8,128)(2,1)S(1)} %get-tuple-element.29.refs_5_), channel_id=1, source_target_pairs={{1,2},{3,4},{5,6},{7,8},{9,10},{11,12},{13,14},{2,1},{4,3},{6,5},{... | collective-permute-start | bytes 1572872 | tf_op jit(solution)/shard_map/ppermute | solution.py:231
  42.0 0.1 collective-permute-start.4
  42.1 0.5 collective-permute-start.5
  42.6 0.1 collective-permute-start.6
  42.7 2.5 %cross_sources.1.refs_0_ = f32[4,1024,256]{2,1,0:T(8,128)S(1)} custom-call(s32[9,49]{1,0:T(8,128)S(1)} %get-tuple-element.20.refs_0_, bf16[48,256,256]{2,1,0:T(8,128)(2,1)S(1)} %get-tuple-element.21.refs_1_.refs_2_, f32[4,1024,256]{2,1,0:T(8,128)S(1)} %own_targets.1.refs_6_.refs_2_, ...), custom_call_target="tpu_custom_call", output_to_operand_aliasing={{}: (2, {})} | custom-call | flops 1 | bytes 1 | tf_op jit(solution)/shard_map/cross_sources/pallas_call | solution.py:221
  45.1 0.8 %collective-permute-done.7.refs_1_ = bf16[2,512,256]{2,1,0:T(8,128)(2,1)S(1)} collective-permute-done((bf16[2,512,256]{2,1,0:T(8,128)(2,1)S(1)}, bf16[2,512,256]{2,1,0:T(8,128)(2,1)S(1)}, u32[]{:S(2)}, u32[]{:S(2)}) %collective-permute-start.7) | collective-permute-done | bytes 524320 | tf_op jit(solution)/shard_map/ppermute | solution.py:231
  46.0 1.0 %residual_near.2.refs_4_ = f32[4,1024,256]{2,1,0:T(8,128)} custom-call(f32[4,1024,256]{2,1,0:T(8,128)S(1)} %cross_sources.1.refs_0_, bf16[2,512,256]{2,1,0:T(8,128)(2,1)S(1)} %collective-permute-done.7.refs_1_), custom_call_target="tpu_custom_call" | custom-call | flops 1 | bytes 1 | tf_op jit(solution)/shard_map/residual_near/pallas_call | solution.py:221
  47.0 0.0 collective-permute-done.4.refs_1_
  47.1 1.4 %residual_far.1.refs_2_ = f32[4,1024,256]{2,1,0:T(8,128)} custom-call(f32[4,1024,256]{2,1,0:T(8,128)S(1)} %cross_sources.1.refs_0_, bf16[2,352,256]{2,1,0:T(8,128)(2,1)S(1)} %collective-permute-done.4.refs_1_, bf16[2,352,256]{2,1,0:T(8,128)(2,1)S(1)} %collective-permute-done.5.refs_2_, ...), custom_call_target="tpu_custom_call", output_to_operand_aliasing={{}: (4, {})} | custom-call | flops 1 | bytes 1 | tf_op jit(solution)/shard_map/residual_far/pallas_call | solution.py:221
  48.5 3.1 %collective-permute-done.3.refs_1_ = bf16[2,512,256]{2,1,0:T(8,128)(2,1)S(1)} collective-permute-done((bf16[2,512,256]{2,1,0:T(8,128)(2,1)S(1)}, bf16[2,512,256]{2,1,0:T(8,128)(2,1)S(1)}, u32[]{:S(2)}, u32[]{:S(2)}) %collective-permute-start.3) | collective-permute-done | bytes 524320 | tf_op jit(solution)/shard_map/ppermute | solution.py:231
  51.6 1.0 %residual_near.3 = f32[4,1024,256]{2,1,0:T(8,128)} custom-call(f32[4,1024,256]{2,1,0:T(8,128)S(1)} %cross_sources.1.refs_0_, bf16[2,512,256]{2,1,0:T(8,128)(2,1)S(1)} %collective-permute-done.3.refs_1_, f32[4,1024,256]{2,1,0:T(8,128)} %residual_far.1.refs_2_), custom_call_target="tpu_custom_call", output_to_operand_aliasing={{}: (2, {})} | custom-call | flops 1 | bytes 1 | tf_op jit(solution)/shard_map/residual_near/pallas_call | solution.py:221
  (3 shorter events, 0.0 us)
Async XLA Ops:
  1.6 6.5 %collective-permute-start = (bf16[2,1024,256]{2,1,0:T(8,128)(2,1)S(1)}, bf16[2,1024,256]{2,1,0:T(8,128)(2,1)S(1)}, u32[]{:S(2)}, u32[]{:S(2)}) collective-permute-start(bf16[2,1024,256]{2,1,0:T(8,128)(2,1)S(1)} %get-tuple-element.19), channel_id=1, source_target_pairs={{0,1},{1,0},{2,3},{3,2},{4,5},{5,4},{6,7},{7,6},{8,9},{9,8},{10,11... | collective-permute-start | bytes 3145736 | tf_op jit(solution)/shard_map/ppermute | solution.py:234
  1.7 21.8 %collective-permute-start.1 = (bf16[2,512,256]{2,1,0:T(8,128)(2,1)S(1)}, bf16[2,512,256]{2,1,0:T(8,128)(2,1)S(1)}, u32[]{:S(2)}, u32[]{:S(2)}) collective-permute-start(bf16[2,512,256]{2,1,0:T(8,128)(2,1)S(1)} %get-tuple-element.24), channel_id=1, source_target_pairs={{1,2},{3,4},{5,6},{7,8},{9,10},{11,12},{13,14},{2,1},{4,3},{6,5},{... | collective-permute-start | bytes 1572872 | tf_op jit(solution)/shard_map/ppermute | solution.py:231
  6.2 28.7 %collective-permute-start.2 = (bf16[2,512,256]{2,1,0:T(8,128)(2,1)S(1)}, bf16[2,512,256]{2,1,0:T(8,128)(2,1)S(1)}, u32[]{:S(2)}, u32[]{:S(2)}) collective-permute-start(bf16[2,512,256]{2,1,0:T(8,128)(2,1)S(1)} %get-tuple-element.26), channel_id=1, source_target_pairs={{1,2},{3,4},{5,6},{7,8},{9,10},{11,12},{13,14},{2,1},{4,3},{6,5},{... | collective-permute-start | bytes 1572872 | tf_op jit(solution)/shard_map/ppermute | solution.py:231
  8.1 0.7 %copy-start = (s32[48,2]{0,1:T(2,128)S(1)}, s32[48,2]{0,1:T(2,128)}, u32[]{:S(2)}) copy-start(s32[48,2]{0,1:T(2,128)} %param.5) | copy-start | bytes 1156
  25.5 20.5 %collective-permute-start.7 = (bf16[2,512,256]{2,1,0:T(8,128)(2,1)S(1)}, bf16[2,512,256]{2,1,0:T(8,128)(2,1)S(1)}, u32[]{:S(2)}, u32[]{:S(2)}) collective-permute-start(bf16[2,512,256]{2,1,0:T(8,128)(2,1)S(1)} %get-tuple-element.25.refs_4_), channel_id=1, source_target_pairs={{1,2},{3,4},{5,6},{7,8},{9,10},{11,12},{13,14},{2,1},{4,3},{6,5},{... | collective-permute-start | bytes 1572872 | tf_op jit(solution)/shard_map/ppermute | solution.py:231
  38.7 12.9 %collective-permute-start.3 = (bf16[2,512,256]{2,1,0:T(8,128)(2,1)S(1)}, bf16[2,512,256]{2,1,0:T(8,128)(2,1)S(1)}, u32[]{:S(2)}, u32[]{:S(2)}) collective-permute-start(bf16[2,512,256]{2,1,0:T(8,128)(2,1)S(1)} %get-tuple-element.29.refs_5_), channel_id=1, source_target_pairs={{1,2},{3,4},{5,6},{7,8},{9,10},{11,12},{13,14},{2,1},{4,3},{6,5},{... | collective-permute-start | bytes 1572872 | tf_op jit(solution)/shard_map/ppermute | solution.py:231
  42.0 5.0 %collective-permute-start.4 = (bf16[2,352,256]{2,1,0:T(8,128)(2,1)S(1)}, bf16[2,352,256]{2,1,0:T(8,128)(2,1)S(1)}, u32[]{:S(2)}, u32[]{:S(2)}) collective-permute-start(bf16[2,352,256]{2,1,0:T(8,128)(2,1)S(1)} %get-tuple-element.30), channel_id=1, source_target_pairs={{0,1},{1,0},{2,3},{3,2},{4,5},{5,4},{6,7},{7,6},{8,9},{9,8},{10,11... | collective-permute-start | bytes 1081352 | tf_op jit(solution)/shard_map/ppermute | solution.py:234
  42.1 5.0 %collective-permute-start.5 = (bf16[2,352,256]{2,1,0:T(8,128)(2,1)S(1)}, bf16[2,352,256]{2,1,0:T(8,128)(2,1)S(1)}, u32[]{:S(2)}, u32[]{:S(2)}) collective-permute-start(bf16[2,352,256]{2,1,0:T(8,128)(2,1)S(1)} %get-tuple-element.31), channel_id=1, source_target_pairs={{0,1},{1,0},{2,3},{3,2},{4,5},{5,4},{6,7},{7,6},{8,9},{9,8},{10,11... | collective-permute-start | bytes 1081352 | tf_op jit(solution)/shard_map/ppermute | solution.py:234
  42.6 4.4 %collective-permute-start.6 = (bf16[2,320,256]{2,1,0:T(8,128)(2,1)S(1)}, bf16[2,320,256]{2,1,0:T(8,128)(2,1)S(1)}, u32[]{:S(2)}, u32[]{:S(2)}) collective-permute-start(bf16[2,320,256]{2,1,0:T(8,128)(2,1)S(1)} %get-tuple-element.32), channel_id=1, source_target_pairs={{0,1},{1,0},{2,3},{3,2},{4,5},{5,4},{6,7},{7,6},{8,9},{9,8},{10,11... | collective-permute-start | bytes 983048 | tf_op jit(solution)/shard_map/ppermute | solution.py:234

commit v3 on v2

--- a/solution.py
+++ b/solution.py
@@ -9,7 +9,7 @@
 
 HALO = 2
 SPLIT = (512, 512)
-CHIP_SPLIT = (352, 352, 320)
+CHIP_SPLIT = (384, 384, 256)
 VMEM_LIMIT = 24 * 1024 * 1024
 
 OWN, CHIP, CROSS = 0, 1, 2
@@ -43,23 +43,24 @@
     return pltpu.with_memory_space_constraint(x, pltpu.HBM)
 
 
-def accumulate(plan, which, source, begin, integrals, sums, offset, size):
-    blocks = [(r, min(256, size - r)) for r in range(0, size, 256)]
+def accumulate(plan, which, integrals, segments):
     count = plan[which, plan.shape[1] - 1]
 
     def some(first, width):
         entries = [plan[which, first + u] for u in range(width)]
-        for r, block in blocks:
-            products = [
-                jnp.dot(
-                    source[(entry >> 4) & 15, pl.ds(begin + r, block)],
-                    integrals[entry >> 8],
-                    preferred_element_type=jnp.float32,
-                )
-                for entry in entries
-            ]
-            for entry, product in zip(entries, products):
-                sums[entry & 15, pl.ds(offset + r, block)] += product
+        for source, begin, sums, offset, size in segments:
+            for r in range(0, size, 256):
+                block = min(256, size - r)
+                products = [
+                    jnp.dot(
+                        source[(entry >> 4) & 15, pl.ds(begin + r, block)],
+                        integrals[entry >> 8],
+                        preferred_element_type=jnp.float32,
+                    )
+                    for entry in entries
+                ]
+                for entry, product in zip(entries, products):
+                    sums[entry & 15, pl.ds(offset + r, block)] += product
 
     def pair(i, carry):
         some(2 * i, 2)
@@ -72,6 +73,21 @@
     pairs = count // 2
     lax.fori_loop(0, pairs, pair, 0)
     lax.fori_loop(2 * pairs, count, single, 0)
+
+
+def overlaps(sources, totals):
+    out = []
+    start = 0
+    for source in sources:
+        end = start + source.shape[1]
+        first = 0
+        for total in totals:
+            low, high = max(start, first), min(end, first + total.shape[1])
+            if low < high:
+                out.append((source, low - start, total, low - first, high - low))
+            first += total.shape[1]
+        start = end
+    return out
 
 
 def make_plan(axis, tile_count, tasks, plan):
@@ -112,67 +128,73 @@
 
 def pick_kernel(axis, chunks, amplitudes, *refs):
     *picked, sems = refs
-    near, far = edges(axis, amplitudes.shape[0])
+    near, _ = edges(axis, amplitudes.shape[0])
     copies = [
         pltpu.make_async_copy(
             amplitudes.at[pl.ds(near, HALO), pl.ds(start, size)], picked[i], sems.at[i]
         )
         for i, (start, size) in enumerate(chunks)
     ]
-    i = len(chunks)
-    copies.append(
-        pltpu.make_async_copy(amplitudes.at[pl.ds(far, HALO)], picked[i], sems.at[i])
-    )
     for copy in copies:
         copy.start()
     for copy in copies:
         copy.wait()
 
 
-def first_kernel(axis, chunks, tasks, amplitudes, integrals, chip, *refs):
-    plan, own, held, chip_sums, *sums, sems = refs
+def load_kernel(axis, chip_chunks, tasks, amplitudes, integrals, plan, own, held, *refs):
+    *picked, sems = refs
+    _, far = edges(axis, amplitudes.shape[0])
     copies = [
         pltpu.make_async_copy(amplitudes, own, sems.at[0]),
         pltpu.make_async_copy(integrals, held, sems.at[1]),
     ]
+    for i, (start, size) in enumerate(chip_chunks):
+        block = amplitudes.at[pl.ds(far, HALO), pl.ds(start, size)]
+        copies.append(pltpu.make_async_copy(block, picked[i], sems.at[2 + i]))
     for copy in copies:
         copy.start()
     make_plan(axis, amplitudes.shape[0], tasks, plan)
+    for copy in copies:
+        copy.wait()
+
+
+def own_rims_kernel(plan, own, integrals, chip_sums, *sums):
     for ref in [chip_sums, *sums]:
         ref[...] = jnp.zeros_like(ref)
-    for copy in copies:
-        copy.wait()
-    for kind, source in ((OWN, own), (CHIP, chip)):
-        for (start, size), total in zip(chunks, sums):
-            accumulate(plan, 3 * kind + CROSS, source, start, held, total, 0, size)
-        accumulate(plan, 3 * kind + CHIP, source, 0, held, chip_sums, 0, chip.shape[1])
+    accumulate(plan, 3 * OWN + CROSS, integrals, overlaps([own], sums))
+    accumulate(plan, 3 * OWN + CHIP, integrals, overlaps([own], [chip_sums]))
+
+
+def chip_rims_kernel(parts, plan, integrals, *refs):
+    chip, refs = refs[:parts], refs[parts:]
+    chip_total, *totals = refs[len(refs) // 2 :]
+    accumulate(plan, 3 * CHIP + CROSS, integrals, overlaps(chip, totals))
+    accumulate(plan, 3 * CHIP + CHIP, integrals, overlaps(chip, [chip_total]))
 
 
 def cross_kernel(plan, integrals, sums, halo, total, rim):
-    accumulate(plan, 3 * CROSS + CROSS, halo, 0, integrals, total, 0, halo.shape[1])
+    accumulate(plan, 3 * CROSS + CROSS, integrals, overlaps([halo], [total]))
     rim[...] = total[...].astype(rim.dtype)
 
 
-def rims_kernel(chunks, chip_chunks, plan, integrals, sums, chip_sums, *refs):
-    halos, (*chip_rims, total, chip_total, rim) = refs[: len(chunks)], refs[len(chunks) :]
-    accumulate(plan, 3 * CROSS + CROSS, halos[-1], 0, integrals, total, 0, total.shape[1])
+def rims_kernel(count, chip_chunks, plan, integrals, sums, chip_sums, *refs):
+    halos, (*chip_rims, total, chip_total, rim) = refs[:count], refs[count:]
+    accumulate(plan, 3 * CROSS + CROSS, integrals, overlaps([halos[-1]], [total]))
     rim[...] = total[...].astype(rim.dtype)
-    for (start, size), halo in zip(chunks, halos):
-        accumulate(plan, 3 * CROSS + CHIP, halo, 0, integrals, chip_total, start, size)
+    accumulate(plan, 3 * CROSS + CHIP, integrals, overlaps(halos, [chip_total]))
     for (start, size), chip_rim in zip(chip_chunks, chip_rims):
         chip_rim[...] = chip_total[:, pl.ds(start, size)].astype(chip_rim.dtype)
 
 
-def own_kernel(plan, own, integrals, chip, total):
+def own_kernel(plan, own, integrals, total):
     total[...] = jnp.zeros_like(total)
-    accumulate(plan, 3 * OWN + OWN, own, 0, integrals, total, 0, own.shape[1])
-    accumulate(plan, 3 * CHIP + OWN, chip, 0, integrals, total, 0, own.shape[1])
-
-
-def resident_kernel(chunks, plan, integrals, sums, *refs):
+    accumulate(plan, 3 * OWN + OWN, integrals, overlaps([own], [total]))
+
+
+def resident_kernel(parts, plan, integrals, sums, *refs):
     *halos, total = refs
-    for (start, size), halo in zip(chunks, halos):
-        accumulate(plan, 3 * CROSS + OWN, halo, 0, integrals, total, start, size)
+    accumulate(plan, 3 * CHIP + OWN, integrals, overlaps(halos[:parts], [total]))
+    accumulate(plan, 3 * CROSS + OWN, integrals, overlaps(halos[parts:], [total]))
 
 
 def add_rim(first, chunks, sums, rims, out, part, sems):
@@ -239,31 +261,52 @@
         "pick",
         [amplitudes],
         [hbm()],
-        out_shape=[jax.ShapeDtypeStruct((HALO, size, width), bf16) for _, size in chunks]
-        + [jax.ShapeDtypeStruct((HALO, rows, width), bf16)],
-        out_specs=[hbm()] * (count + 1),
-        scratch_shapes=[pltpu.SemaphoreType.DMA((count + 1,))],
-    )
-    halos = [swap_cross(x) for x in picked[:count]]
-    chip_halo = swap_chip(picked[count])
-
-    edge_shape = pltpu.VMEM((HALO, rows, width), f32)
-    plan, own, held, chip_sums, *cross_sums = call(
-        functools.partial(first_kernel, axis, chunks),
-        "rim_targets",
-        [tasks.T, amplitudes, integrals, chip_halo],
-        [smem(), hbm(), hbm(), vmem()],
+        out_shape=[jax.ShapeDtypeStruct((HALO, size, width), bf16) for _, size in chunks],
+        out_specs=[hbm()] * count,
+        scratch_shapes=[pltpu.SemaphoreType.DMA((count,))],
+    )
+    halos = [swap_cross(x) for x in picked]
+
+    parts = len(chip_chunks)
+    plan, own, held, *chip_picked = call(
+        functools.partial(load_kernel, axis, chip_chunks),
+        "load",
+        [tasks.T, amplitudes, integrals],
+        [smem(), hbm(), hbm()],
+        after=picked,
         out_shape=[
             jax.ShapeDtypeStruct((LISTS, task_count + 1), i32),
             pltpu.VMEM(amplitudes.shape, bf16),
             pltpu.VMEM(integrals.shape, bf16),
-            edge_shape,
         ]
-        + [pltpu.VMEM((HALO, size, width), f32) for _, size in chunks],
-        out_specs=[smem()] + [vmem()] * (count + 3),
-        scratch_shapes=[pltpu.SemaphoreType.DMA((2,))],
-    )
-    own, held, chip_sums = in_vmem(own), in_vmem(held), in_vmem(chip_sums)
+        + [pltpu.VMEM((HALO, size, width), bf16) for _, size in chip_chunks],
+        out_specs=[smem()] + [vmem()] * (2 + parts),
+        scratch_shapes=[pltpu.SemaphoreType.DMA((2 + parts,))],
+    )
+    own, held = in_vmem(own), in_vmem(held)
+    chip_halos = [swap_chip(x) for x in chip_picked]
+
+    edge_shape = pltpu.VMEM((HALO, rows, width), f32)
+    sums_shapes = [edge_shape] + [pltpu.VMEM((HALO, size, width), f32) for _, size in chunks]
+    sums = call(
+        own_rims_kernel,
+        "own_rims",
+        [plan, own, held],
+        [smem()] + [vmem()] * 2,
+        after=[in_vmem(x) for x in chip_picked],
+        out_shape=sums_shapes,
+        out_specs=[vmem()] * (count + 1),
+    )
+    chip_sums, *cross_sums = call(
+        functools.partial(chip_rims_kernel, parts),
+        "chip_rims",
+        [plan, held, *chip_halos, *[in_vmem(x) for x in sums]],
+        [smem()] + [vmem()] * (count + 2 + parts),
+        out_shape=sums_shapes,
+        out_specs=[vmem()] * (count + 1),
+        input_output_aliases={2 + parts + i: i for i in range(count + 1)},
+    )
+    chip_sums = in_vmem(chip_sums)
 
     rims = []
     after = ()
@@ -288,8 +331,8 @@
     resident = call(
         own_kernel,
         "own_targets",
-        [plan, own, held, chip_halo],
-        [smem()] + [vmem()] * 3,
+        [plan, own, held],
+        [smem()] + [vmem()] * 2,
         after=after,
         out_shape=resident_shape,
         out_specs=vmem(),
@@ -297,7 +340,7 @@
     resident = in_vmem(resident)
     size = chunks[-1][1]
     *chip_rims, _, _, rim = call(
-        functools.partial(rims_kernel, chunks, chip_chunks),
+        functools.partial(rims_kernel, count, chip_chunks),
         "last_rims",
         [plan, held, in_vmem(cross_sums[-1]), chip_sums, *halos],
         [smem()] + [vmem()] * (3 + count),
@@ -315,10 +358,10 @@
     from_chip = [swap_chip(x) for x in chip_rims]
     from_cross = [swap_cross(x) for x in rims]
     resident = call(
-        functools.partial(resident_kernel, chunks),
-        "cross_sources",
-        [plan, held, resident, *halos],
-        [smem()] + [vmem()] * (2 + count),
+        functools.partial(resident_kernel, parts),
+        "halo_sources",
+        [plan, held, resident, *chip_halos, *halos],
+        [smem()] + [vmem()] * (2 + parts + count),
         after=[in_vmem(rim)],
         out_shape=resident_shape,
         out_specs=vmem(),

time: 53.6 us -> 52.7 us (0.983)
  starting transfers between devices: 14.5 us -> 16 us
  waiting for transfers between devices: 9.52 us -> 8.38 us
  Pallas kernels: 27.7 us -> 27 us
    ppermute x4, waiting for transfers between devices: 9.5 us -> 8.36 us  [swap_cross(): return in_vmem(lax.ppermute(x, axis, cross_pairs))]
    ppermute x4, starting transfers between devices: 13.8 us -> 14.7 us  [swap_cross(): return in_vmem(lax.ppermute(x, axis, cross_pairs))]
    pallas_call x9 -> x11, Pallas kernels: 27.7 us -> 27 us  [call(): pl.pallas_call(body, in_specs=in_specs + [pl.BlockSpec(memory_space=pl.AN...]
    ppermute x4 -> x6, starting transfers between devices: 0.77 us -> 1.29 us  [swap_chip(): return in_vmem(lax.ppermute(x, axis, chip_pairs))]
  transfers between devices with their start and end apart: 8 -> 10, of which waited for: 3 -> 4; matrix products, arithmetic and copies ran while one was open for 0% -> 0% of each run, Pallas kernels for 48% -> 47%
where the time goes in v3:
time: 52.7 us; the launch traced here: 52.2 us
  Pallas kernels  27 us (51%)
  starting transfers between devices  16 us (30%)
  waiting for transfers between devices  8.38 us (16%)
  local copies, waits for them, and re-layouts  0.67 us (1%)
    pallas_call x11, Pallas kernels, call(): pl.pallas_call(body, in_specs=in_specs + [pl.BlockSpec(memory_space=pl.AN...  27 us
    ppermute x4, starting transfers between devices, swap_cross(): return in_vmem(lax.ppermute(x, axis, cross_pairs))  14.7 us
    ppermute x4, waiting for transfers between devices, swap_cross(): return in_vmem(lax.ppermute(x, axis, cross_pairs))  8.36 us
    ppermute x6, starting transfers between devices, swap_chip(): return in_vmem(lax.ppermute(x, axis, chip_pairs))  1.29 us
  transfers between devices with their start and end apart: 10, of which 4 were waited for; matrix products, arithmetic and copies ran while one was open for 0% of the time, Pallas kernels for 47%

profile of v3, /device:TPU:1, one launch (start us, length us, event | category | flops | bytes accessed | tf_op | source)
XLA Modules:
  0.0 52.2 jit_solution(10525703076055032077)
XLA Ops:
  0.0 1.2 %pick.1 = (bf16[2,512,256]{2,1,0:T(8,128)(2,1)S(1)}, bf16[2,512,256]{2,1,0:T(8,128)(2,1)S(1)}) custom-call(bf16[4,1024,256]{2,1,0:T(8,128)(2,1)} %refs_1_.1), custom_call_target="tpu_custom_call" | custom-call | flops 1 | bytes 1 | tf_op jit(solution)/shard_map/pick/pallas_call | solution.py:243
  1.2 4.5 %collective-permute-start.3 = (bf16[2,512,256]{2,1,0:T(8,128)(2,1)S(1)}, bf16[2,512,256]{2,1,0:T(8,128)(2,1)S(1)}, u32[]{:S(2)}, u32[]{:S(2)}) collective-permute-start(bf16[2,512,256]{2,1,0:T(8,128)(2,1)S(1)} %get-tuple-element.24.refs_3_), channel_id=1, source_target_pairs={{1,2},{3,4},{5,6},{7,8},{9,10},{11,12},{13,14},{2,1},{4,3},{6,5},{... | collective-permute-start | bytes 1572872 | tf_op jit(solution)/shard_map/ppermute | solution.py:253
  5.7 1.9 %collective-permute-start.4 = (bf16[2,512,256]{2,1,0:T(8,128)(2,1)S(1)}, bf16[2,512,256]{2,1,0:T(8,128)(2,1)S(1)}, u32[]{:S(2)}, u32[]{:S(2)}) collective-permute-start(bf16[2,512,256]{2,1,0:T(8,128)(2,1)S(1)} %get-tuple-element.25.refs_4_), channel_id=1, source_target_pairs={{1,2},{3,4},{5,6},{7,8},{9,10},{11,12},{13,14},{2,1},{4,3},{6,5},{... | collective-permute-start | bytes 1572872 | tf_op jit(solution)/shard_map/ppermute | solution.py:253
  7.7 0.7 %copy-done = s32[48,2]{0,1:T(2,128)S(1)} copy-done((s32[48,2]{0,1:T(2,128)S(1)}, s32[48,2]{0,1:T(2,128)}, u32[]{:S(2)}) %copy-start) | copy-done | bytes 408
  8.4 4.9 %load.1 = (s32[9,49]{1,0:T(8,128)S(1)}, bf16[4,1024,256]{2,1,0:T(8,128)(2,1)S(1)}, bf16[48,256,256]{2,1,0:T(8,128)(2,1)S(1)}, bf16[2,384,256]{2,1,0:T(8,128)(2,1...) custom-call(s32[2,48]{1,0:T(2,128)S(1)} %bitcast.1, bf16[4,1024,256]{2,1,0:T(8,128)(2,1)} %refs_1_.1, ...), custom_call_target="tpu_custom_call" | custom-call | flops 1 | bytes 1 | tf_op jit(solution)/shard_map/load/pallas_call | solution.py:243
  13.4 0.5 collective-permute-start.1
  13.9 0.1 collective-permute-start.2
  13.9 4.5 %own_rims.1 = (f32[2,1024,256]{2,1,0:T(8,128)S(1)}, f32[2,512,256]{2,1,0:T(8,128)S(1)}, f32[2,512,256]{2,1,0:T(8,128)S(1)}) custom-call(s32[9,49]{1,0:T(8,128)S(1)} %get-tuple-element.26.refs_0_, bf16[4,1024,256]{2,1,0:T(8,128)(2,1)S(1)} %get-tuple-element.28.refs_1_, bf16[48,256,256]{2,1,0:T(8,128)(2,1)S(1)} %get-tuple-element.27.refs_2_.refs_1_, ...), custom_call_target="tpu_custom_call" | custom-call | flops 1 | bytes 1 | tf_op jit(solution)/shard_map/own_rims/pallas_call | solution.py:243
  18.5 3.6 %chip_rims.1 = (f32[2,1024,256]{2,1,0:T(8,128)S(1)}, f32[2,512,256]{2,1,0:T(8,128)S(1)}, f32[2,512,256]{2,1,0:T(8,128)S(1)}) custom-call(s32[9,49]{1,0:T(8,128)S(1)} %get-tuple-element.26.refs_0_, bf16[48,256,256]{2,1,0:T(8,128)(2,1)S(1)} %get-tuple-element.27.refs_2_.refs_1_, ...), custom_call_target="tpu_custom_call", output_to_operand_aliasing={{0}: (5, {}), {1}: (6, {}), {2}: (7, {})} | custom-call | flops 1 | bytes 1 | tf_op jit(solution)/shard_map/chip_rims/pallas_call | solution.py:243
  22.1 0.9 %collective-permute-done.3.refs_3_.refs_4_.refs_6_ = bf16[2,512,256]{2,1,0:T(8,128)(2,1)S(1)} collective-permute-done((bf16[2,512,256]{2,1,0:T(8,128)(2,1)S(1)}, bf16[2,512,256]{2,1,0:T(8,128)(2,1)S(1)}, u32[]{:S(2)}, u32[]{:S(2)}) %collective-permute-start.3) | collective-permute-done | bytes 524320 | tf_op jit(solution)/shard_map/ppermute | solution.py:253
  23.1 1.3 %cross_rim.1 = (f32[2,512,256]{2,1,0:T(8,128)S(1)}, bf16[2,512,256]{2,1,0:T(8,128)(2,1)S(1)}) custom-call(s32[9,49]{1,0:T(8,128)S(1)} %get-tuple-element.26.refs_0_, bf16[48,256,256]{2,1,0:T(8,128)(2,1)S(1)} %get-tuple-element.27.refs_2_.refs_1_, f32[2,512,256]{2,1,0:T(8,128)S(1)} %get-tuple-element.35.refs_2_, ...), custom_call_target="tpu_custom_call", output_to_operand_aliasing={{0}: (2, {})} | custom-call | flops 1 | bytes 1 | tf_op jit(solution)/shard_map/cross_rim/pallas_call | solution.py:243
  24.4 4.4 %collective-permute-start.9 = (bf16[2,512,256]{2,1,0:T(8,128)(2,1)S(1)}, bf16[2,512,256]{2,1,0:T(8,128)(2,1)S(1)}, u32[]{:S(2)}, u32[]{:S(2)}) collective-permute-start(bf16[2,512,256]{2,1,0:T(8,128)(2,1)S(1)} %get-tuple-element.36.refs_3_), channel_id=1, source_target_pairs={{1,2},{3,4},{5,6},{7,8},{9,10},{11,12},{13,14},{2,1},{4,3},{6,5},{... | collective-permute-start | bytes 1572872 | tf_op jit(solution)/shard_map/ppermute | solution.py:253
  28.8 2.7 %own_targets.1.refs_6_.refs_2_ = f32[4,1024,256]{2,1,0:T(8,128)S(1)} custom-call(s32[9,49]{1,0:T(8,128)S(1)} %get-tuple-element.26.refs_0_, bf16[4,1024,256]{2,1,0:T(8,128)(2,1)S(1)} %get-tuple-element.28.refs_1_, bf16[48,256,256]{2,1,0:T(8,128)(2,1)S(1)} %get-tuple-element.27.refs_2_.refs_1_, bf16[2,512,256]{2,1,0:T(8,128)(2,1)S(1)} %get-tuple-element.36.refs_3_), custom_call_target="tpu_custom_call" | custom-call | flops 1 | bytes 1 | tf_op jit(solution)/shard_map/own_targets/pallas_call | solution.py:243
  31.5 2.8 %collective-permute-done.4.refs_5_.refs_7_ = bf16[2,512,256]{2,1,0:T(8,128)(2,1)S(1)} collective-permute-done((bf16[2,512,256]{2,1,0:T(8,128)(2,1)S(1)}, bf16[2,512,256]{2,1,0:T(8,128)(2,1)S(1)}, u32[]{:S(2)}, u32[]{:S(2)}) %collective-permute-start.4) | collective-permute-done | bytes 524320 | tf_op jit(solution)/shard_map/ppermute | solution.py:253
  34.3 2.4 %last_rims.1 = (bf16[2,384,256]{2,1,0:T(8,128)(2,1)S(1)}, bf16[2,384,256]{2,1,0:T(8,128)(2,1)S(1)}, bf16[2,256,256]{2,1,0:T(8,128)(2,1)S(1)}, f32[2,512,256]{2,1...) custom-call(s32[9,49]{1,0:T(8,128)S(1)} %get-tuple-element.26.refs_0, ...), custom_call_target="tpu_custom_call", output_to_operand_aliasing={{3}: (2, {}), {4}: (3, {})} | custom-call | flops 1 | bytes 1 | tf_op jit(solution)/shard_map/last_rims/pallas_call | solution.py:243
  36.7 3.9 %collective-permute-start.5 = (bf16[2,512,256]{2,1,0:T(8,128)(2,1)S(1)}, bf16[2,512,256]{2,1,0:T(8,128)(2,1)S(1)}, u32[]{:S(2)}, u32[]{:S(2)}) collective-permute-start(bf16[2,512,256]{2,1,0:T(8,128)(2,1)S(1)} %get-tuple-element.39.refs_8_), channel_id=1, source_target_pairs={{1,2},{3,4},{5,6},{7,8},{9,10},{11,12},{13,14},{2,1},{4,3},{6,5},{... | collective-permute-start | bytes 1572872 | tf_op jit(solution)/shard_map/ppermute | solution.py:253
  40.7 0.5 collective-permute-start.7
  41.2 0.1 collective-permute-start.8
  41.3 2.8 %halo_sources.1.refs_0_ = f32[4,1024,256]{2,1,0:T(8,128)S(1)} custom-call(s32[9,49]{1,0:T(8,128)S(1)} %get-tuple-element.26.refs_0_, bf16[48,256,256]{2,1,0:T(8,128)(2,1)S(1)} %get-tuple-element.27.refs_2_.refs_1_, f32[4,1024,256]{2,1,0:T(8,128)S(1)} %own_targets.1.refs_6_.refs_2_, ...), custom_call_target="tpu_custom_call", output_to_operand_aliasing={{}: (2, {})} | custom-call | flops 1 | bytes 1 | tf_op jit(solution)/shard_map/halo_sources/pallas_call | solution.py:243
  44.1 1.5 %collective-permute-done.9.refs_1_ = bf16[2,512,256]{2,1,0:T(8,128)(2,1)S(1)} collective-permute-done((bf16[2,512,256]{2,1,0:T(8,128)(2,1)S(1)}, bf16[2,512,256]{2,1,0:T(8,128)(2,1)S(1)}, u32[]{:S(2)}, u32[]{:S(2)}) %collective-permute-start.9) | collective-permute-done | bytes 524320 | tf_op jit(solution)/shard_map/ppermute | solution.py:253
  45.6 1.0 %residual_near.2.refs_4_ = f32[4,1024,256]{2,1,0:T(8,128)} custom-call(f32[4,1024,256]{2,1,0:T(8,128)S(1)} %halo_sources.1.refs_0_, bf16[2,512,256]{2,1,0:T(8,128)(2,1)S(1)} %collective-permute-done.9.refs_1_), custom_call_target="tpu_custom_call" | custom-call | flops 1 | bytes 1 | tf_op jit(solution)/shard_map/residual_near/pallas_call | solution.py:243
  46.6 1.4 %residual_far.1.refs_2_ = f32[4,1024,256]{2,1,0:T(8,128)} custom-call(f32[4,1024,256]{2,1,0:T(8,128)S(1)} %halo_sources.1.refs_0_, bf16[2,384,256]{2,1,0:T(8,128)(2,1)S(1)} %collective-permute-done.6.refs_1_, bf16[2,384,256]{2,1,0:T(8,128)(2,1)S(1)} %collective-permute-done.7.refs_2_, ...), custom_call_target="tpu_custom_call", output_to_operand_aliasing={{}: (4, {})} | custom-call | flops 1 | bytes 1 | tf_op jit(solution)/shard_map/residual_far/pallas_call | solution.py:243
  48.1 3.1 %collective-permute-done.5.refs_1_ = bf16[2,512,256]{2,1,0:T(8,128)(2,1)S(1)} collective-permute-done((bf16[2,512,256]{2,1,0:T(8,128)(2,1)S(1)}, bf16[2,512,256]{2,1,0:T(8,128)(2,1)S(1)}, u32[]{:S(2)}, u32[]{:S(2)}) %collective-permute-start.5) | collective-permute-done | bytes 524320 | tf_op jit(solution)/shard_map/ppermute | solution.py:253
  51.2 1.0 %residual_near.3 = f32[4,1024,256]{2,1,0:T(8,128)} custom-call(f32[4,1024,256]{2,1,0:T(8,128)S(1)} %halo_sources.1.refs_0_, bf16[2,512,256]{2,1,0:T(8,128)(2,1)S(1)} %collective-permute-done.5.refs_1_, f32[4,1024,256]{2,1,0:T(8,128)} %residual_far.1.refs_2_), custom_call_target="tpu_custom_call", output_to_operand_aliasing={{}: (2, {})} | custom-call | flops 1 | bytes 1 | tf_op jit(solution)/shard_map/residual_near/pallas_call | solution.py:243
  (9 shorter events, 0.2 us)
Async XLA Ops:
  1.2 21.9 %collective-permute-start.3 = (bf16[2,512,256]{2,1,0:T(8,128)(2,1)S(1)}, bf16[2,512,256]{2,1,0:T(8,128)(2,1)S(1)}, u32[]{:S(2)}, u32[]{:S(2)}) collective-permute-start(bf16[2,512,256]{2,1,0:T(8,128)(2,1)S(1)} %get-tuple-element.24.refs_3_), channel_id=1, source_target_pairs={{1,2},{3,4},{5,6},{7,8},{9,10},{11,12},{13,14},{2,1},{4,3},{6,5},{... | collective-permute-start | bytes 1572872 | tf_op jit(solution)/shard_map/ppermute | solution.py:253
  5.7 28.6 %collective-permute-start.4 = (bf16[2,512,256]{2,1,0:T(8,128)(2,1)S(1)}, bf16[2,512,256]{2,1,0:T(8,128)(2,1)S(1)}, u32[]{:S(2)}, u32[]{:S(2)}) collective-permute-start(bf16[2,512,256]{2,1,0:T(8,128)(2,1)S(1)} %get-tuple-element.25.refs_4_), channel_id=1, source_target_pairs={{1,2},{3,4},{5,6},{7,8},{9,10},{11,12},{13,14},{2,1},{4,3},{6,5},{... | collective-permute-start | bytes 1572872 | tf_op jit(solution)/shard_map/ppermute | solution.py:253
  7.7 0.7 %copy-start = (s32[48,2]{0,1:T(2,128)S(1)}, s32[48,2]{0,1:T(2,128)}, u32[]{:S(2)}) copy-start(s32[48,2]{0,1:T(2,128)} %param.5) | copy-start | bytes 1156
  13.3 5.2 %collective-permute-start = (bf16[2,384,256]{2,1,0:T(8,128)(2,1)S(1)}, bf16[2,384,256]{2,1,0:T(8,128)(2,1)S(1)}, u32[]{:S(2)}, u32[]{:S(2)}) collective-permute-start(bf16[2,384,256]{2,1,0:T(8,128)(2,1)S(1)} %get-tuple-element.29.refs_3_), channel_id=1, source_target_pairs={{0,1},{1,0},{2,3},{3,2},{4,5},{5,4},{6,7},{7,6},{8,9},{9,8},{10,11... | collective-permute-start | bytes 1179656 | tf_op jit(solution)/shard_map/ppermute | solution.py:256
  13.4 5.1 %collective-permute-start.1 = (bf16[2,384,256]{2,1,0:T(8,128)(2,1)S(1)}, bf16[2,384,256]{2,1,0:T(8,128)(2,1)S(1)}, u32[]{:S(2)}, u32[]{:S(2)}) collective-permute-start(bf16[2,384,256]{2,1,0:T(8,128)(2,1)S(1)} %get-tuple-element.30.refs_4_), channel_id=1, source_target_pairs={{0,1},{1,0},{2,3},{3,2},{4,5},{5,4},{6,7},{7,6},{8,9},{9,8},{10,11... | collective-permute-start | bytes 1179656 | tf_op jit(solution)/shard_map/ppermute | solution.py:256
  13.9 4.6 %collective-permute-start.2 = (bf16[2,256,256]{2,1,0:T(8,128)(2,1)S(1)}, bf16[2,256,256]{2,1,0:T(8,128)(2,1)S(1)}, u32[]{:S(2)}, u32[]{:S(2)}) collective-permute-start(bf16[2,256,256]{2,1,0:T(8,128)(2,1)S(1)} %get-tuple-element.31.refs_5_), channel_id=1, source_target_pairs={{0,1},{1,0},{2,3},{3,2},{4,5},{5,4},{6,7},{7,6},{8,9},{9,8},{10,11... | collective-permute-start | bytes 786440 | tf_op jit(solution)/shard_map/ppermute | solution.py:256
  24.4 21.2 %collective-permute-start.9 = (bf16[2,512,256]{2,1,0:T(8,128)(2,1)S(1)}, bf16[2,512,256]{2,1,0:T(8,128)(2,1)S(1)}, u32[]{:S(2)}, u32[]{:S(2)}) collective-permute-start(bf16[2,512,256]{2,1,0:T(8,128)(2,1)S(1)} %get-tuple-element.36.refs_3_), channel_id=1, source_target_pairs={{1,2},{3,4},{5,6},{7,8},{9,10},{11,12},{13,14},{2,1},{4,3},{6,5},{... | collective-permute-start | bytes 1572872 | tf_op jit(solution)/shard_map/ppermute | solution.py:253
  36.7 14.5 %collective-permute-start.5 = (bf16[2,512,256]{2,1,0:T(8,128)(2,1)S(1)}, bf16[2,512,256]{2,1,0:T(8,128)(2,1)S(1)}, u32[]{:S(2)}, u32[]{:S(2)}) collective-permute-start(bf16[2,512,256]{2,1,0:T(8,128)(2,1)S(1)} %get-tuple-element.39.refs_8_), channel_id=1, source_target_pairs={{1,2},{3,4},{5,6},{7,8},{9,10},{11,12},{13,14},{2,1},{4,3},{6,5},{... | collective-permute-start | bytes 1572872 | tf_op jit(solution)/shard_map/ppermute | solution.py:253
  40.6 6.0 %collective-permute-start.6 = (bf16[2,384,256]{2,1,0:T(8,128)(2,1)S(1)}, bf16[2,384,256]{2,1,0:T(8,128)(2,1)S(1)}, u32[]{:S(2)}, u32[]{:S(2)}) collective-permute-start(bf16[2,384,256]{2,1,0:T(8,128)(2,1)S(1)} %get-tuple-element.40), channel_id=1, source_target_pairs={{0,1},{1,0},{2,3},{3,2},{4,5},{5,4},{6,7},{7,6},{8,9},{9,8},{10,11... | collective-permute-start | bytes 1179656 | tf_op jit(solution)/shard_map/ppermute | solution.py:256
  40.7 5.9 %collective-permute-start.7 = (bf16[2,384,256]{2,1,0:T(8,128)(2,1)S(1)}, bf16[2,384,256]{2,1,0:T(8,128)(2,1)S(1)}, u32[]{:S(2)}, u32[]{:S(2)}) collective-permute-start(bf16[2,384,256]{2,1,0:T(8,128)(2,1)S(1)} %get-tuple-element.41), channel_id=1, source_target_pairs={{0,1},{1,0},{2,3},{3,2},{4,5},{5,4},{6,7},{7,6},{8,9},{9,8},{10,11... | collective-permute-start | bytes 1179656 | tf_op jit(solution)/shard_map/ppermute | solution.py:256
  41.2 5.4 %collective-permute-start.8 = (bf16[2,256,256]{2,1,0:T(8,128)(2,1)S(1)}, bf16[2,256,256]{2,1,0:T(8,128)(2,1)S(1)}, u32[]{:S(2)}, u32[]{:S(2)}) collective-permute-start(bf16[2,256,256]{2,1,0:T(8,128)(2,1)S(1)} %get-tuple-element.42), channel_id=1, source_target_pairs={{0,1},{1,0},{2,3},{3,2},{4,5},{5,4},{6,7},{7,6},{8,9},{9,8},{10,11... | collective-permute-start | bytes 786440 | tf_op jit(solution)/shard_map/ppermute | solution.py:256

commit v4 on v3

--- a/solution.py
+++ b/solution.py
@@ -14,6 +14,7 @@
 
 OWN, CHIP, CROSS = 0, 1, 2
 LISTS = 9
+GROUPS = 3
 
 
 def row_chunks(rows, split):
@@ -43,17 +44,17 @@
     return pltpu.with_memory_space_constraint(x, pltpu.HBM)
 
 
-def accumulate(plan, which, integrals, segments):
-    count = plan[which, plan.shape[1] - 1]
+def accumulate(plan, which, integrals, segments, begin=0, end=None):
+    end = plan[which, plan.shape[1] - 1] if end is None else end
 
     def some(first, width):
         entries = [plan[which, first + u] for u in range(width)]
-        for source, begin, sums, offset, size in segments:
+        for source, low, sums, offset, size in segments:
             for r in range(0, size, 256):
                 block = min(256, size - r)
                 products = [
                     jnp.dot(
-                        source[(entry >> 4) & 15, pl.ds(begin + r, block)],
+                        source[(entry >> 4) & 15, pl.ds(low + r, block)],
                         integrals[entry >> 8],
                         preferred_element_type=jnp.float32,
                     )
@@ -63,16 +64,16 @@
                     sums[entry & 15, pl.ds(offset + r, block)] += product
 
     def pair(i, carry):
-        some(2 * i, 2)
+        some(begin + 2 * i, 2)
         return carry
 
     def single(i, carry):
         some(i, 1)
         return carry
 
-    pairs = count // 2
+    pairs = (end - begin) // 2
     lax.fori_loop(0, pairs, pair, 0)
-    lax.fori_loop(2 * pairs, count, single, 0)
+    lax.fori_loop(begin + 2 * pairs, end, single, 0)
 
 
 def overlaps(sources, totals):
@@ -117,7 +118,12 @@
         plan[which, last] = count + 1
         return carry
 
-    lax.fori_loop(0, tasks.shape[1], one, 0)
+    ends = []
+    size = tasks.shape[1] // GROUPS
+    for group in range(GROUPS):
+        lax.fori_loop(group * size, (group + 1) * size, one, 0)
+        ends.append([plan[3 * OWN + kind, last] for kind in (OWN, CHIP, CROSS)])
+    return ends
 
 
 def edges(axis, tile_count):
@@ -126,43 +132,44 @@
     return odd * edge, (1 - odd) * edge
 
 
-def pick_kernel(axis, chunks, amplitudes, *refs):
+def pick_kernel(axis, near_rows, far_rows, amplitudes, *refs):
     *picked, sems = refs
-    near, _ = edges(axis, amplitudes.shape[0])
-    copies = [
-        pltpu.make_async_copy(
-            amplitudes.at[pl.ds(near, HALO), pl.ds(start, size)], picked[i], sems.at[i]
+    near, far = edges(axis, amplitudes.shape[0])
+    copies = []
+    for first, some in ((near, near_rows), (far, far_rows)):
+        for rows in some:
+            i = len(copies)
+            block = amplitudes.at[pl.ds(first, HALO), pl.ds(*rows)]
+            copies.append(pltpu.make_async_copy(block, picked[i], sems.at[i]))
+            copies[-1].start()
+    for copy in copies:
+        copy.wait()
+
+
+def first_kernel(axis, tasks, amplitudes, integrals, plan, own, held, chip_sums, *refs):
+    *sums, sems = refs
+    size = integrals.shape[0] // GROUPS
+    copies = [pltpu.make_async_copy(amplitudes, own, sems.at[GROUPS])]
+    for group in range(GROUPS):
+        tasks_in_it = pl.ds(group * size, size)
+        copies.append(
+            pltpu.make_async_copy(
+                integrals.at[tasks_in_it], held.at[tasks_in_it], sems.at[group]
+            )
         )
-        for i, (start, size) in enumerate(chunks)
-    ]
     for copy in copies:
         copy.start()
-    for copy in copies:
-        copy.wait()
-
-
-def load_kernel(axis, chip_chunks, tasks, amplitudes, integrals, plan, own, held, *refs):
-    *picked, sems = refs
-    _, far = edges(axis, amplitudes.shape[0])
-    copies = [
-        pltpu.make_async_copy(amplitudes, own, sems.at[0]),
-        pltpu.make_async_copy(integrals, held, sems.at[1]),
-    ]
-    for i, (start, size) in enumerate(chip_chunks):
-        block = amplitudes.at[pl.ds(far, HALO), pl.ds(start, size)]
-        copies.append(pltpu.make_async_copy(block, picked[i], sems.at[2 + i]))
-    for copy in copies:
-        copy.start()
-    make_plan(axis, amplitudes.shape[0], tasks, plan)
-    for copy in copies:
-        copy.wait()
-
-
-def own_rims_kernel(plan, own, integrals, chip_sums, *sums):
+    ends = make_plan(axis, amplitudes.shape[0], tasks, plan)
     for ref in [chip_sums, *sums]:
         ref[...] = jnp.zeros_like(ref)
-    accumulate(plan, 3 * OWN + CROSS, integrals, overlaps([own], sums))
-    accumulate(plan, 3 * OWN + CHIP, integrals, overlaps([own], [chip_sums]))
+    copies[0].wait()
+    begins = [0] * 3
+    for copy, now in zip(copies[1:], ends):
+        copy.wait()
+        for kind, totals in ((CROSS, sums), (CHIP, [chip_sums])):
+            segments = overlaps([own], totals)
+            accumulate(plan, 3 * OWN + kind, held, segments, begins[kind], now[kind])
+        begins = now
 
 
 def chip_rims_kernel(parts, plan, integrals, *refs):
@@ -186,39 +193,52 @@
         chip_rim[...] = chip_total[:, pl.ds(start, size)].astype(chip_rim.dtype)
 
 
-def own_kernel(plan, own, integrals, total):
+def own_kernel(plan, own, integrals, *refs):
+    *chip, total = refs
     total[...] = jnp.zeros_like(total)
     accumulate(plan, 3 * OWN + OWN, integrals, overlaps([own], [total]))
-
-
-def resident_kernel(parts, plan, integrals, sums, *refs):
+    accumulate(plan, 3 * CHIP + OWN, integrals, overlaps(chip, [total]))
+
+
+def resident_kernel(plan, integrals, sums, *refs):
     *halos, total = refs
-    accumulate(plan, 3 * CHIP + OWN, integrals, overlaps(halos[:parts], [total]))
-    accumulate(plan, 3 * CROSS + OWN, integrals, overlaps(halos[parts:], [total]))
-
-
-def add_rim(first, chunks, sums, rims, out, part, sems):
-    begin, end = chunks[0][0], sum(chunks[-1])
+    accumulate(plan, 3 * CROSS + OWN, integrals, overlaps(halos, [total]))
+
+
+def add_rim(places, sums, out, sems):
     copies = []
-    for j in range(HALO):
-        for (start, size), rim in zip(chunks, rims):
-            rows = pl.ds(start - begin, size)
-            part[j, rows] = sums[first + j, pl.ds(start, size)] + rim[j].astype(jnp.float32)
-        target = out.at[first + j, pl.ds(begin, end - begin)]
-        copies.append(pltpu.make_async_copy(part.at[j], target, sems.at[j]))
-        copies[-1].start()
+    for first, rims, begin, part, sem in places:
+        row = 0
+        for rim in rims:
+            size = rim.shape[1]
+            here, there = pl.ds(row, size), pl.ds(begin + row, size)
+            for j in range(HALO):
+                part[j, here] = sums[first + j, there] + rim[j].astype(jnp.float32)
+            copies.append(
+                pltpu.make_async_copy(
+                    part.at[:, here], out.at[pl.ds(first, HALO), there], sems.at[sem]
+                )
+            )
+            copies[-1].start()
+            sem += 1
+            row += size
     for copy in copies:
         copy.wait()
 
 
-def far_kernel(axis, chip_chunks, sums, *refs):
-    rims, (*_, out, part, sems) = refs[: len(chip_chunks)], refs[len(chip_chunks) :]
-    add_rim(edges(axis, out.shape[0])[1], chip_chunks, sums, rims, out, part, sems)
-
-
-def near_kernel(axis, chunk, sums, rim, *refs):
-    *_, out, part, sems = refs
-    add_rim(edges(axis, out.shape[0])[0], [chunk], sums, [rim], out, part, sems)
+def rest_kernel(axis, parts, sums, *refs):
+    rims, (out, part, sems) = refs[:-3], refs[-3:]
+    near, far = edges(axis, out.shape[0])
+    places = [
+        (far, rims[:parts], 0, part.at[pl.ds(0, HALO)], 0),
+        (near, rims[parts:], 0, part.at[pl.ds(HALO, HALO)], parts),
+    ]
+    add_rim(places, sums, out, sems)
+
+
+def last_kernel(axis, begin, sums, rim, before, out, part, sems):
+    near, _ = edges(axis, out.shape[0])
+    add_rim([(near, [rim], begin, part, 0)], sums, out, sems)
 
 
 def on_device(amplitudes, integrals, tasks):
@@ -256,47 +276,43 @@
         return in_vmem(lax.ppermute(x, axis, chip_pairs))
 
     amplitudes, integrals = in_hbm(amplitudes), in_hbm(integrals)
-    picked = call(
-        functools.partial(pick_kernel, axis, chunks),
-        "pick",
-        [amplitudes],
-        [hbm()],
-        out_shape=[jax.ShapeDtypeStruct((HALO, size, width), bf16) for _, size in chunks],
-        out_specs=[hbm()] * count,
-        scratch_shapes=[pltpu.SemaphoreType.DMA((count,))],
-    )
-    halos = [swap_cross(x) for x in picked]
+    def pick(near_rows, far_rows, after=()):
+        sizes = [size for _, size in near_rows + far_rows]
+        return call(
+            functools.partial(pick_kernel, axis, near_rows, far_rows),
+            "pick",
+            [amplitudes],
+            [hbm()],
+            after=after,
+            out_shape=[jax.ShapeDtypeStruct((HALO, size, width), bf16) for size in sizes],
+            out_specs=[hbm()] * len(sizes),
+            scratch_shapes=[pltpu.SemaphoreType.DMA((len(sizes),))],
+        )
 
     parts = len(chip_chunks)
-    plan, own, held, *chip_picked = call(
-        functools.partial(load_kernel, axis, chip_chunks),
-        "load",
+    head = pick(chunks[:1], [])
+    rest = pick(chunks[1:], chip_chunks, after=head)
+    halos = [swap_cross(x) for x in head + rest[: count - 1]]
+    chip_halos = [swap_chip(x) for x in rest[count - 1 :]]
+
+    edge_shape = pltpu.VMEM((HALO, rows, width), f32)
+    sums_shapes = [edge_shape] + [pltpu.VMEM((HALO, size, width), f32) for _, size in chunks]
+    plan, own, held, *sums = call(
+        functools.partial(first_kernel, axis),
+        "own_rims",
         [tasks.T, amplitudes, integrals],
         [smem(), hbm(), hbm()],
-        after=picked,
+        after=rest,
         out_shape=[
             jax.ShapeDtypeStruct((LISTS, task_count + 1), i32),
             pltpu.VMEM(amplitudes.shape, bf16),
             pltpu.VMEM(integrals.shape, bf16),
         ]
-        + [pltpu.VMEM((HALO, size, width), bf16) for _, size in chip_chunks],
-        out_specs=[smem()] + [vmem()] * (2 + parts),
-        scratch_shapes=[pltpu.SemaphoreType.DMA((2 + parts,))],
+        + sums_shapes,
+        out_specs=[smem()] + [vmem()] * (3 + count),
+        scratch_shapes=[pltpu.SemaphoreType.DMA((1 + GROUPS,))],
     )
     own, held = in_vmem(own), in_vmem(held)
-    chip_halos = [swap_chip(x) for x in chip_picked]
-
-    edge_shape = pltpu.VMEM((HALO, rows, width), f32)
-    sums_shapes = [edge_shape] + [pltpu.VMEM((HALO, size, width), f32) for _, size in chunks]
-    sums = call(
-        own_rims_kernel,
-        "own_rims",
-        [plan, own, held],
-        [smem()] + [vmem()] * 2,
-        after=[in_vmem(x) for x in chip_picked],
-        out_shape=sums_shapes,
-        out_specs=[vmem()] * (count + 1),
-    )
     chip_sums, *cross_sums = call(
         functools.partial(chip_rims_kernel, parts),
         "chip_rims",
@@ -331,8 +347,8 @@
     resident = call(
         own_kernel,
         "own_targets",
-        [plan, own, held],
-        [smem()] + [vmem()] * 2,
+        [plan, own, held, *chip_halos],
+        [smem()] + [vmem()] * (2 + parts),
         after=after,
         out_shape=resident_shape,
         out_specs=vmem(),
@@ -358,10 +374,10 @@
     from_chip = [swap_chip(x) for x in chip_rims]
     from_cross = [swap_cross(x) for x in rims]
     resident = call(
-        functools.partial(resident_kernel, parts),
-        "halo_sources",
-        [plan, held, resident, *chip_halos, *halos],
-        [smem()] + [vmem()] * (2 + parts + count),
+        resident_kernel,
+        "cross_sources",
+        [plan, held, resident, *halos],
+        [smem()] + [vmem()] * (2 + count),
         after=[in_vmem(rim)],
         out_shape=resident_shape,
         out_specs=vmem(),
@@ -369,31 +385,34 @@
     )
     resident = in_vmem(resident)
 
-    def write(kernel, name, blocks, length, out=None):
-        before = [] if out is None else [out]
-        return call(
-            kernel,
-            name,
-            [resident, *blocks, *before],
-            [vmem()] * (1 + len(blocks)) + [hbm()] * len(before),
-            out_shape=jax.ShapeDtypeStruct((tile_count, rows, width), f32),
-            out_specs=hbm(),
-            scratch_shapes=[
-                pltpu.VMEM((HALO, length, width), f32),
-                pltpu.SemaphoreType.DMA((HALO,)),
-            ],
-            input_output_aliases={1 + len(blocks): 0} if before else {},
-        )
-
-    def near(i, out=None):
-        kernel = functools.partial(near_kernel, axis, chunks[i])
-        return write(kernel, "residual_near", [from_cross[i]], chunks[i][1], out)
-
-    out = near(0)
-    out = write(functools.partial(far_kernel, axis, chip_chunks), "residual_far", from_chip, rows, out)
-    for i in range(1, count):
-        out = near(i, out)
-    return out
+    shape = jax.ShapeDtypeStruct((tile_count, rows, width), f32)
+    blocks = from_chip + from_cross[:-1]
+    out = call(
+        functools.partial(rest_kernel, axis, parts),
+        "residual",
+        [resident, *blocks],
+        [vmem()] * (1 + len(blocks)),
+        out_shape=shape,
+        out_specs=hbm(),
+        scratch_shapes=[
+            pltpu.VMEM((2 * HALO, rows, width), f32),
+            pltpu.SemaphoreType.DMA((len(blocks),)),
+        ],
+    )
+    begin, size = chunks[-1]
+    return call(
+        functools.partial(last_kernel, axis, begin),
+        "residual_last",
+        [resident, from_cross[-1], out],
+        [vmem()] * 2 + [hbm()],
+        out_shape=shape,
+        out_specs=hbm(),
+        scratch_shapes=[
+            pltpu.VMEM((HALO, size, width), f32),
+            pltpu.SemaphoreType.DMA((1,)),
+        ],
+        input_output_aliases={2: 0},
+    )
 
 
 def solution(mesh):

time: 52.7 us -> 52.5 us (level)
  waiting for transfers between devices: 8.38 us -> 9.96 us
  Pallas kernels: 27 us -> 25.5 us
  local copies, waits for them, and re-layouts: 0.67 us -> 0.01 us
    ppermute x4, waiting for transfers between devices: 8.36 us -> 9.94 us  [swap_cross(): return in_vmem(lax.ppermute(x, axis, cross_pairs))]
    pallas_call x11 -> x10, Pallas kernels: 27 us -> 25.5 us  [call(): pl.pallas_call(body, in_specs=in_specs + [pl.BlockSpec(memory_space=pl.AN...]
    unnamed x2, local copies, waits for them, and re-layouts: 0.67 us -> 0.01 us
  transfers between devices with their start and end apart: 10 -> 10, of which waited for: 4 -> 3; matrix products, arithmetic and copies ran while one was open for 0% -> 0% of each run, Pallas kernels for 47% -> 45%
where the time goes in v4:
time: 52.5 us; the launch traced here: 52.1 us
  Pallas kernels  25.5 us (49%)
  starting transfers between devices  16.5 us (31%)
  waiting for transfers between devices  9.96 us (19%)
    pallas_call x10, Pallas kernels, call(): pl.pallas_call(body, in_specs=in_specs + [pl.BlockSpec(memory_space=pl.AN...  25.5 us
    ppermute x4, starting transfers between devices, swap_cross(): return in_vmem(lax.ppermute(x, axis, cross_pairs))  15.2 us
    ppermute x4, waiting for transfers between devices, swap_cross(): return in_vmem(lax.ppermute(x, axis, cross_pairs))  9.94 us
    ppermute x6, starting transfers between devices, swap_chip(): return in_vmem(lax.ppermute(x, axis, chip_pairs))  1.29 us
  transfers between devices with their start and end apart: 10, of which 3 were waited for; matrix products, arithmetic and copies ran while one was open for 0% of the time, Pallas kernels for 45%

profile of v4, /device:TPU:1, one launch (start us, length us, event | category | flops | bytes accessed | tf_op | source)
XLA Modules:
  0.0 52.1 jit_solution(10971340721252702762)
XLA Ops:
  0.0 1.1 %pick.2.refs_1_ = bf16[2,512,256]{2,1,0:T(8,128)(2,1)S(1)} custom-call(bf16[4,1024,256]{2,1,0:T(8,128)(2,1)} %refs_1_.1), custom_call_target="tpu_custom_call" | custom-call | flops 1 | bytes 1 | tf_op jit(solution)/shard_map/pick/pallas_call | solution.py:263
  1.1 4.5 %collective-permute-start.3 = (bf16[2,512,256]{2,1,0:T(8,128)(2,1)S(1)}, bf16[2,512,256]{2,1,0:T(8,128)(2,1)S(1)}, u32[]{:S(2)}, u32[]{:S(2)}) collective-permute-start(bf16[2,512,256]{2,1,0:T(8,128)(2,1)S(1)} %pick.2.refs_1_), channel_id=1, source_target_pairs={{1,2},{3,4},{5,6},{7,8},{9,10},{11,12},{13,14},{2,1},{4,3},{6,5},{... | collective-permute-start | bytes 1572872 | tf_op jit(solution)/shard_map/ppermute | solution.py:273
  5.6 1.4 %pick.3 = (bf16[2,512,256]{2,1,0:T(8,128)(2,1)S(1)}, bf16[2,384,256]{2,1,0:T(8,128)(2,1)S(1)}, bf16[2,384,256]{2,1,0:T(8,128)(2,1)S(1)}, bf16[2,256,256]{2,1,0:T(8,128)(2,1)S(1)}) custom-call(bf16[4,1024,256]{2,1,0:T(8,128)(2,1)} %refs_1_.1, bf16[2,512,256]{2,1,0:T(8,128)(2,1)S(1)} %pick.2.refs_1_), custom_call_target="tpu_custom_call" | custom-call | flops 1 | bytes 1 | tf_op jit(solution)/shard_map/pick/pallas_call | solution.py:263
  7.0 1.9 %collective-permute-start.4 = (bf16[2,512,256]{2,1,0:T(8,128)(2,1)S(1)}, bf16[2,512,256]{2,1,0:T(8,128)(2,1)S(1)}, u32[]{:S(2)}, u32[]{:S(2)}) collective-permute-start(bf16[2,512,256]{2,1,0:T(8,128)(2,1)S(1)} %get-tuple-element.23.refs_3_), channel_id=1, source_target_pairs={{1,2},{3,4},{5,6},{7,8},{9,10},{11,12},{13,14},{2,1},{4,3},{6,5},{... | collective-permute-start | bytes 1572872 | tf_op jit(solution)/shard_map/ppermute | solution.py:273
  8.9 0.1 collective-permute-start
  9.0 0.5 collective-permute-start.1
  9.5 0.1 collective-permute-start.2
  9.6 6.8 %own_rims.1 = (s32[9,49]{1,0:T(8,128)S(1)}, bf16[4,1024,256]{2,1,0:T(8,128)(2,1)S(1)}, bf16[48,256,256]{2,1,0:T(8,128)(2,1)S(1)}, f32[2,1024,256]{2,1,0:T(8,128)...) custom-call(s32[2,48]{1,0:T(2,128)S(1)} %bitcast.1, bf16[4,1024,256]{2,1,0:T(8,128)(2,1)} %refs_1_.1, ...), custom_call_target="tpu_custom_call" | custom-call | flops 1 | bytes 1 | tf_op jit(solution)/shard_map/own_rims/pallas_call | solution.py:263
  16.4 0.0 collective-permute-done.refs_2_.refs_3_
  16.5 1.3 %chip_rims.1 = (f32[2,1024,256]{2,1,0:T(8,128)S(1)}, f32[2,512,256]{2,1,0:T(8,128)S(1)}, f32[2,512,256]{2,1,0:T(8,128)S(1)}) custom-call(s32[9,49]{1,0:T(8,128)S(1)} %get-tuple-element.27.refs_0_, bf16[48,256,256]{2,1,0:T(8,128)(2,1)S(1)} %get-tuple-element.28.refs_1_.refs_2_, ...), custom_call_target="tpu_custom_call", output_to_operand_aliasing={{0}: (5, {}), {1}: (6, {}), {2}: (7, {})} | custom-call | flops 1 | bytes 1 | tf_op jit(solution)/shard_map/chip_rims/pallas_call | solution.py:263
  17.8 5.1 %collective-permute-done.3.refs_3_.refs_4_ = bf16[2,512,256]{2,1,0:T(8,128)(2,1)S(1)} collective-permute-done((bf16[2,512,256]{2,1,0:T(8,128)(2,1)S(1)}, bf16[2,512,256]{2,1,0:T(8,128)(2,1)S(1)}, u32[]{:S(2)}, u32[]{:S(2)}) %collective-permute-start.3) | collective-permute-done | bytes 524320 | tf_op jit(solution)/shard_map/ppermute | solution.py:273
  22.9 1.1 %cross_rim.1 = (f32[2,512,256]{2,1,0:T(8,128)S(1)}, bf16[2,512,256]{2,1,0:T(8,128)(2,1)S(1)}) custom-call(s32[9,49]{1,0:T(8,128)S(1)} %get-tuple-element.27.refs_0_, bf16[48,256,256]{2,1,0:T(8,128)(2,1)S(1)} %get-tuple-element.28.refs_1_.refs_2_, f32[2,512,256]{2,1,0:T(8,128)S(1)} %get-tuple-element.33.refs_2_, ...), custom_call_target="tpu_custom_call", output_to_operand_aliasing={{0}: (2, {})} | custom-call | flops 1 | bytes 1 | tf_op jit(solution)/shard_map/cross_rim/pallas_call | solution.py:263
  24.0 4.7 %collective-permute-start.9 = (bf16[2,512,256]{2,1,0:T(8,128)(2,1)S(1)}, bf16[2,512,256]{2,1,0:T(8,128)(2,1)S(1)}, u32[]{:S(2)}, u32[]{:S(2)}) collective-permute-start(bf16[2,512,256]{2,1,0:T(8,128)(2,1)S(1)} %get-tuple-element.34.refs_6_), channel_id=1, source_target_pairs={{1,2},{3,4},{5,6},{7,8},{9,10},{11,12},{13,14},{2,1},{4,3},{6,5},{... | collective-permute-start | bytes 1572872 | tf_op jit(solution)/shard_map/ppermute | solution.py:273
  28.7 6.3 %own_targets.1.refs_6_.refs_2_ = f32[4,1024,256]{2,1,0:T(8,128)S(1)} custom-call(s32[9,49]{1,0:T(8,128)S(1)} %get-tuple-element.27.refs_0_, bf16[4,1024,256]{2,1,0:T(8,128)(2,1)S(1)} %get-tuple-element.29.refs_1_, bf16[48,256,256]{2,1,0:T(8,128)(2,1)S(1)} %get-tuple-element.28.refs_1_.refs_2_, bf16[2,384,256]{2,1,0:T(8,128)(2,1)S(1)} %collective-permute-done.refs_2_.refs_3_, ...), custom_call_target="tpu_custom_call" | custom-call | flops 1 | bytes 1 | tf_op jit(solution)/shard_map/own_targets/pallas_call | solution.py:263
  35.0 2.5 %last_rims.1 = (bf16[2,384,256]{2,1,0:T(8,128)(2,1)S(1)}, bf16[2,384,256]{2,1,0:T(8,128)(2,1)S(1)}, bf16[2,256,256]{2,1,0:T(8,128)(2,1)S(1)}, f32[2,512,256]{2,1...) custom-call(s32[9,49]{1,0:T(8,128)S(1)} %get-tuple-element.27.refs_0, ...), custom_call_target="tpu_custom_call", output_to_operand_aliasing={{3}: (2, {}), {4}: (3, {})} | custom-call | flops 1 | bytes 1 | tf_op jit(solution)/shard_map/last_rims/pallas_call | solution.py:263
  37.5 4.1 %collective-permute-start.5 = (bf16[2,512,256]{2,1,0:T(8,128)(2,1)S(1)}, bf16[2,512,256]{2,1,0:T(8,128)(2,1)S(1)}, u32[]{:S(2)}, u32[]{:S(2)}) collective-permute-start(bf16[2,512,256]{2,1,0:T(8,128)(2,1)S(1)} %get-tuple-element.37.refs_5_), channel_id=1, source_target_pairs={{1,2},{3,4},{5,6},{7,8},{9,10},{11,12},{13,14},{2,1},{4,3},{6,5},{... | collective-permute-start | bytes 1572872 | tf_op jit(solution)/shard_map/ppermute | solution.py:273
  41.6 0.1 collective-permute-start.6
  41.7 0.5 collective-permute-start.7
  42.2 0.1 collective-permute-start.8
  42.2 2.2 %cross_sources.1.refs_0_ = f32[4,1024,256]{2,1,0:T(8,128)S(1)} custom-call(s32[9,49]{1,0:T(8,128)S(1)} %get-tuple-element.27.refs_0_, bf16[48,256,256]{2,1,0:T(8,128)(2,1)S(1)} %get-tuple-element.28.refs_1_.refs_2_, f32[4,1024,256]{2,1,0:T(8,128)S(1)} %own_targets.1.refs_6_.refs_2_, ...), custom_call_target="tpu_custom_call", output_to_operand_aliasing={{}: (2, {})} | custom-call | flops 1 | bytes 1 | tf_op jit(solution)/shard_map/cross_sources/pallas_call | solution.py:263
  44.4 1.0 %collective-permute-done.9.refs_4_ = bf16[2,512,256]{2,1,0:T(8,128)(2,1)S(1)} collective-permute-done((bf16[2,512,256]{2,1,0:T(8,128)(2,1)S(1)}, bf16[2,512,256]{2,1,0:T(8,128)(2,1)S(1)}, u32[]{:S(2)}, u32[]{:S(2)}) %collective-permute-start.9) | collective-permute-done | bytes 524320 | tf_op jit(solution)/shard_map/ppermute | solution.py:273
  45.4 1.8 %residual.1.refs_2_ = f32[4,1024,256]{2,1,0:T(8,128)} custom-call(f32[4,1024,256]{2,1,0:T(8,128)S(1)} %cross_sources.1.refs_0_, bf16[2,384,256]{2,1,0:T(8,128)(2,1)S(1)} %collective-permute-done.6.refs_1_, bf16[2,384,256]{2,1,0:T(8,128)(2,1)S(1)} %collective-permute-done.7.refs_2_, bf16[2,256,256]{2,1,0:T(8,128)(2,1)S(1)} %collective-permute-done.8.refs_3_, ...), custom_call_target="tpu_custom_call" | custom-call | flops 1 | bytes 1 | tf_op jit(solution)/shard_map/residual/pallas_call | solution.py:263
  47.2 3.8 %collective-permute-done.5.refs_1_ = bf16[2,512,256]{2,1,0:T(8,128)(2,1)S(1)} collective-permute-done((bf16[2,512,256]{2,1,0:T(8,128)(2,1)S(1)}, bf16[2,512,256]{2,1,0:T(8,128)(2,1)S(1)}, u32[]{:S(2)}, u32[]{:S(2)}) %collective-permute-start.5) | collective-permute-done | bytes 524320 | tf_op jit(solution)/shard_map/ppermute | solution.py:273
  51.0 1.1 %residual_last.1 = f32[4,1024,256]{2,1,0:T(8,128)} custom-call(f32[4,1024,256]{2,1,0:T(8,128)S(1)} %cross_sources.1.refs_0_, bf16[2,512,256]{2,1,0:T(8,128)(2,1)S(1)} %collective-permute-done.5.refs_1_, f32[4,1024,256]{2,1,0:T(8,128)} %residual.1.refs_2_), custom_call_target="tpu_custom_call", output_to_operand_aliasing={{}: (2, {})} | custom-call | flops 1 | bytes 1 | tf_op jit(solution)/shard_map/residual_last/pallas_call | solution.py:263
  (8 shorter events, 0.0 us)
Async XLA Ops:
  0.0 9.6 %copy-start = (s32[48,2]{0,1:T(2,128)S(1)}, s32[48,2]{0,1:T(2,128)}, u32[]{:S(2)}) copy-start(s32[48,2]{0,1:T(2,128)} %param.5) | copy-start | bytes 1156
  1.1 21.9 %collective-permute-start.3 = (bf16[2,512,256]{2,1,0:T(8,128)(2,1)S(1)}, bf16[2,512,256]{2,1,0:T(8,128)(2,1)S(1)}, u32[]{:S(2)}, u32[]{:S(2)}) collective-permute-start(bf16[2,512,256]{2,1,0:T(8,128)(2,1)S(1)} %pick.2.refs_1_), channel_id=1, source_target_pairs={{1,2},{3,4},{5,6},{7,8},{9,10},{11,12},{13,14},{2,1},{4,3},{6,5},{... | collective-permute-start | bytes 1572872 | tf_op jit(solution)/shard_map/ppermute | solution.py:273
  7.0 28.0 %collective-permute-start.4 = (bf16[2,512,256]{2,1,0:T(8,128)(2,1)S(1)}, bf16[2,512,256]{2,1,0:T(8,128)(2,1)S(1)}, u32[]{:S(2)}, u32[]{:S(2)}) collective-permute-start(bf16[2,512,256]{2,1,0:T(8,128)(2,1)S(1)} %get-tuple-element.23.refs_3_), channel_id=1, source_target_pairs={{1,2},{3,4},{5,6},{7,8},{9,10},{11,12},{13,14},{2,1},{4,3},{6,5},{... | collective-permute-start | bytes 1572872 | tf_op jit(solution)/shard_map/ppermute | solution.py:273
  8.9 7.5 %collective-permute-start = (bf16[2,384,256]{2,1,0:T(8,128)(2,1)S(1)}, bf16[2,384,256]{2,1,0:T(8,128)(2,1)S(1)}, u32[]{:S(2)}, u32[]{:S(2)}) collective-permute-start(bf16[2,384,256]{2,1,0:T(8,128)(2,1)S(1)} %get-tuple-element.24.refs_4_), channel_id=1, source_target_pairs={{0,1},{1,0},{2,3},{3,2},{4,5},{5,4},{6,7},{7,6},{8,9},{9,8},{10,11... | collective-permute-start | bytes 1179656 | tf_op jit(solution)/shard_map/ppermute | solution.py:276
  9.0 7.4 %collective-permute-start.1 = (bf16[2,384,256]{2,1,0:T(8,128)(2,1)S(1)}, bf16[2,384,256]{2,1,0:T(8,128)(2,1)S(1)}, u32[]{:S(2)}, u32[]{:S(2)}) collective-permute-start(bf16[2,384,256]{2,1,0:T(8,128)(2,1)S(1)} %get-tuple-element.25.refs_5_), channel_id=1, source_target_pairs={{0,1},{1,0},{2,3},{3,2},{4,5},{5,4},{6,7},{7,6},{8,9},{9,8},{10,11... | collective-permute-start | bytes 1179656 | tf_op jit(solution)/shard_map/ppermute | solution.py:276
  9.5 6.9 %collective-permute-start.2 = (bf16[2,256,256]{2,1,0:T(8,128)(2,1)S(1)}, bf16[2,256,256]{2,1,0:T(8,128)(2,1)S(1)}, u32[]{:S(2)}, u32[]{:S(2)}) collective-permute-start(bf16[2,256,256]{2,1,0:T(8,128)(2,1)S(1)} %get-tuple-element.26.refs_6_), channel_id=1, source_target_pairs={{0,1},{1,0},{2,3},{3,2},{4,5},{5,4},{6,7},{7,6},{8,9},{9,8},{10,11... | collective-permute-start | bytes 786440 | tf_op jit(solution)/shard_map/ppermute | solution.py:276
  24.0 21.4 %collective-permute-start.9 = (bf16[2,512,256]{2,1,0:T(8,128)(2,1)S(1)}, bf16[2,512,256]{2,1,0:T(8,128)(2,1)S(1)}, u32[]{:S(2)}, u32[]{:S(2)}) collective-permute-start(bf16[2,512,256]{2,1,0:T(8,128)(2,1)S(1)} %get-tuple-element.34.refs_6_), channel_id=1, source_target_pairs={{1,2},{3,4},{5,6},{7,8},{9,10},{11,12},{13,14},{2,1},{4,3},{6,5},{... | collective-permute-start | bytes 1572872 | tf_op jit(solution)/shard_map/ppermute | solution.py:273
  37.5 13.5 %collective-permute-start.5 = (bf16[2,512,256]{2,1,0:T(8,128)(2,1)S(1)}, bf16[2,512,256]{2,1,0:T(8,128)(2,1)S(1)}, u32[]{:S(2)}, u32[]{:S(2)}) collective-permute-start(bf16[2,512,256]{2,1,0:T(8,128)(2,1)S(1)} %get-tuple-element.37.refs_5_), channel_id=1, source_target_pairs={{1,2},{3,4},{5,6},{7,8},{9,10},{11,12},{13,14},{2,1},{4,3},{6,5},{... | collective-permute-start | bytes 1572872 | tf_op jit(solution)/shard_map/ppermute | solution.py:273
  41.6 2.8 %collective-permute-start.6 = (bf16[2,384,256]{2,1,0:T(8,128)(2,1)S(1)}, bf16[2,384,256]{2,1,0:T(8,128)(2,1)S(1)}, u32[]{:S(2)}, u32[]{:S(2)}) collective-permute-start(bf16[2,384,256]{2,1,0:T(8,128)(2,1)S(1)} %get-tuple-element.38), channel_id=1, source_target_pairs={{0,1},{1,0},{2,3},{3,2},{4,5},{5,4},{6,7},{7,6},{8,9},{9,8},{10,11... | collective-permute-start | bytes 1179656 | tf_op jit(solution)/shard_map/ppermute | solution.py:276
  41.7 2.8 %collective-permute-start.7 = (bf16[2,384,256]{2,1,0:T(8,128)(2,1)S(1)}, bf16[2,384,256]{2,1,0:T(8,128)(2,1)S(1)}, u32[]{:S(2)}, u32[]{:S(2)}) collective-permute-start(bf16[2,384,256]{2,1,0:T(8,128)(2,1)S(1)} %get-tuple-element.39), channel_id=1, source_target_pairs={{0,1},{1,0},{2,3},{3,2},{4,5},{5,4},{6,7},{7,6},{8,9},{9,8},{10,11... | collective-permute-start | bytes 1179656 | tf_op jit(solution)/shard_map/ppermute | solution.py:276
  42.2 2.2 %collective-permute-start.8 = (bf16[2,256,256]{2,1,0:T(8,128)(2,1)S(1)}, bf16[2,256,256]{2,1,0:T(8,128)(2,1)S(1)}, u32[]{:S(2)}, u32[]{:S(2)}) collective-permute-start(bf16[2,256,256]{2,1,0:T(8,128)(2,1)S(1)} %get-tuple-element.40), channel_id=1, source_target_pairs={{0,1},{1,0},{2,3},{3,2},{4,5},{5,4},{6,7},{7,6},{8,9},{9,8},{10,11... | collective-permute-start | bytes 786440 | tf_op jit(solution)/shard_map/ppermute | solution.py:276

commit v5 on v4

--- a/solution.py
+++ b/solution.py
@@ -8,7 +8,7 @@
 from jax.sharding import PartitionSpec as P
 
 HALO = 2
-SPLIT = (512, 512)
+SPLIT = (544, 480)
 CHIP_SPLIT = (384, 384, 256)
 VMEM_LIMIT = 24 * 1024 * 1024
 

time: 52.5 us -> 52.3 us (level)
  starting transfers between devices: 16.5 us -> 15.8 us
    ppermute x4, starting transfers between devices: 15.2 us -> 14.5 us  [swap_cross(): return in_vmem(lax.ppermute(x, axis, cross_pairs))]
  transfers between devices with their start and end apart: 10 -> 10, of which waited for: 3 -> 4; matrix products, arithmetic and copies ran while one was open for 0% -> 0% of each run, Pallas kernels for 45% -> 46%
where the time goes in v5:
time: 52.3 us; the launch traced here: 52.1 us
  Pallas kernels  25.9 us (50%)
  starting transfers between devices  15.8 us (30%)
  waiting for transfers between devices  10.2 us (20%)
    pallas_call x10, Pallas kernels, call(): pl.pallas_call(body, in_specs=in_specs + [pl.BlockSpec(memory_space=pl.AN...  25.9 us
    ppermute x4, starting transfers between devices, swap_cross(): return in_vmem(lax.ppermute(x, axis, cross_pairs))  14.5 us
    ppermute x4, waiting for transfers between devices, swap_cross(): return in_vmem(lax.ppermute(x, axis, cross_pairs))  10.1 us
    ppermute x6, starting transfers between devices, swap_chip(): return in_vmem(lax.ppermute(x, axis, chip_pairs))  1.29 us
  transfers between devices with their start and end apart: 10, of which 4 were waited for; matrix products, arithmetic and copies ran while one was open for 0% of the time, Pallas kernels for 46%

profile of v5, /device:TPU:1, one launch (start us, length us, event | category | flops | bytes accessed | tf_op | source)
XLA Modules:
  0.0 52.1 jit_solution(11019705223169841918)
XLA Ops:
  0.0 1.1 %pick.2.refs_1_ = bf16[2,544,256]{2,1,0:T(8,128)(2,1)S(1)} custom-call(bf16[4,1024,256]{2,1,0:T(8,128)(2,1)} %refs_1_.1), custom_call_target="tpu_custom_call" | custom-call | flops 1 | bytes 1 | tf_op jit(solution)/shard_map/pick/pallas_call | solution.py:263
  1.1 4.5 %collective-permute-start.3 = (bf16[2,544,256]{2,1,0:T(8,128)(2,1)S(1)}, bf16[2,544,256]{2,1,0:T(8,128)(2,1)S(1)}, u32[]{:S(2)}, u32[]{:S(2)}) collective-permute-start(bf16[2,544,256]{2,1,0:T(8,128)(2,1)S(1)} %pick.2.refs_1_), channel_id=1, source_target_pairs={{1,2},{3,4},{5,6},{7,8},{9,10},{11,12},{13,14},{2,1},{4,3},{6,5},{... | collective-permute-start | bytes 1671176 | tf_op jit(solution)/shard_map/ppermute | solution.py:273
  5.6 1.4 %pick.3 = (bf16[2,480,256]{2,1,0:T(8,128)(2,1)S(1)}, bf16[2,384,256]{2,1,0:T(8,128)(2,1)S(1)}, bf16[2,384,256]{2,1,0:T(8,128)(2,1)S(1)}, bf16[2,256,256]{2,1,0:T(8,128)(2,1)S(1)}) custom-call(bf16[4,1024,256]{2,1,0:T(8,128)(2,1)} %refs_1_.1, bf16[2,544,256]{2,1,0:T(8,128)(2,1)S(1)} %pick.2.refs_1_), custom_call_target="tpu_custom_call" | custom-call | flops 1 | bytes 1 | tf_op jit(solution)/shard_map/pick/pallas_call | solution.py:263
  7.0 1.9 %collective-permute-start.4 = (bf16[2,480,256]{2,1,0:T(8,128)(2,1)S(1)}, bf16[2,480,256]{2,1,0:T(8,128)(2,1)S(1)}, u32[]{:S(2)}, u32[]{:S(2)}) collective-permute-start(bf16[2,480,256]{2,1,0:T(8,128)(2,1)S(1)} %get-tuple-element.23.refs_3_), channel_id=1, source_target_pairs={{1,2},{3,4},{5,6},{7,8},{9,10},{11,12},{13,14},{2,1},{4,3},{6,5},{... | collective-permute-start | bytes 1474568 | tf_op jit(solution)/shard_map/ppermute | solution.py:273
  8.9 0.1 collective-permute-start
  9.0 0.5 collective-permute-start.1
  9.5 0.1 collective-permute-start.2
  9.6 6.9 %own_rims.1 = (s32[9,49]{1,0:T(8,128)S(1)}, bf16[4,1024,256]{2,1,0:T(8,128)(2,1)S(1)}, bf16[48,256,256]{2,1,0:T(8,128)(2,1)S(1)}, f32[2,1024,256]{2,1,0:T(8,128)...) custom-call(s32[2,48]{1,0:T(2,128)S(1)} %bitcast.1, bf16[4,1024,256]{2,1,0:T(8,128)(2,1)} %refs_1_.1, ...), custom_call_target="tpu_custom_call" | custom-call | flops 1 | bytes 1 | tf_op jit(solution)/shard_map/own_rims/pallas_call | solution.py:263
  16.5 2.2 %chip_rims.1 = (f32[2,1024,256]{2,1,0:T(8,128)S(1)}, f32[2,544,256]{2,1,0:T(8,128)S(1)}, f32[2,480,256]{2,1,0:T(8,128)S(1)}) custom-call(s32[9,49]{1,0:T(8,128)S(1)} %get-tuple-element.27.refs_0_, bf16[48,256,256]{2,1,0:T(8,128)(2,1)S(1)} %get-tuple-element.28.refs_1_.refs_2_, ...), custom_call_target="tpu_custom_call", output_to_operand_aliasing={{0}: (5, {}), {1}: (6, {}), {2}: (7, {})} | custom-call | flops 1 | bytes 1 | tf_op jit(solution)/shard_map/chip_rims/pallas_call | solution.py:263
  18.7 4.6 %collective-permute-done.3.refs_3_.refs_4_ = bf16[2,544,256]{2,1,0:T(8,128)(2,1)S(1)} collective-permute-done((bf16[2,544,256]{2,1,0:T(8,128)(2,1)S(1)}, bf16[2,544,256]{2,1,0:T(8,128)(2,1)S(1)}, u32[]{:S(2)}, u32[]{:S(2)}) %collective-permute-start.3) | collective-permute-done | bytes 557088 | tf_op jit(solution)/shard_map/ppermute | solution.py:273
  23.3 1.7 %cross_rim.1 = (f32[2,544,256]{2,1,0:T(8,128)S(1)}, bf16[2,544,256]{2,1,0:T(8,128)(2,1)S(1)}) custom-call(s32[9,49]{1,0:T(8,128)S(1)} %get-tuple-element.27.refs_0_, bf16[48,256,256]{2,1,0:T(8,128)(2,1)S(1)} %get-tuple-element.28.refs_1_.refs_2_, f32[2,544,256]{2,1,0:T(8,128)S(1)} %get-tuple-element.33.refs_2_, ...), custom_call_target="tpu_custom_call", output_to_operand_aliasing={{0}: (2, {})} | custom-call | flops 1 | bytes 1 | tf_op jit(solution)/shard_map/cross_rim/pallas_call | solution.py:263
  25.0 4.1 %collective-permute-start.9 = (bf16[2,544,256]{2,1,0:T(8,128)(2,1)S(1)}, bf16[2,544,256]{2,1,0:T(8,128)(2,1)S(1)}, u32[]{:S(2)}, u32[]{:S(2)}) collective-permute-start(bf16[2,544,256]{2,1,0:T(8,128)(2,1)S(1)} %get-tuple-element.34.refs_6_), channel_id=1, source_target_pairs={{1,2},{3,4},{5,6},{7,8},{9,10},{11,12},{13,14},{2,1},{4,3},{6,5},{... | collective-permute-start | bytes 1671176 | tf_op jit(solution)/shard_map/ppermute | solution.py:273
  29.1 4.8 %own_targets.1.refs_6_.refs_2_ = f32[4,1024,256]{2,1,0:T(8,128)S(1)} custom-call(s32[9,49]{1,0:T(8,128)S(1)} %get-tuple-element.27.refs_0_, bf16[4,1024,256]{2,1,0:T(8,128)(2,1)S(1)} %get-tuple-element.29.refs_1_, bf16[48,256,256]{2,1,0:T(8,128)(2,1)S(1)} %get-tuple-element.28.refs_1_.refs_2_, bf16[2,384,256]{2,1,0:T(8,128)(2,1)S(1)} %collective-permute-done.refs_2_.refs_3_, ...), custom_call_target="tpu_custom_call" | custom-call | flops 1 | bytes 1 | tf_op jit(solution)/shard_map/own_targets/pallas_call | solution.py:263
  33.9 0.6 %collective-permute-done.4.refs_5_.refs_4_ = bf16[2,480,256]{2,1,0:T(8,128)(2,1)S(1)} collective-permute-done((bf16[2,480,256]{2,1,0:T(8,128)(2,1)S(1)}, bf16[2,480,256]{2,1,0:T(8,128)(2,1)S(1)}, u32[]{:S(2)}, u32[]{:S(2)}) %collective-permute-start.4) | collective-permute-done | bytes 491552 | tf_op jit(solution)/shard_map/ppermute | solution.py:273
  34.5 2.8 %last_rims.1 = (bf16[2,384,256]{2,1,0:T(8,128)(2,1)S(1)}, bf16[2,384,256]{2,1,0:T(8,128)(2,1)S(1)}, bf16[2,256,256]{2,1,0:T(8,128)(2,1)S(1)}, f32[2,480,256]{2,1...) custom-call(s32[9,49]{1,0:T(8,128)S(1)} %get-tuple-element.27.refs_0, ...), custom_call_target="tpu_custom_call", output_to_operand_aliasing={{3}: (2, {}), {4}: (3, {})} | custom-call | flops 1 | bytes 1 | tf_op jit(solution)/shard_map/last_rims/pallas_call | solution.py:263
  37.3 3.9 %collective-permute-start.5 = (bf16[2,480,256]{2,1,0:T(8,128)(2,1)S(1)}, bf16[2,480,256]{2,1,0:T(8,128)(2,1)S(1)}, u32[]{:S(2)}, u32[]{:S(2)}) collective-permute-start(bf16[2,480,256]{2,1,0:T(8,128)(2,1)S(1)} %get-tuple-element.37.refs_5_), channel_id=1, source_target_pairs={{1,2},{3,4},{5,6},{7,8},{9,10},{11,12},{13,14},{2,1},{4,3},{6,5},{... | collective-permute-start | bytes 1474568 | tf_op jit(solution)/shard_map/ppermute | solution.py:273
  41.3 0.1 collective-permute-start.6
  41.4 0.5 collective-permute-start.7
  41.9 0.1 collective-permute-start.8
  41.9 2.3 %cross_sources.1.refs_0_ = f32[4,1024,256]{2,1,0:T(8,128)S(1)} custom-call(s32[9,49]{1,0:T(8,128)S(1)} %get-tuple-element.27.refs_0_, bf16[48,256,256]{2,1,0:T(8,128)(2,1)S(1)} %get-tuple-element.28.refs_1_.refs_2_, f32[4,1024,256]{2,1,0:T(8,128)S(1)} %own_targets.1.refs_6_.refs_2_, ...), custom_call_target="tpu_custom_call", output_to_operand_aliasing={{}: (2, {})} | custom-call | flops 1 | bytes 1 | tf_op jit(solution)/shard_map/cross_sources/pallas_call | solution.py:263
  44.3 1.5 %collective-permute-done.9.refs_4_ = bf16[2,544,256]{2,1,0:T(8,128)(2,1)S(1)} collective-permute-done((bf16[2,544,256]{2,1,0:T(8,128)(2,1)S(1)}, bf16[2,544,256]{2,1,0:T(8,128)(2,1)S(1)}, u32[]{:S(2)}, u32[]{:S(2)}) %collective-permute-start.9) | collective-permute-done | bytes 557088 | tf_op jit(solution)/shard_map/ppermute | solution.py:273
  45.8 1.8 %residual.1.refs_2_ = f32[4,1024,256]{2,1,0:T(8,128)} custom-call(f32[4,1024,256]{2,1,0:T(8,128)S(1)} %cross_sources.1.refs_0_, bf16[2,384,256]{2,1,0:T(8,128)(2,1)S(1)} %collective-permute-done.6.refs_1_, bf16[2,384,256]{2,1,0:T(8,128)(2,1)S(1)} %collective-permute-done.7.refs_2_, bf16[2,256,256]{2,1,0:T(8,128)(2,1)S(1)} %collective-permute-done.8.refs_3_, ...), custom_call_target="tpu_custom_call" | custom-call | flops 1 | bytes 1 | tf_op jit(solution)/shard_map/residual/pallas_call | solution.py:263
  47.6 3.5 %collective-permute-done.5.refs_1_ = bf16[2,480,256]{2,1,0:T(8,128)(2,1)S(1)} collective-permute-done((bf16[2,480,256]{2,1,0:T(8,128)(2,1)S(1)}, bf16[2,480,256]{2,1,0:T(8,128)(2,1)S(1)}, u32[]{:S(2)}, u32[]{:S(2)}) %collective-permute-start.5) | collective-permute-done | bytes 491552 | tf_op jit(solution)/shard_map/ppermute | solution.py:273
  51.0 1.0 %residual_last.1 = f32[4,1024,256]{2,1,0:T(8,128)} custom-call(f32[4,1024,256]{2,1,0:T(8,128)S(1)} %cross_sources.1.refs_0_, bf16[2,480,256]{2,1,0:T(8,128)(2,1)S(1)} %collective-permute-done.5.refs_1_, f32[4,1024,256]{2,1,0:T(8,128)} %residual.1.refs_2_), custom_call_target="tpu_custom_call", output_to_operand_aliasing={{}: (2, {})} | custom-call | flops 1 | bytes 1 | tf_op jit(solution)/shard_map/residual_last/pallas_call | solution.py:263
  (8 shorter events, 0.0 us)
Async XLA Ops:
  0.0 9.6 %copy-start = (s32[48,2]{0,1:T(2,128)S(1)}, s32[48,2]{0,1:T(2,128)}, u32[]{:S(2)}) copy-start(s32[48,2]{0,1:T(2,128)} %param.5) | copy-start | bytes 1156
  1.1 22.2 %collective-permute-start.3 = (bf16[2,544,256]{2,1,0:T(8,128)(2,1)S(1)}, bf16[2,544,256]{2,1,0:T(8,128)(2,1)S(1)}, u32[]{:S(2)}, u32[]{:S(2)}) collective-permute-start(bf16[2,544,256]{2,1,0:T(8,128)(2,1)S(1)} %pick.2.refs_1_), channel_id=1, source_target_pairs={{1,2},{3,4},{5,6},{7,8},{9,10},{11,12},{13,14},{2,1},{4,3},{6,5},{... | collective-permute-start | bytes 1671176 | tf_op jit(solution)/shard_map/ppermute | solution.py:273
  7.0 27.5 %collective-permute-start.4 = (bf16[2,480,256]{2,1,0:T(8,128)(2,1)S(1)}, bf16[2,480,256]{2,1,0:T(8,128)(2,1)S(1)}, u32[]{:S(2)}, u32[]{:S(2)}) collective-permute-start(bf16[2,480,256]{2,1,0:T(8,128)(2,1)S(1)} %get-tuple-element.23.refs_3_), channel_id=1, source_target_pairs={{1,2},{3,4},{5,6},{7,8},{9,10},{11,12},{13,14},{2,1},{4,3},{6,5},{... | collective-permute-start | bytes 1474568 | tf_op jit(solution)/shard_map/ppermute | solution.py:273
  8.9 7.6 %collective-permute-start = (bf16[2,384,256]{2,1,0:T(8,128)(2,1)S(1)}, bf16[2,384,256]{2,1,0:T(8,128)(2,1)S(1)}, u32[]{:S(2)}, u32[]{:S(2)}) collective-permute-start(bf16[2,384,256]{2,1,0:T(8,128)(2,1)S(1)} %get-tuple-element.24.refs_4_), channel_id=1, source_target_pairs={{0,1},{1,0},{2,3},{3,2},{4,5},{5,4},{6,7},{7,6},{8,9},{9,8},{10,11... | collective-permute-start | bytes 1179656 | tf_op jit(solution)/shard_map/ppermute | solution.py:276
  9.0 7.5 %collective-permute-start.1 = (bf16[2,384,256]{2,1,0:T(8,128)(2,1)S(1)}, bf16[2,384,256]{2,1,0:T(8,128)(2,1)S(1)}, u32[]{:S(2)}, u32[]{:S(2)}) collective-permute-start(bf16[2,384,256]{2,1,0:T(8,128)(2,1)S(1)} %get-tuple-element.25.refs_5_), channel_id=1, source_target_pairs={{0,1},{1,0},{2,3},{3,2},{4,5},{5,4},{6,7},{7,6},{8,9},{9,8},{10,11... | collective-permute-start | bytes 1179656 | tf_op jit(solution)/shard_map/ppermute | solution.py:276
  9.5 7.0 %collective-permute-start.2 = (bf16[2,256,256]{2,1,0:T(8,128)(2,1)S(1)}, bf16[2,256,256]{2,1,0:T(8,128)(2,1)S(1)}, u32[]{:S(2)}, u32[]{:S(2)}) collective-permute-start(bf16[2,256,256]{2,1,0:T(8,128)(2,1)S(1)} %get-tuple-element.26.refs_6_), channel_id=1, source_target_pairs={{0,1},{1,0},{2,3},{3,2},{4,5},{5,4},{6,7},{7,6},{8,9},{9,8},{10,11... | collective-permute-start | bytes 786440 | tf_op jit(solution)/shard_map/ppermute | solution.py:276
  25.0 20.8 %collective-permute-start.9 = (bf16[2,544,256]{2,1,0:T(8,128)(2,1)S(1)}, bf16[2,544,256]{2,1,0:T(8,128)(2,1)S(1)}, u32[]{:S(2)}, u32[]{:S(2)}) collective-permute-start(bf16[2,544,256]{2,1,0:T(8,128)(2,1)S(1)} %get-tuple-element.34.refs_6_), channel_id=1, source_target_pairs={{1,2},{3,4},{5,6},{7,8},{9,10},{11,12},{13,14},{2,1},{4,3},{6,5},{... | collective-permute-start | bytes 1671176 | tf_op jit(solution)/shard_map/ppermute | solution.py:273
  37.3 13.7 %collective-permute-start.5 = (bf16[2,480,256]{2,1,0:T(8,128)(2,1)S(1)}, bf16[2,480,256]{2,1,0:T(8,128)(2,1)S(1)}, u32[]{:S(2)}, u32[]{:S(2)}) collective-permute-start(bf16[2,480,256]{2,1,0:T(8,128)(2,1)S(1)} %get-tuple-element.37.refs_5_), channel_id=1, source_target_pairs={{1,2},{3,4},{5,6},{7,8},{9,10},{11,12},{13,14},{2,1},{4,3},{6,5},{... | collective-permute-start | bytes 1474568 | tf_op jit(solution)/shard_map/ppermute | solution.py:273
  41.3 3.0 %collective-permute-start.6 = (bf16[2,384,256]{2,1,0:T(8,128)(2,1)S(1)}, bf16[2,384,256]{2,1,0:T(8,128)(2,1)S(1)}, u32[]{:S(2)}, u32[]{:S(2)}) collective-permute-start(bf16[2,384,256]{2,1,0:T(8,128)(2,1)S(1)} %get-tuple-element.38), channel_id=1, source_target_pairs={{0,1},{1,0},{2,3},{3,2},{4,5},{5,4},{6,7},{7,6},{8,9},{9,8},{10,11... | collective-permute-start | bytes 1179656 | tf_op jit(solution)/shard_map/ppermute | solution.py:276
  41.4 2.9 %collective-permute-start.7 = (bf16[2,384,256]{2,1,0:T(8,128)(2,1)S(1)}, bf16[2,384,256]{2,1,0:T(8,128)(2,1)S(1)}, u32[]{:S(2)}, u32[]{:S(2)}) collective-permute-start(bf16[2,384,256]{2,1,0:T(8,128)(2,1)S(1)} %get-tuple-element.39), channel_id=1, source_target_pairs={{0,1},{1,0},{2,3},{3,2},{4,5},{5,4},{6,7},{7,6},{8,9},{9,8},{10,11... | collective-permute-start | bytes 1179656 | tf_op jit(solution)/shard_map/ppermute | solution.py:276
  41.9 2.4 %collective-permute-start.8 = (bf16[2,256,256]{2,1,0:T(8,128)(2,1)S(1)}, bf16[2,256,256]{2,1,0:T(8,128)(2,1)S(1)}, u32[]{:S(2)}, u32[]{:S(2)}) collective-permute-start(bf16[2,256,256]{2,1,0:T(8,128)(2,1)S(1)} %get-tuple-element.40), channel_id=1, source_target_pairs={{0,1},{1,0},{2,3},{3,2},{4,5},{5,4},{6,7},{7,6},{8,9},{9,8},{10,11... | collective-permute-start | bytes 786440 | tf_op jit(solution)/shard_map/ppermute | solution.py:276

commit v6 on v4

--- a/solution.py
+++ b/solution.py
@@ -9,6 +9,8 @@
 
 HALO = 2
 SPLIT = (512, 512)
+RIM_SPLIT = (512, 432, 80)
+CHIP_RIM_SPLIT = (352, 336, 336)
 CHIP_SPLIT = (384, 384, 256)
 VMEM_LIMIT = 24 * 1024 * 1024
 
@@ -184,10 +186,15 @@
     rim[...] = total[...].astype(rim.dtype)
 
 
-def rims_kernel(count, chip_chunks, plan, integrals, sums, chip_sums, *refs):
-    halos, (*chip_rims, total, chip_total, rim) = refs[:count], refs[count:]
-    accumulate(plan, 3 * CROSS + CROSS, integrals, overlaps([halos[-1]], [total]))
-    rim[...] = total[...].astype(rim.dtype)
+def rims_kernel(count, chip_chunks, plan, integrals, chip_sums, *refs):
+    halos, refs = refs[:count], refs[count:]
+    parts = len(chip_chunks)
+    more = (len(refs) - parts - 1) // 3
+    chip_rims, chip_total = refs[more : more + parts], refs[more + parts]
+    totals, rims = refs[more + parts + 1 : -more], refs[-more:]
+    accumulate(plan, 3 * CROSS + CROSS, integrals, overlaps([halos[-1]], totals))
+    for rim, total in zip(rims, totals):
+        rim[...] = total[...].astype(rim.dtype)
     accumulate(plan, 3 * CROSS + CHIP, integrals, overlaps(halos, [chip_total]))
     for (start, size), chip_rim in zip(chip_chunks, chip_rims):
         chip_rim[...] = chip_total[:, pl.ds(start, size)].astype(chip_rim.dtype)
@@ -245,8 +252,11 @@
     tile_count, rows, width = amplitudes.shape
     task_count = integrals.shape[0]
     chunks = row_chunks(rows, SPLIT)
+    rim_chunks = row_chunks(rows, RIM_SPLIT)
     chip_chunks = row_chunks(rows, CHIP_SPLIT)
+    chip_rim_chunks = row_chunks(rows, CHIP_RIM_SPLIT)
     count = len(chunks)
+    many = len(rim_chunks)
     axis = "own"
     devices = lax.axis_size(axis)
     cross_pairs = [(i, i + 1) for i in range(1, devices - 1, 2)]
@@ -296,7 +306,7 @@
     chip_halos = [swap_chip(x) for x in rest[count - 1 :]]
 
     edge_shape = pltpu.VMEM((HALO, rows, width), f32)
-    sums_shapes = [edge_shape] + [pltpu.VMEM((HALO, size, width), f32) for _, size in chunks]
+    sums_shapes = [edge_shape] + [pltpu.VMEM((HALO, size, width), f32) for _, size in rim_chunks]
     plan, own, held, *sums = call(
         functools.partial(first_kernel, axis),
         "own_rims",
@@ -309,7 +319,7 @@
             pltpu.VMEM(integrals.shape, bf16),
         ]
         + sums_shapes,
-        out_specs=[smem()] + [vmem()] * (3 + count),
+        out_specs=[smem()] + [vmem()] * (3 + many),
         scratch_shapes=[pltpu.SemaphoreType.DMA((1 + GROUPS,))],
     )
     own, held = in_vmem(own), in_vmem(held)
@@ -317,10 +327,10 @@
         functools.partial(chip_rims_kernel, parts),
         "chip_rims",
         [plan, held, *chip_halos, *[in_vmem(x) for x in sums]],
-        [smem()] + [vmem()] * (count + 2 + parts),
+        [smem()] + [vmem()] * (many + 2 + parts),
         out_shape=sums_shapes,
-        out_specs=[vmem()] * (count + 1),
-        input_output_aliases={2 + parts + i: i for i in range(count + 1)},
+        out_specs=[vmem()] * (many + 1),
+        input_output_aliases={2 + parts + i: i for i in range(many + 1)},
     )
     chip_sums = in_vmem(chip_sums)
 
@@ -354,23 +364,25 @@
         out_specs=vmem(),
     )
     resident = in_vmem(resident)
-    size = chunks[-1][1]
-    *chip_rims, _, _, rim = call(
-        functools.partial(rims_kernel, count, chip_chunks),
+    more = many - count + 1
+    chip_parts = len(chip_rim_chunks)
+    last = [pltpu.VMEM((HALO, size, width), bf16) for _, size in rim_chunks[-more:]]
+    got = call(
+        functools.partial(rims_kernel, count, chip_rim_chunks),
         "last_rims",
-        [plan, held, in_vmem(cross_sums[-1]), chip_sums, *halos],
-        [smem()] + [vmem()] * (3 + count),
+        [plan, held, chip_sums, *halos, *[in_vmem(x) for x in cross_sums[-more:]]],
+        [smem()] + [vmem()] * (2 + count + more),
         after=[resident],
-        out_shape=[pltpu.VMEM((HALO, part, width), bf16) for _, part in chip_chunks]
-        + [
-            pltpu.VMEM((HALO, size, width), f32),
-            edge_shape,
-            pltpu.VMEM((HALO, size, width), bf16),
-        ],
-        out_specs=[vmem()] * (3 + len(chip_chunks)),
-        input_output_aliases={2: len(chip_chunks), 3: len(chip_chunks) + 1},
-    )
-    rims.append(rim)
+        out_shape=[pltpu.VMEM((HALO, size, width), bf16) for _, size in chip_rim_chunks]
+        + [edge_shape]
+        + [pltpu.VMEM((HALO, size, width), f32) for _, size in rim_chunks[-more:]]
+        + last,
+        out_specs=[vmem()] * (chip_parts + 1 + 2 * more),
+        input_output_aliases={2: chip_parts}
+        | {3 + count + i: chip_parts + 1 + i for i in range(more)},
+    )
+    chip_rims, rim = got[:chip_parts], got[-1]
+    rims += got[-more:]
     from_chip = [swap_chip(x) for x in chip_rims]
     from_cross = [swap_cross(x) for x in rims]
     resident = call(
@@ -386,9 +398,9 @@
     resident = in_vmem(resident)
 
     shape = jax.ShapeDtypeStruct((tile_count, rows, width), f32)
-    blocks = from_chip + from_cross[:-1]
+    blocks = from_chip + from_cross[:1]
     out = call(
-        functools.partial(rest_kernel, axis, parts),
+        functools.partial(rest_kernel, axis, chip_parts),
         "residual",
         [resident, *blocks],
         [vmem()] * (1 + len(blocks)),
@@ -399,20 +411,21 @@
             pltpu.SemaphoreType.DMA((len(blocks),)),
         ],
     )
-    begin, size = chunks[-1]
-    return call(
-        functools.partial(last_kernel, axis, begin),
-        "residual_last",
-        [resident, from_cross[-1], out],
-        [vmem()] * 2 + [hbm()],
-        out_shape=shape,
-        out_specs=hbm(),
-        scratch_shapes=[
-            pltpu.VMEM((HALO, size, width), f32),
-            pltpu.SemaphoreType.DMA((1,)),
-        ],
-        input_output_aliases={2: 0},
-    )
+    for (begin, size), rim in zip(rim_chunks[1:], from_cross[1:]):
+        out = call(
+            functools.partial(last_kernel, axis, begin),
+            "residual_last",
+            [resident, rim, out],
+            [vmem()] * 2 + [hbm()],
+            out_shape=shape,
+            out_specs=hbm(),
+            scratch_shapes=[
+                pltpu.VMEM((HALO, size, width), f32),
+                pltpu.SemaphoreType.DMA((1,)),
+            ],
+            input_output_aliases={2: 0},
+        )
+    return out
 
 
 def solution(mesh):

time: 52.5 us -> 52.5 us (level)
  waiting for transfers between devices: 9.96 us -> 5.85 us
  starting transfers between devices: 16.5 us -> 19.9 us
    ppermute x4 -> x5, waiting for transfers between devices: 9.94 us -> 4.77 us  [swap_cross(): return in_vmem(lax.ppermute(x, axis, cross_pairs))]
    ppermute x4 -> x5, starting transfers between devices: 15.2 us -> 18.6 us  [swap_cross(): return in_vmem(lax.ppermute(x, axis, cross_pairs))]
    ppermute x6, waiting for transfers between devices: 0.02 us -> 1.08 us  [swap_chip(): return in_vmem(lax.ppermute(x, axis, chip_pairs))]
    pallas_call x10 -> x11, Pallas kernels: 25.5 us -> 25.9 us  [call(): pl.pallas_call(body, in_specs=in_specs + [pl.BlockSpec(memory_space=pl.AN...]
  transfers between devices with their start and end apart: 10 -> 11, of which waited for: 3 -> 4; matrix products, arithmetic and copies ran while one was open for 0% -> 0% of each run, Pallas kernels for 45% -> 46%
where the time goes in v6:
time: 52.5 us; the launch traced here: 51.9 us
  Pallas kernels  25.9 us (49%)
  starting transfers between devices  19.9 us (38%)
  waiting for transfers between devices  5.85 us (11%)
    pallas_call x11, Pallas kernels, call(): pl.pallas_call(body, in_specs=in_specs + [pl.BlockSpec(memory_space=pl.AN...  25.9 us
    ppermute x5, starting transfers between devices, swap_cross(): return in_vmem(lax.ppermute(x, axis, cross_pairs))  18.6 us
    ppermute x5, waiting for transfers between devices, swap_cross(): return in_vmem(lax.ppermute(x, axis, cross_pairs))  4.77 us
    ppermute x6, starting transfers between devices, swap_chip(): return in_vmem(lax.ppermute(x, axis, chip_pairs))  1.29 us
    ppermute x6, waiting for transfers between devices, swap_chip(): return in_vmem(lax.ppermute(x, axis, chip_pairs))  1.08 us
  transfers between devices with their start and end apart: 11, of which 4 were waited for; matrix products, arithmetic and copies ran while one was open for 0% of the time, Pallas kernels for 46%

profile of v6, /device:TPU:1, one launch (start us, length us, event | category | flops | bytes accessed | tf_op | source)
XLA Modules:
  0.0 51.9 jit_solution(8202048002792402620)
XLA Ops:
  0.0 1.1 %pick.2.refs_1_ = bf16[2,512,256]{2,1,0:T(8,128)(2,1)S(1)} custom-call(bf16[4,1024,256]{2,1,0:T(8,128)(2,1)} %refs_1_.1), custom_call_target="tpu_custom_call" | custom-call | flops 1 | bytes 1 | tf_op jit(solution)/shard_map/pick/pallas_call | solution.py:273
  1.1 4.5 %collective-permute-start.3 = (bf16[2,512,256]{2,1,0:T(8,128)(2,1)S(1)}, bf16[2,512,256]{2,1,0:T(8,128)(2,1)S(1)}, u32[]{:S(2)}, u32[]{:S(2)}) collective-permute-start(bf16[2,512,256]{2,1,0:T(8,128)(2,1)S(1)} %pick.2.refs_1_), channel_id=1, source_target_pairs={{1,2},{3,4},{5,6},{7,8},{9,10},{11,12},{13,14},{2,1},{4,3},{6,5},{... | collective-permute-start | bytes 1572872 | tf_op jit(solution)/shard_map/ppermute | solution.py:283
  5.6 1.4 %pick.3 = (bf16[2,512,256]{2,1,0:T(8,128)(2,1)S(1)}, bf16[2,384,256]{2,1,0:T(8,128)(2,1)S(1)}, bf16[2,384,256]{2,1,0:T(8,128)(2,1)S(1)}, bf16[2,256,256]{2,1,0:T(8,128)(2,1)S(1)}) custom-call(bf16[4,1024,256]{2,1,0:T(8,128)(2,1)} %refs_1_.1, bf16[2,512,256]{2,1,0:T(8,128)(2,1)S(1)} %pick.2.refs_1_), custom_call_target="tpu_custom_call" | custom-call | flops 1 | bytes 1 | tf_op jit(solution)/shard_map/pick/pallas_call | solution.py:273
  7.0 1.9 %collective-permute-start.4 = (bf16[2,512,256]{2,1,0:T(8,128)(2,1)S(1)}, bf16[2,512,256]{2,1,0:T(8,128)(2,1)S(1)}, u32[]{:S(2)}, u32[]{:S(2)}) collective-permute-start(bf16[2,512,256]{2,1,0:T(8,128)(2,1)S(1)} %get-tuple-element.26.refs_3_), channel_id=1, source_target_pairs={{1,2},{3,4},{5,6},{7,8},{9,10},{11,12},{13,14},{2,1},{4,3},{6,5},{... | collective-permute-start | bytes 1572872 | tf_op jit(solution)/shard_map/ppermute | solution.py:283
  9.0 0.5 collective-permute-start.1
  9.5 0.1 collective-permute-start.2
  9.6 7.5 %own_rims.1 = (s32[9,49]{1,0:T(8,128)S(1)}, bf16[4,1024,256]{2,1,0:T(8,128)(2,1)S(1)}, bf16[48,256,256]{2,1,0:T(8,128)(2,1)S(1)}, f32[2,1024,256]{2,1,0:T(8,128)...) custom-call(s32[2,48]{1,0:T(2,128)S(1)} %bitcast.1, ...), custom_call_target="tpu_custom_call" | custom-call | flops 1 | bytes 1 | tf_op jit(solution)/shard_map/own_rims/pallas_call | solution.py:273
  17.1 2.7 %chip_rims.1 = (f32[2,1024,256]{2,1,0:T(8,128)S(1)}, f32[2,512,256]{2,1,0:T(8,128)S(1)}, f32[2,432,256]{2,1,0:T(8,128)S(1)}, f32[2,80,256]{2,1,0:T(8,128)S(1)}) custom-call(s32[9,49]{1,0:T(8,128)S(1)} %get-tuple-element.30.refs_0_, ...), custom_call_target="tpu_custom_call", output_to_operand_aliasing={{0}: (5, {}), {1}: (6, {}), {2}: (7, {}), {3}: (8, {})} | custom-call | flops 1 | bytes 1 | tf_op jit(solution)/shard_map/chip_rims/pallas_call | solution.py:273
  19.8 3.2 %collective-permute-done.3.refs_3_ = bf16[2,512,256]{2,1,0:T(8,128)(2,1)S(1)} collective-permute-done((bf16[2,512,256]{2,1,0:T(8,128)(2,1)S(1)}, bf16[2,512,256]{2,1,0:T(8,128)(2,1)S(1)}, u32[]{:S(2)}, u32[]{:S(2)}) %collective-permute-start.3) | collective-permute-done | bytes 524320 | tf_op jit(solution)/shard_map/ppermute | solution.py:283
  22.9 1.0 %cross_rim.1 = (f32[2,512,256]{2,1,0:T(8,128)S(1)}, bf16[2,512,256]{2,1,0:T(8,128)(2,1)S(1)}) custom-call(s32[9,49]{1,0:T(8,128)S(1)} %get-tuple-element.30.refs_0_, bf16[48,256,256]{2,1,0:T(8,128)(2,1)S(1)} %get-tuple-element.31.refs_1_.refs_2_, f32[2,512,256]{2,1,0:T(8,128)S(1)} %get-tuple-element.37.refs_2_, ...), custom_call_target="tpu_custom_call", output_to_operand_aliasing={{0}: (2, {})} | custom-call | flops 1 | bytes 1 | tf_op jit(solution)/shard_map/cross_rim/pallas_call | solution.py:273
  23.9 4.8 %collective-permute-start.10 = (bf16[2,512,256]{2,1,0:T(8,128)(2,1)S(1)}, bf16[2,512,256]{2,1,0:T(8,128)(2,1)S(1)}, u32[]{:S(2)}, u32[]{:S(2)}) collective-permute-start(bf16[2,512,256]{2,1,0:T(8,128)(2,1)S(1)} %get-tuple-element.38.refs_6_), channel_id=1, source_target_pairs={{1,2},{3,4},{5,6},{7,8},{9,10},{11,12},{13,14},{2,1},{4,3},{6,5},{... | collective-permute-start | bytes 1572872 | tf_op jit(solution)/shard_map/ppermute | solution.py:283
  28.7 4.8 %own_targets.1.refs_7_.refs_2_ = f32[4,1024,256]{2,1,0:T(8,128)S(1)} custom-call(s32[9,49]{1,0:T(8,128)S(1)} %get-tuple-element.30.refs_0_, bf16[4,1024,256]{2,1,0:T(8,128)(2,1)S(1)} %get-tuple-element.32.refs_1_, bf16[48,256,256]{2,1,0:T(8,128)(2,1)S(1)} %get-tuple-element.31.refs_1_.refs_2_, bf16[2,384,256]{2,1,0:T(8,128)(2,1)S(1)} %collective-permute-done.refs_2_.refs_3_, ...), custom_call_target="tpu_custom_call" | custom-call | flops 1 | bytes 1 | tf_op jit(solution)/shard_map/own_targets/pallas_call | solution.py:273
  33.5 0.6 %collective-permute-done.4.refs_4_ = bf16[2,512,256]{2,1,0:T(8,128)(2,1)S(1)} collective-permute-done((bf16[2,512,256]{2,1,0:T(8,128)(2,1)S(1)}, bf16[2,512,256]{2,1,0:T(8,128)(2,1)S(1)}, u32[]{:S(2)}, u32[]{:S(2)}) %collective-permute-start.4) | collective-permute-done | bytes 524320 | tf_op jit(solution)/shard_map/ppermute | solution.py:283
  34.2 1.9 %last_rims.1 = (bf16[2,352,256]{2,1,0:T(8,128)(2,1)S(1)}, bf16[2,336,256]{2,1,0:T(8,128)(2,1)S(1)}, bf16[2,336,256]{2,1,0:T(8,128)(2,1)S(1)}, f32[2,1024,256]{2,...) custom-call(s32[9,49]{1,0:T(8,128)S(1)} %get-tuple-element.30.refs_0, ...), custom_call_target="tpu_custom_call", output_to_operand_aliasing={{3}: (2, {}), {4}: (5, {}), {5}: (6, {})} | custom-call | flops 1 | bytes 1 | tf_op jit(solution)/shard_map/last_rims/pallas_call | solution.py:273
  36.0 5.5 %collective-permute-start.6 = (bf16[2,432,256]{2,1,0:T(8,128)(2,1)S(1)}, bf16[2,432,256]{2,1,0:T(8,128)(2,1)S(1)}, u32[]{:S(2)}, u32[]{:S(2)}) collective-permute-start(bf16[2,432,256]{2,1,0:T(8,128)(2,1)S(1)} %get-tuple-element.43), channel_id=1, source_target_pairs={{1,2},{3,4},{5,6},{7,8},{9,10},{11,12},{13,14},{2,1},{4,3},{6,5},{... | collective-permute-start | bytes 1327112 | tf_op jit(solution)/shard_map/ppermute | solution.py:283
  41.6 0.5 collective-permute-start.7
  42.1 0.1 collective-permute-start.9
  42.2 1.1 %collective-permute-done.8.refs_2_ = bf16[2,336,256]{2,1,0:T(8,128)(2,1)S(1)} collective-permute-done((bf16[2,336,256]{2,1,0:T(8,128)(2,1)S(1)}, bf16[2,336,256]{2,1,0:T(8,128)(2,1)S(1)}, u32[]{:S(2)}, u32[]{:S(2)}) %collective-permute-start.8) | collective-permute-done | bytes 344096 | tf_op jit(solution)/shard_map/ppermute | solution.py:286
  43.2 1.9 %collective-permute-start.5 = (bf16[2,80,256]{2,1,0:T(8,128)(2,1)S(1)}, bf16[2,80,256]{2,1,0:T(8,128)(2,1)S(1)}, u32[]{:S(2)}, u32[]{:S(2)}) collective-permute-start(bf16[2,80,256]{2,1,0:T(8,128)(2,1)S(1)} %get-tuple-element.42.refs_5_), channel_id=1, source_target_pairs={{1,2},{3,4},{5,6},{7,8},{9,10},{11,12},{13,14},{2,1},{4,3},{6,5},{... | collective-permute-start | bytes 245768 | tf_op jit(solution)/shard_map/ppermute | solution.py:283
  45.2 2.2 %cross_sources.1.refs_0_ = f32[4,1024,256]{2,1,0:T(8,128)S(1)} custom-call(s32[9,49]{1,0:T(8,128)S(1)} %get-tuple-element.30.refs_0_, bf16[48,256,256]{2,1,0:T(8,128)(2,1)S(1)} %get-tuple-element.31.refs_1_.refs_2_, f32[4,1024,256]{2,1,0:T(8,128)S(1)} %own_targets.1.refs_7_.refs_2_, ...), custom_call_target="tpu_custom_call", output_to_operand_aliasing={{}: (2, {})} | custom-call | flops 1 | bytes 1 | tf_op jit(solution)/shard_map/cross_sources/pallas_call | solution.py:273
  47.4 1.8 %residual.1.refs_2_ = f32[4,1024,256]{2,1,0:T(8,128)} custom-call(f32[4,1024,256]{2,1,0:T(8,128)S(1)} %cross_sources.1.refs_0_, bf16[2,352,256]{2,1,0:T(8,128)(2,1)S(1)} %collective-permute-done.7.refs_1_, bf16[2,336,256]{2,1,0:T(8,128)(2,1)S(1)} %collective-permute-done.8.refs_2_, bf16[2,336,256]{2,1,0:T(8,128)(2,1)S(1)} %collective-permute-done.9.refs_3_, ...), custom_call_target="tpu_custom_call" | custom-call | flops 1 | bytes 1 | tf_op jit(solution)/shard_map/residual/pallas_call | solution.py:273
  49.2 1.0 %collective-permute-done.6.refs_1_ = bf16[2,432,256]{2,1,0:T(8,128)(2,1)S(1)} collective-permute-done((bf16[2,432,256]{2,1,0:T(8,128)(2,1)S(1)}, bf16[2,432,256]{2,1,0:T(8,128)(2,1)S(1)}, u32[]{:S(2)}, u32[]{:S(2)}) %collective-permute-start.6) | collective-permute-done | bytes 442400 | tf_op jit(solution)/shard_map/ppermute | solution.py:283
  50.1 1.0 %residual_last.2.refs_2_ = f32[4,1024,256]{2,1,0:T(8,128)} custom-call(f32[4,1024,256]{2,1,0:T(8,128)S(1)} %cross_sources.1.refs_0_, bf16[2,432,256]{2,1,0:T(8,128)(2,1)S(1)} %collective-permute-done.6.refs_1_, f32[4,1024,256]{2,1,0:T(8,128)} %residual.1.refs_2_), custom_call_target="tpu_custom_call", output_to_operand_aliasing={{}: (2, {})} | custom-call | flops 1 | bytes 1 | tf_op jit(solution)/shard_map/residual_last/pallas_call | solution.py:273
  51.2 0.7 %residual_last.3 = f32[4,1024,256]{2,1,0:T(8,128)} custom-call(f32[4,1024,256]{2,1,0:T(8,128)S(1)} %cross_sources.1.refs_0_, bf16[2,80,256]{2,1,0:T(8,128)(2,1)S(1)} %collective-permute-done.5.refs_1_, f32[4,1024,256]{2,1,0:T(8,128)} %residual_last.2.refs_2_), custom_call_target="tpu_custom_call", output_to_operand_aliasing={{}: (2, {})} | custom-call | flops 1 | bytes 1 | tf_op jit(solution)/shard_map/residual_last/pallas_call | solution.py:273
  (11 shorter events, 0.2 us)
Async XLA Ops:
  0.0 9.6 %copy-start = (s32[48,2]{0,1:T(2,128)S(1)}, s32[48,2]{0,1:T(2,128)}, u32[]{:S(2)}) copy-start(s32[48,2]{0,1:T(2,128)} %param.5) | copy-start | bytes 1156
  1.1 21.9 %collective-permute-start.3 = (bf16[2,512,256]{2,1,0:T(8,128)(2,1)S(1)}, bf16[2,512,256]{2,1,0:T(8,128)(2,1)S(1)}, u32[]{:S(2)}, u32[]{:S(2)}) collective-permute-start(bf16[2,512,256]{2,1,0:T(8,128)(2,1)S(1)} %pick.2.refs_1_), channel_id=1, source_target_pairs={{1,2},{3,4},{5,6},{7,8},{9,10},{11,12},{13,14},{2,1},{4,3},{6,5},{... | collective-permute-start | bytes 1572872 | tf_op jit(solution)/shard_map/ppermute | solution.py:283
  7.0 27.2 %collective-permute-start.4 = (bf16[2,512,256]{2,1,0:T(8,128)(2,1)S(1)}, bf16[2,512,256]{2,1,0:T(8,128)(2,1)S(1)}, u32[]{:S(2)}, u32[]{:S(2)}) collective-permute-start(bf16[2,512,256]{2,1,0:T(8,128)(2,1)S(1)} %get-tuple-element.26.refs_3_), channel_id=1, source_target_pairs={{1,2},{3,4},{5,6},{7,8},{9,10},{11,12},{13,14},{2,1},{4,3},{6,5},{... | collective-permute-start | bytes 1572872 | tf_op jit(solution)/shard_map/ppermute | solution.py:283
  8.9 8.1 %collective-permute-start = (bf16[2,384,256]{2,1,0:T(8,128)(2,1)S(1)}, bf16[2,384,256]{2,1,0:T(8,128)(2,1)S(1)}, u32[]{:S(2)}, u32[]{:S(2)}) collective-permute-start(bf16[2,384,256]{2,1,0:T(8,128)(2,1)S(1)} %get-tuple-element.27.refs_4_), channel_id=1, source_target_pairs={{0,1},{1,0},{2,3},{3,2},{4,5},{5,4},{6,7},{7,6},{8,9},{9,8},{10,11... | collective-permute-start | bytes 1179656 | tf_op jit(solution)/shard_map/ppermute | solution.py:286
  9.0 8.1 %collective-permute-start.1 = (bf16[2,384,256]{2,1,0:T(8,128)(2,1)S(1)}, bf16[2,384,256]{2,1,0:T(8,128)(2,1)S(1)}, u32[]{:S(2)}, u32[]{:S(2)}) collective-permute-start(bf16[2,384,256]{2,1,0:T(8,128)(2,1)S(1)} %get-tuple-element.28.refs_5_), channel_id=1, source_target_pairs={{0,1},{1,0},{2,3},{3,2},{4,5},{5,4},{6,7},{7,6},{8,9},{9,8},{10,11... | collective-permute-start | bytes 1179656 | tf_op jit(solution)/shard_map/ppermute | solution.py:286
  9.5 7.6 %collective-permute-start.2 = (bf16[2,256,256]{2,1,0:T(8,128)(2,1)S(1)}, bf16[2,256,256]{2,1,0:T(8,128)(2,1)S(1)}, u32[]{:S(2)}, u32[]{:S(2)}) collective-permute-start(bf16[2,256,256]{2,1,0:T(8,128)(2,1)S(1)} %get-tuple-element.29.refs_6_), channel_id=1, source_target_pairs={{0,1},{1,0},{2,3},{3,2},{4,5},{5,4},{6,7},{7,6},{8,9},{9,8},{10,11... | collective-permute-start | bytes 786440 | tf_op jit(solution)/shard_map/ppermute | solution.py:286
  23.9 23.5 %collective-permute-start.10 = (bf16[2,512,256]{2,1,0:T(8,128)(2,1)S(1)}, bf16[2,512,256]{2,1,0:T(8,128)(2,1)S(1)}, u32[]{:S(2)}, u32[]{:S(2)}) collective-permute-start(bf16[2,512,256]{2,1,0:T(8,128)(2,1)S(1)} %get-tuple-element.38.refs_6_), channel_id=1, source_target_pairs={{1,2},{3,4},{5,6},{7,8},{9,10},{11,12},{13,14},{2,1},{4,3},{6,5},{... | collective-permute-start | bytes 1572872 | tf_op jit(solution)/shard_map/ppermute | solution.py:283
  36.0 14.1 %collective-permute-start.6 = (bf16[2,432,256]{2,1,0:T(8,128)(2,1)S(1)}, bf16[2,432,256]{2,1,0:T(8,128)(2,1)S(1)}, u32[]{:S(2)}, u32[]{:S(2)}) collective-permute-start(bf16[2,432,256]{2,1,0:T(8,128)(2,1)S(1)} %get-tuple-element.43), channel_id=1, source_target_pairs={{1,2},{3,4},{5,6},{7,8},{9,10},{11,12},{13,14},{2,1},{4,3},{6,5},{... | collective-permute-start | bytes 1327112 | tf_op jit(solution)/shard_map/ppermute | solution.py:283
  41.5 1.7 %collective-permute-start.8 = (bf16[2,336,256]{2,1,0:T(8,128)(2,1)S(1)}, bf16[2,336,256]{2,1,0:T(8,128)(2,1)S(1)}, u32[]{:S(2)}, u32[]{:S(2)}) collective-permute-start(bf16[2,336,256]{2,1,0:T(8,128)(2,1)S(1)} %get-tuple-element.45), channel_id=1, source_target_pairs={{0,1},{1,0},{2,3},{3,2},{4,5},{5,4},{6,7},{7,6},{8,9},{9,8},{10,11... | collective-permute-start | bytes 1032200 | tf_op jit(solution)/shard_map/ppermute | solution.py:286
  41.6 5.8 %collective-permute-start.7 = (bf16[2,352,256]{2,1,0:T(8,128)(2,1)S(1)}, bf16[2,352,256]{2,1,0:T(8,128)(2,1)S(1)}, u32[]{:S(2)}, u32[]{:S(2)}) collective-permute-start(bf16[2,352,256]{2,1,0:T(8,128)(2,1)S(1)} %get-tuple-element.44), channel_id=1, source_target_pairs={{0,1},{1,0},{2,3},{3,2},{4,5},{5,4},{6,7},{7,6},{8,9},{9,8},{10,11... | collective-permute-start | bytes 1081352 | tf_op jit(solution)/shard_map/ppermute | solution.py:286
  42.1 5.3 %collective-permute-start.9 = (bf16[2,336,256]{2,1,0:T(8,128)(2,1)S(1)}, bf16[2,336,256]{2,1,0:T(8,128)(2,1)S(1)}, u32[]{:S(2)}, u32[]{:S(2)}) collective-permute-start(bf16[2,336,256]{2,1,0:T(8,128)(2,1)S(1)} %get-tuple-element.46), channel_id=1, source_target_pairs={{0,1},{1,0},{2,3},{3,2},{4,5},{5,4},{6,7},{7,6},{8,9},{9,8},{10,11... | collective-permute-start | bytes 1032200 | tf_op jit(solution)/shard_map/ppermute | solution.py:286
  43.2 7.9 %collective-permute-start.5 = (bf16[2,80,256]{2,1,0:T(8,128)(2,1)S(1)}, bf16[2,80,256]{2,1,0:T(8,128)(2,1)S(1)}, u32[]{:S(2)}, u32[]{:S(2)}) collective-permute-start(bf16[2,80,256]{2,1,0:T(8,128)(2,1)S(1)} %get-tuple-element.42.refs_5_), channel_id=1, source_target_pairs={{1,2},{3,4},{5,6},{7,8},{9,10},{11,12},{13,14},{2,1},{4,3},{6,5},{... | collective-permute-start | bytes 245768 | tf_op jit(solution)/shard_map/ppermute | solution.py:283

commit v7 on v6

--- a/solution.py
+++ b/solution.py
@@ -212,6 +212,10 @@
     accumulate(plan, 3 * CROSS + OWN, integrals, overlaps(halos, [total]))
 
 
+def pass_kernel(block, same):
+    pass
+
+
 def add_rim(places, sums, out, sems):
     copies = []
     for first, rims, begin, part, sem in places:
@@ -294,8 +298,8 @@
             [amplitudes],
             [hbm()],
             after=after,
-            out_shape=[jax.ShapeDtypeStruct((HALO, size, width), bf16) for size in sizes],
-            out_specs=[hbm()] * len(sizes),
+            out_shape=[pltpu.VMEM((HALO, size, width), bf16) for size in sizes],
+            out_specs=[vmem()] * len(sizes),
             scratch_shapes=[pltpu.SemaphoreType.DMA((len(sizes),))],
         )
 
@@ -384,18 +388,29 @@
     chip_rims, rim = got[:chip_parts], got[-1]
     rims += got[-more:]
     from_chip = [swap_chip(x) for x in chip_rims]
-    from_cross = [swap_cross(x) for x in rims]
+    from_cross = [swap_cross(x) for x in rims[:-1]]
     resident = call(
         resident_kernel,
         "cross_sources",
         [plan, held, resident, *halos],
         [smem()] + [vmem()] * (2 + count),
-        after=[in_vmem(rim)],
+        after=[in_vmem(rims[-2])],
         out_shape=resident_shape,
         out_specs=vmem(),
         input_output_aliases={2: 0},
     )
     resident = in_vmem(resident)
+    rim = call(
+        pass_kernel,
+        "pass_on",
+        [in_vmem(rim)],
+        [vmem()],
+        after=[resident],
+        out_shape=pltpu.VMEM(rim.shape, bf16),
+        out_specs=vmem(),
+        input_output_aliases={0: 0},
+    )
+    from_cross.append(swap_cross(rim))
 
     shape = jax.ShapeDtypeStruct((tile_count, rows, width), f32)
     blocks = from_chip + from_cross[:1]

time: 52.5 us -> 52.1 us (level)
  starting transfers between devices: 19.9 us -> 18.7 us
  waiting for transfers between devices: 5.85 us -> 6.89 us
    ppermute x5, waiting for transfers between devices: 4.77 us -> 6.87 us  [swap_cross(): return in_vmem(lax.ppermute(x, axis, cross_pairs))]
    ppermute x5, starting transfers between devices: 18.6 us -> 17.4 us  [swap_cross(): return in_vmem(lax.ppermute(x, axis, cross_pairs))]
    ppermute x6, waiting for transfers between devices: 1.08 us -> 0.02 us  [swap_chip(): return in_vmem(lax.ppermute(x, axis, chip_pairs))]
    pallas_call x11 -> x12, Pallas kernels: 25.9 us -> 26 us  [call(): pl.pallas_call(body, in_specs=in_specs + [pl.BlockSpec(memory_space=pl.AN...]
  transfers between devices with their start and end apart: 11 -> 11, of which waited for: 4 -> 3; matrix products, arithmetic and copies ran while one was open for 0% -> 0% of each run, Pallas kernels for 46% -> 47%
where the time goes in v7:
time: 52.1 us; the launch traced here: 51.9 us
  Pallas kernels  26 us (50%)
  starting transfers between devices  18.7 us (36%)
  waiting for transfers between devices  6.89 us (13%)
    pallas_call x12, Pallas kernels, call(): pl.pallas_call(body, in_specs=in_specs + [pl.BlockSpec(memory_space=pl.AN...  26 us
    ppermute x5, starting transfers between devices, swap_cross(): return in_vmem(lax.ppermute(x, axis, cross_pairs))  17.4 us
    ppermute x5, waiting for transfers between devices, swap_cross(): return in_vmem(lax.ppermute(x, axis, cross_pairs))  6.87 us
    ppermute x6, starting transfers between devices, swap_chip(): return in_vmem(lax.ppermute(x, axis, chip_pairs))  1.29 us
  transfers between devices with their start and end apart: 11, of which 3 were waited for; matrix products, arithmetic and copies ran while one was open for 0% of the time, Pallas kernels for 47%

profile of v7, /device:TPU:1, one launch (start us, length us, event | category | flops | bytes accessed | tf_op | source)
XLA Modules:
  0.0 51.9 jit_solution(3196720352579191341)
XLA Ops:
  0.0 1.1 %pick.2.refs_1_ = bf16[2,512,256]{2,1,0:T(8,128)(2,1)S(1)} custom-call(bf16[4,1024,256]{2,1,0:T(8,128)(2,1)} %refs_1_.1), custom_call_target="tpu_custom_call" | custom-call | flops 1 | bytes 1 | tf_op jit(solution)/shard_map/pick/pallas_call | solution.py:277
  1.1 4.5 %collective-permute-start.3 = (bf16[2,512,256]{2,1,0:T(8,128)(2,1)S(1)}, bf16[2,512,256]{2,1,0:T(8,128)(2,1)S(1)}, u32[]{:S(2)}, u32[]{:S(2)}) collective-permute-start(bf16[2,512,256]{2,1,0:T(8,128)(2,1)S(1)} %pick.2.refs_1_), channel_id=1, source_target_pairs={{1,2},{3,4},{5,6},{7,8},{9,10},{11,12},{13,14},{2,1},{4,3},{6,5},{... | collective-permute-start | bytes 1572872 | tf_op jit(solution)/shard_map/ppermute | solution.py:287
  5.6 1.4 %pick.3 = (bf16[2,512,256]{2,1,0:T(8,128)(2,1)S(1)}, bf16[2,384,256]{2,1,0:T(8,128)(2,1)S(1)}, bf16[2,384,256]{2,1,0:T(8,128)(2,1)S(1)}, bf16[2,256,256]{2,1,0:T(8,128)(2,1)S(1)}) custom-call(bf16[4,1024,256]{2,1,0:T(8,128)(2,1)} %refs_1_.1, bf16[2,512,256]{2,1,0:T(8,128)(2,1)S(1)} %pick.2.refs_1_), custom_call_target="tpu_custom_call" | custom-call | flops 1 | bytes 1 | tf_op jit(solution)/shard_map/pick/pallas_call | solution.py:277
  7.0 1.9 %collective-permute-start.4 = (bf16[2,512,256]{2,1,0:T(8,128)(2,1)S(1)}, bf16[2,512,256]{2,1,0:T(8,128)(2,1)S(1)}, u32[]{:S(2)}, u32[]{:S(2)}) collective-permute-start(bf16[2,512,256]{2,1,0:T(8,128)(2,1)S(1)} %get-tuple-element.26.refs_3_), channel_id=1, source_target_pairs={{1,2},{3,4},{5,6},{7,8},{9,10},{11,12},{13,14},{2,1},{4,3},{6,5},{... | collective-permute-start | bytes 1572872 | tf_op jit(solution)/shard_map/ppermute | solution.py:287
  9.0 0.5 collective-permute-start.1
  9.5 0.1 collective-permute-start.2
  9.6 7.5 %own_rims.1 = (s32[9,49]{1,0:T(8,128)S(1)}, bf16[4,1024,256]{2,1,0:T(8,128)(2,1)S(1)}, bf16[48,256,256]{2,1,0:T(8,128)(2,1)S(1)}, f32[2,1024,256]{2,1,0:T(8,128)...) custom-call(s32[2,48]{1,0:T(2,128)S(1)} %bitcast.1, ...), custom_call_target="tpu_custom_call" | custom-call | flops 1 | bytes 1 | tf_op jit(solution)/shard_map/own_rims/pallas_call | solution.py:277
  17.1 2.3 %chip_rims.1 = (f32[2,1024,256]{2,1,0:T(8,128)S(1)}, f32[2,512,256]{2,1,0:T(8,128)S(1)}, f32[2,432,256]{2,1,0:T(8,128)S(1)}, f32[2,80,256]{2,1,0:T(8,128)S(1)}) custom-call(s32[9,49]{1,0:T(8,128)S(1)} %get-tuple-element.30.refs_0_, ...), custom_call_target="tpu_custom_call", output_to_operand_aliasing={{0}: (5, {}), {1}: (6, {}), {2}: (7, {}), {3}: (8, {})} | custom-call | flops 1 | bytes 1 | tf_op jit(solution)/shard_map/chip_rims/pallas_call | solution.py:277
  19.4 3.5 %collective-permute-done.3.refs_3_ = bf16[2,512,256]{2,1,0:T(8,128)(2,1)S(1)} collective-permute-done((bf16[2,512,256]{2,1,0:T(8,128)(2,1)S(1)}, bf16[2,512,256]{2,1,0:T(8,128)(2,1)S(1)}, u32[]{:S(2)}, u32[]{:S(2)}) %collective-permute-start.3) | collective-permute-done | bytes 524320 | tf_op jit(solution)/shard_map/ppermute | solution.py:287
  22.9 1.1 %cross_rim.1 = (f32[2,512,256]{2,1,0:T(8,128)S(1)}, bf16[2,512,256]{2,1,0:T(8,128)(2,1)S(1)}) custom-call(s32[9,49]{1,0:T(8,128)S(1)} %get-tuple-element.30.refs_0_, bf16[48,256,256]{2,1,0:T(8,128)(2,1)S(1)} %get-tuple-element.31.refs_1_.refs_2_, f32[2,512,256]{2,1,0:T(8,128)S(1)} %get-tuple-element.37.refs_2_, ...), custom_call_target="tpu_custom_call", output_to_operand_aliasing={{0}: (2, {})} | custom-call | flops 1 | bytes 1 | tf_op jit(solution)/shard_map/cross_rim/pallas_call | solution.py:277
  24.0 4.4 %collective-permute-start.10 = (bf16[2,512,256]{2,1,0:T(8,128)(2,1)S(1)}, bf16[2,512,256]{2,1,0:T(8,128)(2,1)S(1)}, u32[]{:S(2)}, u32[]{:S(2)}) collective-permute-start(bf16[2,512,256]{2,1,0:T(8,128)(2,1)S(1)} %get-tuple-element.38.refs_6_), channel_id=1, source_target_pairs={{1,2},{3,4},{5,6},{7,8},{9,10},{11,12},{13,14},{2,1},{4,3},{6,5},{... | collective-permute-start | bytes 1572872 | tf_op jit(solution)/shard_map/ppermute | solution.py:287
  28.4 4.1 %own_targets.1.refs_7_.refs_2_ = f32[4,1024,256]{2,1,0:T(8,128)S(1)} custom-call(s32[9,49]{1,0:T(8,128)S(1)} %get-tuple-element.30.refs_0_, bf16[4,1024,256]{2,1,0:T(8,128)(2,1)S(1)} %get-tuple-element.32.refs_1_, bf16[48,256,256]{2,1,0:T(8,128)(2,1)S(1)} %get-tuple-element.31.refs_1_.refs_2_, bf16[2,384,256]{2,1,0:T(8,128)(2,1)S(1)} %collective-permute-done.refs_2_.refs_3_, ...), custom_call_target="tpu_custom_call" | custom-call | flops 1 | bytes 1 | tf_op jit(solution)/shard_map/own_targets/pallas_call | solution.py:277
  32.5 1.7 %collective-permute-done.4.refs_4_ = bf16[2,512,256]{2,1,0:T(8,128)(2,1)S(1)} collective-permute-done((bf16[2,512,256]{2,1,0:T(8,128)(2,1)S(1)}, bf16[2,512,256]{2,1,0:T(8,128)(2,1)S(1)}, u32[]{:S(2)}, u32[]{:S(2)}) %collective-permute-start.4) | collective-permute-done | bytes 524320 | tf_op jit(solution)/shard_map/ppermute | solution.py:287
  34.2 2.1 %last_rims.1 = (bf16[2,352,256]{2,1,0:T(8,128)(2,1)S(1)}, bf16[2,336,256]{2,1,0:T(8,128)(2,1)S(1)}, bf16[2,336,256]{2,1,0:T(8,128)(2,1)S(1)}, f32[2,1024,256]{2,...) custom-call(s32[9,49]{1,0:T(8,128)S(1)} %get-tuple-element.30.refs_0, ...), custom_call_target="tpu_custom_call", output_to_operand_aliasing={{3}: (2, {}), {4}: (5, {}), {5}: (6, {})} | custom-call | flops 1 | bytes 1 | tf_op jit(solution)/shard_map/last_rims/pallas_call | solution.py:277
  36.3 4.2 %collective-permute-start.6 = (bf16[2,432,256]{2,1,0:T(8,128)(2,1)S(1)}, bf16[2,432,256]{2,1,0:T(8,128)(2,1)S(1)}, u32[]{:S(2)}, u32[]{:S(2)}) collective-permute-start(bf16[2,432,256]{2,1,0:T(8,128)(2,1)S(1)} %get-tuple-element.42.refs_5_), channel_id=1, source_target_pairs={{1,2},{3,4},{5,6},{7,8},{9,10},{11,12},{13,14},{2,1},{4,3},{6,5},{... | collective-permute-start | bytes 1327112 | tf_op jit(solution)/shard_map/ppermute | solution.py:287
  40.5 0.1 collective-permute-start.8
  40.6 0.5 collective-permute-start.7
  41.1 0.1 collective-permute-start.9
  41.2 3.0 %cross_sources.1.refs_1_.refs_0_ = f32[4,1024,256]{2,1,0:T(8,128)S(1)} custom-call(s32[9,49]{1,0:T(8,128)S(1)} %get-tuple-element.30.refs_0_, bf16[48,256,256]{2,1,0:T(8,128)(2,1)S(1)} %get-tuple-element.31.refs_1_.refs_2_, f32[4,1024,256]{2,1,0:T(8,128)S(1)} %own_targets.1.refs_7_.refs_2_, ...), custom_call_target="tpu_custom_call", output_to_operand_aliasing={{}: (2, {})} | custom-call | flops 1 | bytes 1 | tf_op jit(solution)/shard_map/cross_sources/pallas_call | solution.py:277
  44.2 2.4 %collective-permute-start.5 = (bf16[2,80,256]{2,1,0:T(8,128)(2,1)S(1)}, bf16[2,80,256]{2,1,0:T(8,128)(2,1)S(1)}, u32[]{:S(2)}, u32[]{:S(2)}) collective-permute-start(bf16[2,80,256]{2,1,0:T(8,128)(2,1)S(1)} %pass_on.1), channel_id=1, source_target_pairs={{1,2},{3,4},{5,6},{7,8},{9,10},{11,12},{13,14},{2,1},{4,3},{6,5},{... | collective-permute-start | bytes 245768 | tf_op jit(solution)/shard_map/ppermute | solution.py:287
  46.6 1.8 %residual.1.refs_2_ = f32[4,1024,256]{2,1,0:T(8,128)} custom-call(f32[4,1024,256]{2,1,0:T(8,128)S(1)} %cross_sources.1.refs_1_.refs_0_, bf16[2,352,256]{2,1,0:T(8,128)(2,1)S(1)} %collective-permute-done.7.refs_1_, bf16[2,336,256]{2,1,0:T(8,128)(2,1)S(1)} %collective-permute-done.8.refs_2_, bf16[2,336,256]{2,1,0:T(8,128)(2,1)S(1)} %collective-permute-done.9.refs_3_, ...), custom_call_target="tpu_custom_call" | custom-call | flops 1 | bytes 1 | tf_op jit(solution)/shard_map/residual/pallas_call | solution.py:277
  48.4 1.7 %collective-permute-done.6.refs_1_ = bf16[2,432,256]{2,1,0:T(8,128)(2,1)S(1)} collective-permute-done((bf16[2,432,256]{2,1,0:T(8,128)(2,1)S(1)}, bf16[2,432,256]{2,1,0:T(8,128)(2,1)S(1)}, u32[]{:S(2)}, u32[]{:S(2)}) %collective-permute-start.6) | collective-permute-done | bytes 442400 | tf_op jit(solution)/shard_map/ppermute | solution.py:287
  50.1 1.0 %residual_last.2.refs_2_ = f32[4,1024,256]{2,1,0:T(8,128)} custom-call(f32[4,1024,256]{2,1,0:T(8,128)S(1)} %cross_sources.1.refs_1_.refs_0_, bf16[2,432,256]{2,1,0:T(8,128)(2,1)S(1)} %collective-permute-done.6.refs_1_, f32[4,1024,256]{2,1,0:T(8,128)} %residual.1.refs_2_), custom_call_target="tpu_custom_call", output_to_operand_aliasing={{}: (2, {})} | custom-call | flops 1 | bytes 1 | tf_op jit(solution)/shard_map/residual_last/pallas_call | solution.py:277
  51.2 0.7 %residual_last.3 = f32[4,1024,256]{2,1,0:T(8,128)} custom-call(f32[4,1024,256]{2,1,0:T(8,128)S(1)} %cross_sources.1.refs_1_.refs_0_, bf16[2,80,256]{2,1,0:T(8,128)(2,1)S(1)} %collective-permute-done.5.refs_1_, f32[4,1024,256]{2,1,0:T(8,128)} %residual_last.2.refs_2_), custom_call_target="tpu_custom_call", output_to_operand_aliasing={{}: (2, {})} | custom-call | flops 1 | bytes 1 | tf_op jit(solution)/shard_map/residual_last/pallas_call | solution.py:277
  (12 shorter events, 0.1 us)
Async XLA Ops:
  0.0 9.6 %copy-start = (s32[48,2]{0,1:T(2,128)S(1)}, s32[48,2]{0,1:T(2,128)}, u32[]{:S(2)}) copy-start(s32[48,2]{0,1:T(2,128)} %param.5) | copy-start | bytes 1156
  1.1 21.9 %collective-permute-start.3 = (bf16[2,512,256]{2,1,0:T(8,128)(2,1)S(1)}, bf16[2,512,256]{2,1,0:T(8,128)(2,1)S(1)}, u32[]{:S(2)}, u32[]{:S(2)}) collective-permute-start(bf16[2,512,256]{2,1,0:T(8,128)(2,1)S(1)} %pick.2.refs_1_), channel_id=1, source_target_pairs={{1,2},{3,4},{5,6},{7,8},{9,10},{11,12},{13,14},{2,1},{4,3},{6,5},{... | collective-permute-start | bytes 1572872 | tf_op jit(solution)/shard_map/ppermute | solution.py:287
  7.0 27.2 %collective-permute-start.4 = (bf16[2,512,256]{2,1,0:T(8,128)(2,1)S(1)}, bf16[2,512,256]{2,1,0:T(8,128)(2,1)S(1)}, u32[]{:S(2)}, u32[]{:S(2)}) collective-permute-start(bf16[2,512,256]{2,1,0:T(8,128)(2,1)S(1)} %get-tuple-element.26.refs_3_), channel_id=1, source_target_pairs={{1,2},{3,4},{5,6},{7,8},{9,10},{11,12},{13,14},{2,1},{4,3},{6,5},{... | collective-permute-start | bytes 1572872 | tf_op jit(solution)/shard_map/ppermute | solution.py:287
  8.9 8.1 %collective-permute-start = (bf16[2,384,256]{2,1,0:T(8,128)(2,1)S(1)}, bf16[2,384,256]{2,1,0:T(8,128)(2,1)S(1)}, u32[]{:S(2)}, u32[]{:S(2)}) collective-permute-start(bf16[2,384,256]{2,1,0:T(8,128)(2,1)S(1)} %get-tuple-element.27.refs_4_), channel_id=1, source_target_pairs={{0,1},{1,0},{2,3},{3,2},{4,5},{5,4},{6,7},{7,6},{8,9},{9,8},{10,11... | collective-permute-start | bytes 1179656 | tf_op jit(solution)/shard_map/ppermute | solution.py:290
  9.0 8.1 %collective-permute-start.1 = (bf16[2,384,256]{2,1,0:T(8,128)(2,1)S(1)}, bf16[2,384,256]{2,1,0:T(8,128)(2,1)S(1)}, u32[]{:S(2)}, u32[]{:S(2)}) collective-permute-start(bf16[2,384,256]{2,1,0:T(8,128)(2,1)S(1)} %get-tuple-element.28.refs_5_), channel_id=1, source_target_pairs={{0,1},{1,0},{2,3},{3,2},{4,5},{5,4},{6,7},{7,6},{8,9},{9,8},{10,11... | collective-permute-start | bytes 1179656 | tf_op jit(solution)/shard_map/ppermute | solution.py:290
  9.5 7.6 %collective-permute-start.2 = (bf16[2,256,256]{2,1,0:T(8,128)(2,1)S(1)}, bf16[2,256,256]{2,1,0:T(8,128)(2,1)S(1)}, u32[]{:S(2)}, u32[]{:S(2)}) collective-permute-start(bf16[2,256,256]{2,1,0:T(8,128)(2,1)S(1)} %get-tuple-element.29.refs_6_), channel_id=1, source_target_pairs={{0,1},{1,0},{2,3},{3,2},{4,5},{5,4},{6,7},{7,6},{8,9},{9,8},{10,11... | collective-permute-start | bytes 786440 | tf_op jit(solution)/shard_map/ppermute | solution.py:290
  24.0 22.6 %collective-permute-start.10 = (bf16[2,512,256]{2,1,0:T(8,128)(2,1)S(1)}, bf16[2,512,256]{2,1,0:T(8,128)(2,1)S(1)}, u32[]{:S(2)}, u32[]{:S(2)}) collective-permute-start(bf16[2,512,256]{2,1,0:T(8,128)(2,1)S(1)} %get-tuple-element.38.refs_6_), channel_id=1, source_target_pairs={{1,2},{3,4},{5,6},{7,8},{9,10},{11,12},{13,14},{2,1},{4,3},{6,5},{... | collective-permute-start | bytes 1572872 | tf_op jit(solution)/shard_map/ppermute | solution.py:287
  36.3 13.8 %collective-permute-start.6 = (bf16[2,432,256]{2,1,0:T(8,128)(2,1)S(1)}, bf16[2,432,256]{2,1,0:T(8,128)(2,1)S(1)}, u32[]{:S(2)}, u32[]{:S(2)}) collective-permute-start(bf16[2,432,256]{2,1,0:T(8,128)(2,1)S(1)} %get-tuple-element.42.refs_5_), channel_id=1, source_target_pairs={{1,2},{3,4},{5,6},{7,8},{9,10},{11,12},{13,14},{2,1},{4,3},{6,5},{... | collective-permute-start | bytes 1327112 | tf_op jit(solution)/shard_map/ppermute | solution.py:287
  40.5 3.6 %collective-permute-start.8 = (bf16[2,336,256]{2,1,0:T(8,128)(2,1)S(1)}, bf16[2,336,256]{2,1,0:T(8,128)(2,1)S(1)}, u32[]{:S(2)}, u32[]{:S(2)}) collective-permute-start(bf16[2,336,256]{2,1,0:T(8,128)(2,1)S(1)} %get-tuple-element.45), channel_id=1, source_target_pairs={{0,1},{1,0},{2,3},{3,2},{4,5},{5,4},{6,7},{7,6},{8,9},{9,8},{10,11... | collective-permute-start | bytes 1032200 | tf_op jit(solution)/shard_map/ppermute | solution.py:290
  40.6 6.0 %collective-permute-start.7 = (bf16[2,352,256]{2,1,0:T(8,128)(2,1)S(1)}, bf16[2,352,256]{2,1,0:T(8,128)(2,1)S(1)}, u32[]{:S(2)}, u32[]{:S(2)}) collective-permute-start(bf16[2,352,256]{2,1,0:T(8,128)(2,1)S(1)} %get-tuple-element.44), channel_id=1, source_target_pairs={{0,1},{1,0},{2,3},{3,2},{4,5},{5,4},{6,7},{7,6},{8,9},{9,8},{10,11... | collective-permute-start | bytes 1081352 | tf_op jit(solution)/shard_map/ppermute | solution.py:290
  41.1 5.5 %collective-permute-start.9 = (bf16[2,336,256]{2,1,0:T(8,128)(2,1)S(1)}, bf16[2,336,256]{2,1,0:T(8,128)(2,1)S(1)}, u32[]{:S(2)}, u32[]{:S(2)}) collective-permute-start(bf16[2,336,256]{2,1,0:T(8,128)(2,1)S(1)} %get-tuple-element.46), channel_id=1, source_target_pairs={{0,1},{1,0},{2,3},{3,2},{4,5},{5,4},{6,7},{7,6},{8,9},{9,8},{10,11... | collective-permute-start | bytes 1032200 | tf_op jit(solution)/shard_map/ppermute | solution.py:290
  44.2 7.0 %collective-permute-start.5 = (bf16[2,80,256]{2,1,0:T(8,128)(2,1)S(1)}, bf16[2,80,256]{2,1,0:T(8,128)(2,1)S(1)}, u32[]{:S(2)}, u32[]{:S(2)}) collective-permute-start(bf16[2,80,256]{2,1,0:T(8,128)(2,1)S(1)} %pass_on.1), channel_id=1, source_target_pairs={{1,2},{3,4},{5,6},{7,8},{9,10},{11,12},{13,14},{2,1},{4,3},{6,5},{... | collective-permute-start | bytes 245768 | tf_op jit(solution)/shard_map/ppermute | solution.py:287

commit v8 on v7

--- a/solution.py
+++ b/solution.py
@@ -8,8 +8,8 @@
 from jax.sharding import PartitionSpec as P
 
 HALO = 2
-SPLIT = (512, 512)
-RIM_SPLIT = (512, 432, 80)
+SPLIT = (496, 528)
+RIM_SPLIT = (496, 432, 96)
 CHIP_RIM_SPLIT = (352, 336, 336)
 CHIP_SPLIT = (384, 384, 256)
 VMEM_LIMIT = 24 * 1024 * 1024

time: 52.1 us -> 52.2 us (level)
  waiting for transfers between devices: 6.89 us -> 5.69 us
  starting transfers between devices: 18.7 us -> 19.4 us
    ppermute x5, waiting for transfers between devices: 6.87 us -> 5.67 us  [swap_cross(): return in_vmem(lax.ppermute(x, axis, cross_pairs))]
    ppermute x5, starting transfers between devices: 17.4 us -> 18.1 us  [swap_cross(): return in_vmem(lax.ppermute(x, axis, cross_pairs))]
  transfers between devices with their start and end apart: 11 -> 11, of which waited for: 3 -> 3; matrix products, arithmetic and copies ran while one was open for 0% -> 0% of each run, Pallas kernels for 47% -> 48%
where the time goes in v8:
time: 52.2 us; the launch traced here: 51.7 us
  Pallas kernels  26.4 us (51%)
  starting transfers between devices  19.4 us (37%)
  waiting for transfers between devices  5.69 us (11%)
    pallas_call x12, Pallas kernels, call(): pl.pallas_call(body, in_specs=in_specs + [pl.BlockSpec(memory_space=pl.AN...  26.4 us
    ppermute x5, starting transfers between devices, swap_cross(): return in_vmem(lax.ppermute(x, axis, cross_pairs))  18.1 us
    ppermute x5, waiting for transfers between devices, swap_cross(): return in_vmem(lax.ppermute(x, axis, cross_pairs))  5.67 us
    ppermute x6, starting transfers between devices, swap_chip(): return in_vmem(lax.ppermute(x, axis, chip_pairs))  1.29 us
  transfers between devices with their start and end apart: 11, of which 3 were waited for; matrix products, arithmetic and copies ran while one was open for 0% of the time, Pallas kernels for 48%

profile of v8, /device:TPU:1, one launch (start us, length us, event | category | flops | bytes accessed | tf_op | source)
XLA Modules:
  0.0 51.7 jit_solution(6146872907147491902)
XLA Ops:
  0.0 1.1 %pick.2.refs_1_ = bf16[2,496,256]{2,1,0:T(8,128)(2,1)S(1)} custom-call(bf16[4,1024,256]{2,1,0:T(8,128)(2,1)} %refs_1_.1), custom_call_target="tpu_custom_call" | custom-call | flops 1 | bytes 1 | tf_op jit(solution)/shard_map/pick/pallas_call | solution.py:277
  1.1 4.5 %collective-permute-start.3 = (bf16[2,496,256]{2,1,0:T(8,128)(2,1)S(1)}, bf16[2,496,256]{2,1,0:T(8,128)(2,1)S(1)}, u32[]{:S(2)}, u32[]{:S(2)}) collective-permute-start(bf16[2,496,256]{2,1,0:T(8,128)(2,1)S(1)} %pick.2.refs_1_), channel_id=1, source_target_pairs={{1,2},{3,4},{5,6},{7,8},{9,10},{11,12},{13,14},{2,1},{4,3},{6,5},{... | collective-permute-start | bytes 1523720 | tf_op jit(solution)/shard_map/ppermute | solution.py:287
  5.6 1.4 %pick.3 = (bf16[2,528,256]{2,1,0:T(8,128)(2,1)S(1)}, bf16[2,384,256]{2,1,0:T(8,128)(2,1)S(1)}, bf16[2,384,256]{2,1,0:T(8,128)(2,1)S(1)}, bf16[2,256,256]{2,1,0:T(8,128)(2,1)S(1)}) custom-call(bf16[4,1024,256]{2,1,0:T(8,128)(2,1)} %refs_1_.1, bf16[2,496,256]{2,1,0:T(8,128)(2,1)S(1)} %pick.2.refs_1_), custom_call_target="tpu_custom_call" | custom-call | flops 1 | bytes 1 | tf_op jit(solution)/shard_map/pick/pallas_call | solution.py:277
  7.0 1.9 %collective-permute-start.4 = (bf16[2,528,256]{2,1,0:T(8,128)(2,1)S(1)}, bf16[2,528,256]{2,1,0:T(8,128)(2,1)S(1)}, u32[]{:S(2)}, u32[]{:S(2)}) collective-permute-start(bf16[2,528,256]{2,1,0:T(8,128)(2,1)S(1)} %get-tuple-element.26.refs_3_), channel_id=1, source_target_pairs={{1,2},{3,4},{5,6},{7,8},{9,10},{11,12},{13,14},{2,1},{4,3},{6,5},{... | collective-permute-start | bytes 1622024 | tf_op jit(solution)/shard_map/ppermute | solution.py:287
  8.9 0.1 collective-permute-start
  9.0 0.5 collective-permute-start.1
  9.5 0.1 collective-permute-start.2
  9.6 7.1 %own_rims.1 = (s32[9,49]{1,0:T(8,128)S(1)}, bf16[4,1024,256]{2,1,0:T(8,128)(2,1)S(1)}, bf16[48,256,256]{2,1,0:T(8,128)(2,1)S(1)}, f32[2,1024,256]{2,1,0:T(8,128)...) custom-call(s32[2,48]{1,0:T(2,128)S(1)} %bitcast.1, ...), custom_call_target="tpu_custom_call" | custom-call | flops 1 | bytes 1 | tf_op jit(solution)/shard_map/own_rims/pallas_call | solution.py:277
  16.7 2.6 %chip_rims.1 = (f32[2,1024,256]{2,1,0:T(8,128)S(1)}, f32[2,496,256]{2,1,0:T(8,128)S(1)}, f32[2,432,256]{2,1,0:T(8,128)S(1)}, f32[2,96,256]{2,1,0:T(8,128)S(1)}) custom-call(s32[9,49]{1,0:T(8,128)S(1)} %get-tuple-element.30.refs_0_, ...), custom_call_target="tpu_custom_call", output_to_operand_aliasing={{0}: (5, {}), {1}: (6, {}), {2}: (7, {}), {3}: (8, {})} | custom-call | flops 1 | bytes 1 | tf_op jit(solution)/shard_map/chip_rims/pallas_call | solution.py:277
  19.3 3.4 %collective-permute-done.3.refs_3_ = bf16[2,496,256]{2,1,0:T(8,128)(2,1)S(1)} collective-permute-done((bf16[2,496,256]{2,1,0:T(8,128)(2,1)S(1)}, bf16[2,496,256]{2,1,0:T(8,128)(2,1)S(1)}, u32[]{:S(2)}, u32[]{:S(2)}) %collective-permute-start.3) | collective-permute-done | bytes 507936 | tf_op jit(solution)/shard_map/ppermute | solution.py:287
  22.7 1.3 %cross_rim.1 = (f32[2,496,256]{2,1,0:T(8,128)S(1)}, bf16[2,496,256]{2,1,0:T(8,128)(2,1)S(1)}) custom-call(s32[9,49]{1,0:T(8,128)S(1)} %get-tuple-element.30.refs_0_, bf16[48,256,256]{2,1,0:T(8,128)(2,1)S(1)} %get-tuple-element.31.refs_1_.refs_2_, f32[2,496,256]{2,1,0:T(8,128)S(1)} %get-tuple-element.37.refs_2_, ...), custom_call_target="tpu_custom_call", output_to_operand_aliasing={{0}: (2, {})} | custom-call | flops 1 | bytes 1 | tf_op jit(solution)/shard_map/cross_rim/pallas_call | solution.py:277
  24.0 4.5 %collective-permute-start.10 = (bf16[2,496,256]{2,1,0:T(8,128)(2,1)S(1)}, bf16[2,496,256]{2,1,0:T(8,128)(2,1)S(1)}, u32[]{:S(2)}, u32[]{:S(2)}) collective-permute-start(bf16[2,496,256]{2,1,0:T(8,128)(2,1)S(1)} %get-tuple-element.38.refs_6_), channel_id=1, source_target_pairs={{1,2},{3,4},{5,6},{7,8},{9,10},{11,12},{13,14},{2,1},{4,3},{6,5},{... | collective-permute-start | bytes 1523720 | tf_op jit(solution)/shard_map/ppermute | solution.py:287
  28.5 4.6 %own_targets.1.refs_7_.refs_2_ = f32[4,1024,256]{2,1,0:T(8,128)S(1)} custom-call(s32[9,49]{1,0:T(8,128)S(1)} %get-tuple-element.30.refs_0_, bf16[4,1024,256]{2,1,0:T(8,128)(2,1)S(1)} %get-tuple-element.32.refs_1_, bf16[48,256,256]{2,1,0:T(8,128)(2,1)S(1)} %get-tuple-element.31.refs_1_.refs_2_, bf16[2,384,256]{2,1,0:T(8,128)(2,1)S(1)} %collective-permute-done.refs_2_.refs_3_, ...), custom_call_target="tpu_custom_call" | custom-call | flops 1 | bytes 1 | tf_op jit(solution)/shard_map/own_targets/pallas_call | solution.py:277
  33.1 0.9 %collective-permute-done.4.refs_4_ = bf16[2,528,256]{2,1,0:T(8,128)(2,1)S(1)} collective-permute-done((bf16[2,528,256]{2,1,0:T(8,128)(2,1)S(1)}, bf16[2,528,256]{2,1,0:T(8,128)(2,1)S(1)}, u32[]{:S(2)}, u32[]{:S(2)}) %collective-permute-start.4) | collective-permute-done | bytes 540704 | tf_op jit(solution)/shard_map/ppermute | solution.py:287
  34.0 1.9 %last_rims.1 = (bf16[2,352,256]{2,1,0:T(8,128)(2,1)S(1)}, bf16[2,336,256]{2,1,0:T(8,128)(2,1)S(1)}, bf16[2,336,256]{2,1,0:T(8,128)(2,1)S(1)}, f32[2,1024,256]{2,...) custom-call(s32[9,49]{1,0:T(8,128)S(1)} %get-tuple-element.30.refs_0, ...), custom_call_target="tpu_custom_call", output_to_operand_aliasing={{3}: (2, {}), {4}: (5, {}), {5}: (6, {})} | custom-call | flops 1 | bytes 1 | tf_op jit(solution)/shard_map/last_rims/pallas_call | solution.py:277
  35.9 5.3 %collective-permute-start.6 = (bf16[2,432,256]{2,1,0:T(8,128)(2,1)S(1)}, bf16[2,432,256]{2,1,0:T(8,128)(2,1)S(1)}, u32[]{:S(2)}, u32[]{:S(2)}) collective-permute-start(bf16[2,432,256]{2,1,0:T(8,128)(2,1)S(1)} %get-tuple-element.42.refs_5_), channel_id=1, source_target_pairs={{1,2},{3,4},{5,6},{7,8},{9,10},{11,12},{13,14},{2,1},{4,3},{6,5},{... | collective-permute-start | bytes 1327112 | tf_op jit(solution)/shard_map/ppermute | solution.py:287
  41.3 0.5 collective-permute-start.7
  41.8 0.1 collective-permute-start.9
  41.9 3.0 %cross_sources.1.refs_1_.refs_0_ = f32[4,1024,256]{2,1,0:T(8,128)S(1)} custom-call(s32[9,49]{1,0:T(8,128)S(1)} %get-tuple-element.30.refs_0_, bf16[48,256,256]{2,1,0:T(8,128)(2,1)S(1)} %get-tuple-element.31.refs_1_.refs_2_, f32[4,1024,256]{2,1,0:T(8,128)S(1)} %own_targets.1.refs_7_.refs_2_, ...), custom_call_target="tpu_custom_call", output_to_operand_aliasing={{}: (2, {})} | custom-call | flops 1 | bytes 1 | tf_op jit(solution)/shard_map/cross_sources/pallas_call | solution.py:277
  44.9 1.9 %collective-permute-start.5 = (bf16[2,96,256]{2,1,0:T(8,128)(2,1)S(1)}, bf16[2,96,256]{2,1,0:T(8,128)(2,1)S(1)}, u32[]{:S(2)}, u32[]{:S(2)}) collective-permute-start(bf16[2,96,256]{2,1,0:T(8,128)(2,1)S(1)} %pass_on.1), channel_id=1, source_target_pairs={{1,2},{3,4},{5,6},{7,8},{9,10},{11,12},{13,14},{2,1},{4,3},{6,5},{... | collective-permute-start | bytes 294920 | tf_op jit(solution)/shard_map/ppermute | solution.py:287
  46.9 1.8 %residual.1.refs_2_ = f32[4,1024,256]{2,1,0:T(8,128)} custom-call(f32[4,1024,256]{2,1,0:T(8,128)S(1)} %cross_sources.1.refs_1_.refs_0_, bf16[2,352,256]{2,1,0:T(8,128)(2,1)S(1)} %collective-permute-done.7.refs_1_, bf16[2,336,256]{2,1,0:T(8,128)(2,1)S(1)} %collective-permute-done.8.refs_2_, bf16[2,336,256]{2,1,0:T(8,128)(2,1)S(1)} %collective-permute-done.9.refs_3_, ...), custom_call_target="tpu_custom_call" | custom-call | flops 1 | bytes 1 | tf_op jit(solution)/shard_map/residual/pallas_call | solution.py:277
  48.6 1.3 %collective-permute-done.6.refs_1_ = bf16[2,432,256]{2,1,0:T(8,128)(2,1)S(1)} collective-permute-done((bf16[2,432,256]{2,1,0:T(8,128)(2,1)S(1)}, bf16[2,432,256]{2,1,0:T(8,128)(2,1)S(1)}, u32[]{:S(2)}, u32[]{:S(2)}) %collective-permute-start.6) | collective-permute-done | bytes 442400 | tf_op jit(solution)/shard_map/ppermute | solution.py:287
  50.0 1.0 %residual_last.2.refs_2_ = f32[4,1024,256]{2,1,0:T(8,128)} custom-call(f32[4,1024,256]{2,1,0:T(8,128)S(1)} %cross_sources.1.refs_1_.refs_0_, bf16[2,432,256]{2,1,0:T(8,128)(2,1)S(1)} %collective-permute-done.6.refs_1_, f32[4,1024,256]{2,1,0:T(8,128)} %residual.1.refs_2_), custom_call_target="tpu_custom_call", output_to_operand_aliasing={{}: (2, {})} | custom-call | flops 1 | bytes 1 | tf_op jit(solution)/shard_map/residual_last/pallas_call | solution.py:277
  51.0 0.7 %residual_last.3 = f32[4,1024,256]{2,1,0:T(8,128)} custom-call(f32[4,1024,256]{2,1,0:T(8,128)S(1)} %cross_sources.1.refs_1_.refs_0_, bf16[2,96,256]{2,1,0:T(8,128)(2,1)S(1)} %collective-permute-done.5.refs_1_, f32[4,1024,256]{2,1,0:T(8,128)} %residual_last.2.refs_2_), custom_call_target="tpu_custom_call", output_to_operand_aliasing={{}: (2, {})} | custom-call | flops 1 | bytes 1 | tf_op jit(solution)/shard_map/residual_last/pallas_call | solution.py:277
  (12 shorter events, 0.1 us)
Async XLA Ops:
  0.0 9.6 %copy-start = (s32[48,2]{0,1:T(2,128)S(1)}, s32[48,2]{0,1:T(2,128)}, u32[]{:S(2)}) copy-start(s32[48,2]{0,1:T(2,128)} %param.5) | copy-start | bytes 1156
  1.1 21.7 %collective-permute-start.3 = (bf16[2,496,256]{2,1,0:T(8,128)(2,1)S(1)}, bf16[2,496,256]{2,1,0:T(8,128)(2,1)S(1)}, u32[]{:S(2)}, u32[]{:S(2)}) collective-permute-start(bf16[2,496,256]{2,1,0:T(8,128)(2,1)S(1)} %pick.2.refs_1_), channel_id=1, source_target_pairs={{1,2},{3,4},{5,6},{7,8},{9,10},{11,12},{13,14},{2,1},{4,3},{6,5},{... | collective-permute-start | bytes 1523720 | tf_op jit(solution)/shard_map/ppermute | solution.py:287
  7.0 27.0 %collective-permute-start.4 = (bf16[2,528,256]{2,1,0:T(8,128)(2,1)S(1)}, bf16[2,528,256]{2,1,0:T(8,128)(2,1)S(1)}, u32[]{:S(2)}, u32[]{:S(2)}) collective-permute-start(bf16[2,528,256]{2,1,0:T(8,128)(2,1)S(1)} %get-tuple-element.26.refs_3_), channel_id=1, source_target_pairs={{1,2},{3,4},{5,6},{7,8},{9,10},{11,12},{13,14},{2,1},{4,3},{6,5},{... | collective-permute-start | bytes 1622024 | tf_op jit(solution)/shard_map/ppermute | solution.py:287
  8.9 7.8 %collective-permute-start = (bf16[2,384,256]{2,1,0:T(8,128)(2,1)S(1)}, bf16[2,384,256]{2,1,0:T(8,128)(2,1)S(1)}, u32[]{:S(2)}, u32[]{:S(2)}) collective-permute-start(bf16[2,384,256]{2,1,0:T(8,128)(2,1)S(1)} %get-tuple-element.27.refs_4_), channel_id=1, source_target_pairs={{0,1},{1,0},{2,3},{3,2},{4,5},{5,4},{6,7},{7,6},{8,9},{9,8},{10,11... | collective-permute-start | bytes 1179656 | tf_op jit(solution)/shard_map/ppermute | solution.py:290
  9.0 7.7 %collective-permute-start.1 = (bf16[2,384,256]{2,1,0:T(8,128)(2,1)S(1)}, bf16[2,384,256]{2,1,0:T(8,128)(2,1)S(1)}, u32[]{:S(2)}, u32[]{:S(2)}) collective-permute-start(bf16[2,384,256]{2,1,0:T(8,128)(2,1)S(1)} %get-tuple-element.28.refs_5_), channel_id=1, source_target_pairs={{0,1},{1,0},{2,3},{3,2},{4,5},{5,4},{6,7},{7,6},{8,9},{9,8},{10,11... | collective-permute-start | bytes 1179656 | tf_op jit(solution)/shard_map/ppermute | solution.py:290
  9.5 7.2 %collective-permute-start.2 = (bf16[2,256,256]{2,1,0:T(8,128)(2,1)S(1)}, bf16[2,256,256]{2,1,0:T(8,128)(2,1)S(1)}, u32[]{:S(2)}, u32[]{:S(2)}) collective-permute-start(bf16[2,256,256]{2,1,0:T(8,128)(2,1)S(1)} %get-tuple-element.29.refs_6_), channel_id=1, source_target_pairs={{0,1},{1,0},{2,3},{3,2},{4,5},{5,4},{6,7},{7,6},{8,9},{9,8},{10,11... | collective-permute-start | bytes 786440 | tf_op jit(solution)/shard_map/ppermute | solution.py:290
  24.0 22.8 %collective-permute-start.10 = (bf16[2,496,256]{2,1,0:T(8,128)(2,1)S(1)}, bf16[2,496,256]{2,1,0:T(8,128)(2,1)S(1)}, u32[]{:S(2)}, u32[]{:S(2)}) collective-permute-start(bf16[2,496,256]{2,1,0:T(8,128)(2,1)S(1)} %get-tuple-element.38.refs_6_), channel_id=1, source_target_pairs={{1,2},{3,4},{5,6},{7,8},{9,10},{11,12},{13,14},{2,1},{4,3},{6,5},{... | collective-permute-start | bytes 1523720 | tf_op jit(solution)/shard_map/ppermute | solution.py:287
  35.9 14.1 %collective-permute-start.6 = (bf16[2,432,256]{2,1,0:T(8,128)(2,1)S(1)}, bf16[2,432,256]{2,1,0:T(8,128)(2,1)S(1)}, u32[]{:S(2)}, u32[]{:S(2)}) collective-permute-start(bf16[2,432,256]{2,1,0:T(8,128)(2,1)S(1)} %get-tuple-element.42.refs_5_), channel_id=1, source_target_pairs={{1,2},{3,4},{5,6},{7,8},{9,10},{11,12},{13,14},{2,1},{4,3},{6,5},{... | collective-permute-start | bytes 1327112 | tf_op jit(solution)/shard_map/ppermute | solution.py:287
  41.2 3.7 %collective-permute-start.8 = (bf16[2,336,256]{2,1,0:T(8,128)(2,1)S(1)}, bf16[2,336,256]{2,1,0:T(8,128)(2,1)S(1)}, u32[]{:S(2)}, u32[]{:S(2)}) collective-permute-start(bf16[2,336,256]{2,1,0:T(8,128)(2,1)S(1)} %get-tuple-element.45), channel_id=1, source_target_pairs={{0,1},{1,0},{2,3},{3,2},{4,5},{5,4},{6,7},{7,6},{8,9},{9,8},{10,11... | collective-permute-start | bytes 1032200 | tf_op jit(solution)/shard_map/ppermute | solution.py:290
  41.3 5.6 %collective-permute-start.7 = (bf16[2,352,256]{2,1,0:T(8,128)(2,1)S(1)}, bf16[2,352,256]{2,1,0:T(8,128)(2,1)S(1)}, u32[]{:S(2)}, u32[]{:S(2)}) collective-permute-start(bf16[2,352,256]{2,1,0:T(8,128)(2,1)S(1)} %get-tuple-element.44), channel_id=1, source_target_pairs={{0,1},{1,0},{2,3},{3,2},{4,5},{5,4},{6,7},{7,6},{8,9},{9,8},{10,11... | collective-permute-start | bytes 1081352 | tf_op jit(solution)/shard_map/ppermute | solution.py:290
  41.8 5.1 %collective-permute-start.9 = (bf16[2,336,256]{2,1,0:T(8,128)(2,1)S(1)}, bf16[2,336,256]{2,1,0:T(8,128)(2,1)S(1)}, u32[]{:S(2)}, u32[]{:S(2)}) collective-permute-start(bf16[2,336,256]{2,1,0:T(8,128)(2,1)S(1)} %get-tuple-element.46), channel_id=1, source_target_pairs={{0,1},{1,0},{2,3},{3,2},{4,5},{5,4},{6,7},{7,6},{8,9},{9,8},{10,11... | collective-permute-start | bytes 1032200 | tf_op jit(solution)/shard_map/ppermute | solution.py:290
  44.9 6.1 %collective-permute-start.5 = (bf16[2,96,256]{2,1,0:T(8,128)(2,1)S(1)}, bf16[2,96,256]{2,1,0:T(8,128)(2,1)S(1)}, u32[]{:S(2)}, u32[]{:S(2)}) collective-permute-start(bf16[2,96,256]{2,1,0:T(8,128)(2,1)S(1)} %pass_on.1), channel_id=1, source_target_pairs={{1,2},{3,4},{5,6},{7,8},{9,10},{11,12},{13,14},{2,1},{4,3},{6,5},{... | collective-permute-start | bytes 294920 | tf_op jit(solution)/shard_map/ppermute | solution.py:287
